TPU v7x, 32 devices: a whole 2x2x4 slice. The times are simulated.
32 devices in a mesh: groups: 2 (over y), expert: 8 (over z, x), tensor: 2 (over core).
Axes of the slice: x: 2, y: 2, z: 4, core: 2. Of those that a mesh axis runs over, the one named last changes fastest.
Arguments:
- tokens: bfloat16 [2048, 4096], P(('groups', 'expert'), 'tensor'), parts along dimension 0, may hold values from -6 to 6
- grad_query: bfloat16 [2048, 4096], P(('groups', 'expert'), 'tensor'), parts along dimension 0, may hold values from -0.29882812 to 0.29882812
- grad_value: bfloat16 [2048, 1024], P(('groups', 'expert'), 'tensor'), parts along dimension 0, may hold values from -0.29882812 to 0.29882812
- a_proj: bfloat16 [16, 4096, 128], P(('groups', 'expert'), 'tensor'), parts along dimension 0, may hold values from -0.09375 to 0.09375
- b_query: bfloat16 [16, 64, 4096], P(('groups', 'expert'), None, 'tensor'), parts along dimension 0, may hold values from -0.75 to 0.75
- b_value: bfloat16 [16, 64, 1024], P(('groups', 'expert'), None, 'tensor'), parts along dimension 0, may hold values from -0.75 to 0.75
- token_request: int32 [16, 128], P(('groups', 'expert')), parts along dimension 0, may hold values from 0 to 31, never falling along the last dimension, each value on 1 to 5 neighbouring positions
- req_adapter: int32 [16, 32, 4], P(('groups', 'expert')), parts along dimension 0, may hold values from 0 to 7, as said below
- req_count: int32 [16, 32], P(('groups', 'expert')), parts along dimension 0, may hold values from 1 to 4
- req_mix: bfloat16 [16, 32, 4], P(('groups', 'expert')), parts along dimension 0, may hold values from 0.19921875 to 1.5
Outputs:
- out_query: bfloat16 [2048, 4096], P(('groups', 'expert'), 'tensor'), parts along dimension 0
- out_value: bfloat16 [2048, 1024], P(('groups', 'expert'), 'tensor'), parts along dimension 0
- grad_a: bfloat16 [16, 4096, 128], P(('groups', 'expert'), 'tensor'), parts along dimension 0
- grad_bq: bfloat16 [16, 64, 4096], P(('groups', 'expert'), None, 'tensor'), parts along dimension 0
- grad_bv: bfloat16 [16, 64, 1024], P(('groups', 'expert'), None, 'tensor'), parts along dimension 0
- grad_mix: float32 [16, 32, 4], P(('groups', 'expert')), parts along dimension 0
There are 2 independent parts, one for each index of `groups`. A program takes and returns all parts, laid end to end along the dimension named above; each array names one. Nothing has to cross between parts.
Inputs may be any that keep to these rules, and one draw needn't show every extreme that they name: `req_adapter`: adapter a is held at index a of expert. In each block's 4 * 32 entries (used or not), every adapter appears exactly 4 * 32 / 8 times. `token_request`: never falls along a block; request r of a block holds 1 to 5 tokens, and one request of every block holds exactly 5.
All inputs are finite; a program needn't handle non-finite values.
Results may differ from a plain program's by a relative error of at most 0.0085.
Values may be sent and summed in bfloat16 or wider, within the bound.
No kernel may reach another device: no remote copies, remote signals or barrier semaphores. Data moves between devices by JAX's collectives and lax.ppermute only.
A program may use at most 128 MiB of HBM per device.

v0:
```python
import jax
import jax.numpy as jnp
from jax import lax
from jax.sharding import PartitionSpec as P

REQ_MOST = 5


def shards(
    tokens,
    grad_query,
    grad_value,
    a_proj,
    b_query,
    b_value,
    token_request,
    req_adapter,
    req_count,
    req_mix,
):
    peer_count = lax.axis_size("expert")
    tok_count = tokens.shape[0]
    feat_width = tokens.shape[1]
    value_width = grad_value.shape[1]
    requests = req_count.shape[1]
    slot_count = 4 * requests
    per_peer = slot_count // peer_count
    row_count = REQ_MOST
    rank_width = a_proj.shape[2] // 2
    nothing = jnp.zeros((), jnp.bfloat16)
    request_of = token_request[0]
    member = (request_of[:, None] == jnp.arange(requests, dtype=jnp.int32)[None, :]).astype(
        jnp.int32
    )
    lengths = jnp.sum(member, axis=0)
    starts = jnp.cumsum(lengths) - lengths
    owners = req_adapter[0].reshape(slot_count)
    slot_ids = jnp.arange(slot_count, dtype=jnp.int32)
    earlier = (owners[:, None] == owners[None, :]) & (slot_ids[None, :] < slot_ids[:, None])
    placed = owners * per_peer + jnp.sum(earlier.astype(jnp.int32), axis=1)
    slot_order = jnp.zeros((slot_count,), jnp.int32).at[placed].set(slot_ids)
    req_index = slot_order // 4
    pick_index = slot_order % 4
    row_ids = jnp.arange(row_count, dtype=jnp.int32)
    live_rows = (row_ids[None, :] < lengths[req_index][:, None]) & (
        pick_index < req_count[0][req_index]
    )[:, None]
    token_idx = jnp.where(live_rows, starts[req_index][:, None] + row_ids[None, :], 0)
    flat_idx = token_idx.reshape(-1)
    keep_rows = live_rows.reshape(-1, 1)
    x_rows = jnp.where(keep_rows, tokens[flat_idx], nothing).reshape(
        slot_count, row_count, feat_width
    )
    query_rows = jnp.where(keep_rows, grad_query[flat_idx], nothing).reshape(
        slot_count, row_count, feat_width
    )
    value_rows = jnp.where(keep_rows, grad_value[flat_idx], nothing).reshape(
        slot_count, row_count, value_width
    )
    weights = jnp.where(live_rows, req_mix[0][req_index, pick_index][:, None], nothing)
    a_matrix = a_proj[0]
    bq_matrix = b_query[0]
    bv_matrix = b_value[0]
    contract_last = (((1,), (1,)), ((), ()))
    contract_first = (((0,), (0,)), ((), ()))
    x_recv, q_recv, v_recv, w_recv = (
        lax.all_to_all(x_rows, "expert", split_axis=0, concat_axis=0, tiled=True),
        lax.all_to_all(query_rows, "expert", split_axis=0, concat_axis=0, tiled=True),
        lax.all_to_all(value_rows, "expert", split_axis=0, concat_axis=0, tiled=True),
        lax.all_to_all(weights, "expert", split_axis=0, concat_axis=0, tiled=True),
    )
    x_flat = x_recv.reshape(-1, feat_width)
    hidden_part = jnp.dot(x_flat, a_matrix, preferred_element_type=jnp.float32)
    q_flat = q_recv.reshape(-1, feat_width)
    v_flat = v_recv.reshape(-1, value_width)
    hidden = lax.psum(hidden_part, "tensor")
    slope_part = jnp.concatenate(
        [
            lax.dot_general(q_flat, bq_matrix, contract_last, preferred_element_type=jnp.float32),
            lax.dot_general(v_flat, bv_matrix, contract_last, preferred_element_type=jnp.float32),
        ],
        axis=1,
    )
    slopes = lax.psum(slope_part, "tensor")
    hidden_bf = hidden.astype(jnp.bfloat16)
    up_query = jnp.dot(
        hidden_bf[:, :rank_width], bq_matrix, preferred_element_type=jnp.float32
    ).astype(jnp.bfloat16)
    up_value = jnp.dot(
        hidden_bf[:, rank_width:], bv_matrix, preferred_element_type=jnp.float32
    ).astype(jnp.bfloat16)
    row_grad = jnp.sum(slopes * hidden_bf.astype(jnp.float32), axis=1).astype(jnp.bfloat16)
    weight_col = w_recv.reshape(-1, 1).astype(jnp.float32)
    grad_hidden = (weight_col * slopes).astype(jnp.bfloat16)
    grad_down = lax.dot_general(
        x_flat, grad_hidden, contract_first, preferred_element_type=jnp.float32
    ).astype(jnp.bfloat16)
    weighted = (weight_col * hidden).astype(jnp.bfloat16)
    grad_upq = lax.dot_general(
        weighted[:, :rank_width], q_flat, contract_first, preferred_element_type=jnp.float32
    ).astype(jnp.bfloat16)
    grad_upv = lax.dot_general(
        weighted[:, rank_width:], v_flat, contract_first, preferred_element_type=jnp.float32
    ).astype(jnp.bfloat16)
    back_query, back_value, back_grad = (
        lax.all_to_all(
            up_query.reshape(slot_count, row_count, feat_width),
            "expert",
            split_axis=0,
            concat_axis=0,
            tiled=True,
        ),
        lax.all_to_all(
            up_value.reshape(slot_count, row_count, value_width),
            "expert",
            split_axis=0,
            concat_axis=0,
            tiled=True,
        ),
        lax.all_to_all(
            row_grad.reshape(slot_count, row_count),
            "expert",
            split_axis=0,
            concat_axis=0,
            tiled=True,
        ),
    )
    scale_col = weights.reshape(-1, 1).astype(jnp.float32)
    out_query = (
        jnp.zeros((tok_count, feat_width), jnp.float32)
        .at[flat_idx]
        .add(scale_col * back_query.reshape(-1, feat_width).astype(jnp.float32))
    )
    out_value = (
        jnp.zeros((tok_count, value_width), jnp.float32)
        .at[flat_idx]
        .add(scale_col * back_value.reshape(-1, value_width).astype(jnp.float32))
    )
    slot_grad = jnp.sum(back_grad.astype(jnp.float32), axis=1)
    grad_mix = (
        jnp.zeros((slot_count,), jnp.float32).at[slot_order].set(slot_grad).reshape(1, requests, 4)
    )
    return (
        out_query.astype(jnp.bfloat16),
        out_value.astype(jnp.bfloat16),
        grad_down[None],
        grad_upq[None],
        grad_upv[None],
        grad_mix,
    )


def solution(mesh):
    in_specs = (
        P(("groups", "expert"), "tensor"),
        P(("groups", "expert"), "tensor"),
        P(("groups", "expert"), "tensor"),
        P(("groups", "expert"), "tensor", None),
        P(("groups", "expert"), None, "tensor"),
        P(("groups", "expert"), None, "tensor"),
        P(("groups", "expert"), None),
        P(("groups", "expert"), None, None),
        P(("groups", "expert"), None),
        P(("groups", "expert"), None, None),
    )
    out_specs = (
        P(("groups", "expert"), "tensor"),
        P(("groups", "expert"), "tensor"),
        P(("groups", "expert"), "tensor", None),
        P(("groups", "expert"), None, "tensor"),
        P(("groups", "expert"), None, "tensor"),
        P(("groups", "expert"), None, None),
    )
    return jax.shard_map(shards, mesh=mesh, in_specs=in_specs, out_specs=out_specs, check_vma=False)
```

profile of v0, /device:TPU:0, one launch (start us, length us, event | category | flops | bytes accessed | tf_op | source)
XLA Modules:
  0.0 443.6 jit_solution(12400787810104516473)
XLA Ops:
  15.8 2.8 gather_fusion.6
  20.1 7.3 %all-to-all-start.5 = ((bf16[128,5,512]{2,1,0:T(8,128)(2,1)}), bf16[128,5,512]{2,1,0:T(8,128)(2,1)}, u32[]{:S(2)}, u32[]{:S(2)}) async-start(bf16[128,5,512]{2,1,0:T(8,128)(2,1)} %broadcast_select_fusion.2), calls=%async_computation.5 | async-start | bytes 2097152 | tf_op jit(solution)/shard_map/all_to_all | solution.py:69
  27.3 3.4 gather_fusion.4
  30.8 2.9 gather.32
  33.7 3.4 gather_fusion.5
  37.1 2.9 gather.34
  40.0 5.9 %broadcast_select_fusion = (bf16[128,5,2048]{2,1,0:T(8,128)(2,1)}, bf16[128,5,2048]{2,1,0:T(8,128)(2,1)}) fusion(bf16[128,5,2048]{2,1,0:T(8,128)(2,1)} %gather.34, pred[128,5]{1,0:T(8,128)(4,1)S(1)} %fusion.24, bf16[128,5,2048]{2,1,0:T(8,128)(2,1)} %gather.32), kind=kLoop, calls=%fused_computation.13 | loop fusion | flops 2621440 | bytes 10486400 | tf_op jit(solution)/shard_map/jit(_where)/select_n | solution.py:54
  45.9 7.3 %all-to-all-done.5 = bf16[128,5,512]{2,1,0:T(8,128)(2,1)} async-done(((bf16[128,5,512]{2,1,0:T(8,128)(2,1)}), bf16[128,5,512]{2,1,0:T(8,128)(2,1)}, u32[]{:S(2)}, u32[]{:S(2)}) %all-to-all-start.5) | async-done | bytes 655392 | tf_op jit(solution)/shard_map/all_to_all | solution.py:69
  53.2 97.3 %all_to_all.37 = bf16[128,5,2048]{2,1,0:T(8,128)(2,1)} all-to-all(bf16[128,5,2048]{2,1,0:T(8,128)(2,1)} %get-tuple-element.44), channel_id=1, replica_groups=mesh['groups'=2,'expert'=8,'tensor'=2] {'expert'}, dimensions={0} | all-to-all | bytes 5242880 | tf_op jit(solution)/shard_map/all_to_all | solution.py:68
  150.5 4.7 %all-to-all-start = ((bf16[128,5,2048]{2,1,0:T(8,128)(2,1)}), bf16[128,5,2048]{2,1,0:T(8,128)(2,1)}, u32[]{:S(2)}, u32[]{:S(2)}) async-start(bf16[128,5,2048]{2,1,0:T(8,128)(2,1)} %get-tuple-element.45), calls=%async_computation | async-start | bytes 8388608 | tf_op jit(solution)/shard_map/all_to_all | solution.py:67
  157.8 4.2 reshape.266
  162.0 2.0 fusion.12
  164.9 82.4 %all-to-all-done = bf16[128,5,2048]{2,1,0:T(8,128)(2,1)} async-done(((bf16[128,5,2048]{2,1,0:T(8,128)(2,1)}), bf16[128,5,2048]{2,1,0:T(8,128)(2,1)}, u32[]{:S(2)}, u32[]{:S(2)}) %all-to-all-start) | async-done | bytes 2621472 | tf_op jit(solution)/shard_map/all_to_all | solution.py:67
  247.3 4.2 reshape.263
  251.5 2.6 fusion.9
  255.9 10.0 %all_to_all.38 = bf16[8,16,5]{1,2,0:T(8,128)(2,1)S(1)} all-to-all(bf16[8,16,5]{1,2,0:T(8,128)(2,1)S(1)} %fusion.27), channel_id=1, replica_groups=mesh['groups'=2,'expert'=8,'tensor'=2] {'expert'}, dimensions={0} | all-to-all | bytes 2560 | tf_op jit(solution)/shard_map/all_to_all | solution.py:70
  266.3 6.1 %all-reduce.3.cloned.1.call-done = (f32[640,128]{1,0:T(8,128)}, f32[640,128]{1,0:T(8,128)}) async-done(((f32[640,128]{1,0:T(8,128)}, f32[640,128]{1,0:T(8,128)}), (f32[640,128]{1,0:T(8,128)}, f32[640,128]{1,0:T(8,128)})) %all-reduce.3.cloned.1.call-update) | async-done | bytes 655376 | tf_op jit(solution)/shard_map/psum | solution.py:76
  274.8 5.8 %all-to-all-start.6 = ((bf16[8,16,5]{1,2,0:T(8,128)(2,1)}), bf16[8,16,5]{1,2,0:T(8,128)(2,1)S(1)}, u32[]{:S(2)}, u32[]{:S(2)}) async-start(bf16[8,16,5]{1,2,0:T(8,128)(2,1)} %copy.51), calls=%async_computation.6 | async-start | bytes 32768 | tf_op jit(solution)/shard_map/all_to_all | solution.py:120
  281.8 2.1 reshape.265
  283.9 3.2 all-to-all-done.6
  287.1 4.4 all-to-all-start.2
  291.6 2.4 convolution_convert_fusion
  293.9 5.5 %reshape.264 = bf16[128,5,2048]{2,1,0:T(8,128)(2,1)} reshape(bf16[640,2048]{1,0:T(8,128)(2,1)} %convolution_convert_fusion) | data formatting | bytes 5242880 | tf_op jit(solution)/shard_map/reshape | solution.py:107
  299.4 17.5 %all-to-all-done.2 = bf16[128,5,512]{2,1,0:T(8,128)(2,1)} async-done(((bf16[128,5,512]{2,1,0:T(8,128)(2,1)}), bf16[128,5,512]{2,1,0:T(8,128)(2,1)}, u32[]{:S(2)}, u32[]{:S(2)}) %all-to-all-start.2) | async-done | bytes 655392 | tf_op jit(solution)/shard_map/all_to_all | solution.py:113
  316.9 4.6 %all-to-all-start.1 = ((bf16[128,5,2048]{2,1,0:T(8,128)(2,1)}), bf16[128,5,2048]{2,1,0:T(8,128)(2,1)}, u32[]{:S(2)}, u32[]{:S(2)}) async-start(bf16[128,5,2048]{2,1,0:T(8,128)(2,1)} %reshape.264), calls=%async_computation.1 | async-start | bytes 8388608 | tf_op jit(solution)/shard_map/all_to_all | solution.py:106
  321.8 2.1 fusion.7
  323.9 3.0 fusion.4
  326.9 1.8 fusion.3
  331.9 8.0 %scatter_custom_fusion.2 = f32[128,512]{1,0:T(8,128)S(1)} fusion(s32[640]{0:T(1024)S(1)} %fusion.28, f32[640,512]{1,0:T(8,128)S(1)} %reshape.271, f32[640]{0:T(1024)S(1)} %reshape.269, f32[]{:T(128)} %constant.21.clone.1), kind=kCustom, calls=%fused_computation.22 | custom fusion | flops 655360 | bytes 1576964 | tf_op jit(solution)/shard_map/scatter-add | solution.py:137
  340.6 73.2 %all-to-all-done.1 = bf16[128,5,2048]{2,1,0:T(8,128)(2,1)} async-done(((bf16[128,5,2048]{2,1,0:T(8,128)(2,1)}), bf16[128,5,2048]{2,1,0:T(8,128)(2,1)}, u32[]{:S(2)}, u32[]{:S(2)}) %all-to-all-start.1) | async-done | bytes 2621472 | tf_op jit(solution)/shard_map/all_to_all | solution.py:106
  413.7 6.4 %reshape.270 = f32[640,2048]{1,0:T(8,128)} reshape(bf16[128,5,2048]{2,1,0:T(8,128)(2,1)} %all-to-all-done.1) | data formatting | bytes 7864320 | tf_op jit(solution)/shard_map/convert_element_type | solution.py:132
  420.1 15.8 %scatter_custom_fusion.1 = f32[128,2048]{1,0:T(8,128)S(1)} fusion(s32[640]{0:T(1024)S(1)} %fusion.28, f32[640,2048]{1,0:T(8,128)} %reshape.270, f32[640]{0:T(1024)S(1)} %reshape.269, f32[]{:T(128)} %constant.21.clone.1), kind=kCustom, calls=%fused_computation.11 | custom fusion | flops 2621440 | bytes 6295556 | tf_op jit(solution)/shard_map/scatter-add | solution.py:132
  (74 shorter events, 24.3 us)
Async XLA Ops:
  7.2 20.2 %copy-start = (bf16[128,2048]{1,0:T(8,128)(2,1)S(1)}, bf16[128,2048]{1,0:T(8,128)(2,1)}, u32[]{:S(2)}) copy-start(bf16[128,2048]{1,0:T(8,128)(2,1)} %param.10) | copy-start | bytes 1572868
  7.2 8.7 %copy-start.4 = (bf16[128,512]{1,0:T(8,128)(2,1)S(1)}, bf16[128,512]{1,0:T(8,128)(2,1)}, u32[]{:S(2)}) copy-start(bf16[128,512]{1,0:T(8,128)(2,1)} %param.12) | copy-start | bytes 393220
  20.1 33.1 %all-to-all-start.5 = ((bf16[128,5,512]{2,1,0:T(8,128)(2,1)}), bf16[128,5,512]{2,1,0:T(8,128)(2,1)}, u32[]{:S(2)}, u32[]{:S(2)}) async-start(bf16[128,5,512]{2,1,0:T(8,128)(2,1)} %broadcast_select_fusion.2), calls=%async_computation.5 | async-start | bytes 2097152 | tf_op jit(solution)/shard_map/all_to_all | solution.py:69
  30.8 2.9 copy-start.2
  150.5 7.0 %copy-start.9 = (bf16[1,64,512]{2,1,0:T(8,128)(2,1)S(1)}, bf16[1,64,512]{2,1,0:T(8,128)(2,1)}, u32[]{:S(2)}) copy-start(bf16[1,64,512]{2,1,0:T(8,128)(2,1)} %param.15) | copy-start | bytes 196612
  150.5 96.8 %all-to-all-start = ((bf16[128,5,2048]{2,1,0:T(8,128)(2,1)}), bf16[128,5,2048]{2,1,0:T(8,128)(2,1)}, u32[]{:S(2)}, u32[]{:S(2)}) async-start(bf16[128,5,2048]{2,1,0:T(8,128)(2,1)} %get-tuple-element.45), calls=%async_computation | async-start | bytes 8388608 | tf_op jit(solution)/shard_map/all_to_all | solution.py:67
  155.2 117.2 %all-reduce.3.cloned.1.call-start = ((), (), s32[]{:S(2)}) async-start(), calls=%async_computation.7 | async-start | bytes 1310720 | tf_op jit(solution)/shard_map/psum | solution.py:76
  156.7 0.9 copy-start.6
  162.0 2.9 copy-start.5
  251.5 2.8 copy-start.3
  273.8 17.8 %copy-start.8 = (bf16[1,64,2048]{2,1,0:T(8,128)(2,1)S(1)}, bf16[1,64,2048]{2,1,0:T(8,128)(2,1)}, u32[]{:S(2)}) copy-start(bf16[1,64,2048]{2,1,0:T(8,128)(2,1)} %param.14) | copy-start | bytes 786436
  274.8 12.4 %all-to-all-start.6 = ((bf16[8,16,5]{1,2,0:T(8,128)(2,1)}), bf16[8,16,5]{1,2,0:T(8,128)(2,1)S(1)}, u32[]{:S(2)}, u32[]{:S(2)}) async-start(bf16[8,16,5]{1,2,0:T(8,128)(2,1)} %copy.51), calls=%async_computation.6 | async-start | bytes 32768 | tf_op jit(solution)/shard_map/all_to_all | solution.py:120
  287.1 29.7 %all-to-all-start.2 = ((bf16[128,5,512]{2,1,0:T(8,128)(2,1)}), bf16[128,5,512]{2,1,0:T(8,128)(2,1)}, u32[]{:S(2)}, u32[]{:S(2)}) async-start(bf16[128,5,512]{2,1,0:T(8,128)(2,1)} %reshape.265), calls=%async_computation.2 | async-start | bytes 2097152 | tf_op jit(solution)/shard_map/all_to_all | solution.py:113
  316.9 96.9 %all-to-all-start.1 = ((bf16[128,5,2048]{2,1,0:T(8,128)(2,1)}), bf16[128,5,2048]{2,1,0:T(8,128)(2,1)}, u32[]{:S(2)}, u32[]{:S(2)}) async-start(bf16[128,5,2048]{2,1,0:T(8,128)(2,1)} %reshape.264), calls=%async_computation.1 | async-start | bytes 8388608 | tf_op jit(solution)/shard_map/all_to_all | solution.py:106
  321.5 5.4 %copy-start.7 = (f32[640,128]{1,0:T(8,128)S(1)}, f32[640,128]{1,0:T(8,128)}, u32[]{:S(2)}) copy-start(f32[640,128]{1,0:T(8,128)} %get-tuple-element.37) | copy-start | bytes 983044
  413.7 23.0 %copy-start.1 = (bf16[128,2048]{1,0:T(8,128)(2,1)S(1)}, bf16[128,2048]{1,0:T(8,128)(2,1)}, u32[]{:S(2)}) copy-start(bf16[128,2048]{1,0:T(8,128)(2,1)} %param.10) | copy-start | bytes 1572868
Sparse Core Ops, SparseCore 0:
  254.2 18.0 all-reduce.2
where the time goes:
time: 445 us; the launch traced here: 444 us
  waiting for transfers between devices  190 us (43%)
  blocking collectives  107 us (24%)
  local copies, waits for them, and re-layouts  53.1 us (12%)
  other arithmetic  37 us (8%)
  starting transfers between devices  26.7 us (6%)
  matrix products  15.4 us (3%)
  between operations  14.4 us (3%)
    all_to_all x1, blocking collectives, shards(): lax.all_to_all(query_rows, 'expert', split_axis=0, concat_axis=0, tiled=T...  97.3 us
    all_to_all x1, waiting for transfers between devices, shards(): lax.all_to_all(x_rows, 'expert', split_axis=0, concat_axis=0, tiled=True)  82.4 us
    all_to_all x1, waiting for transfers between devices, shards(): lax.all_to_all(up_query.reshape(slot_count, row_count, feat_width), 'expe...  73.2 us
    all_to_all x1, waiting for transfers between devices, shards(): lax.all_to_all(up_value.reshape(slot_count, row_count, value_width), 'exp...  17.5 us
    scatter-add x1, other arithmetic, shards(): out_query = jnp.zeros((tok_count, feat_width), jnp.float32).at[flat_idx]....  15.8 us
    all_to_all x1, blocking collectives, shards(): lax.all_to_all(weights, 'expert', split_axis=0, concat_axis=0, tiled=True)  9.99 us
  transfers between devices with their start and end apart: 6, of which 6 were waited for; matrix products, arithmetic and copies ran while one was open for 13% of the time, Pallas kernels for 0%

commit v1 on v0

--- a/solution.py
+++ b/solution.py
@@ -6,7 +6,7 @@
 REQ_MOST = 5
 
 
-def shards(
+def row_exchange(
     tokens,
     grad_query,
     grad_value,
@@ -150,6 +150,127 @@
     )
 
 
+LINE, PAIR = 4, 2
+F32, BF16 = jnp.float32, jnp.bfloat16
+MID = [(2, 4), (3, 5), (4, 2), (5, 3)]
+OUT = [(2, 0), (3, 1), (4, 6), (5, 7)]
+
+
+def to_place(array, place):
+    return lax.ppermute(array, "expert", [(i, i ^ place) for i in range(LINE * PAIR)])
+
+
+def sum_cores(part):
+    return part + lax.ppermute(part, "tensor", [(0, 1), (1, 0)])
+
+
+def line_gather(own):
+    near = to_place(own, 2)
+    inner = lax.ppermute(own, "expert", MID)
+    second_out = lax.ppermute(inner, "expert", OUT)
+    second_mid = lax.ppermute(near, "expert", MID)
+    third_out = lax.ppermute(second_mid, "expert", OUT)
+    return [own, near, second_out + second_mid, third_out + inner]
+
+
+def dot(a, b, over):
+    return lax.dot_general(a, b, (over, ((), ())), preferred_element_type=F32)
+
+
+def pair_plan(
+    tokens,
+    grad_query,
+    grad_value,
+    a_proj,
+    b_query,
+    b_value,
+    token_request,
+    req_adapter,
+    req_count,
+    req_mix,
+):
+    me = lax.axis_index("expert")
+    requests = req_count.shape[1]
+    rank = b_query.shape[1]
+    wide = grad_query.shape[1]
+    places = jnp.arange(LINE * PAIR, dtype=jnp.int32)
+
+    member = (token_request[0][:, None] == jnp.arange(requests, dtype=jnp.int32)).astype(F32)
+    used = jnp.arange(4, dtype=jnp.int32)[None, :] < req_count[0][:, None]
+    picks = ((req_adapter[0] ^ me)[:, :, None] == places) & used[:, :, None]
+    req_weight = jnp.sum(jnp.where(picks, req_mix[0].astype(F32)[:, :, None], 0.0), axis=1)
+    weight = jnp.sum(member[:, :, None] * req_weight[None], axis=1)
+
+    x = line_gather(tokens)
+    a_other = to_place(a_proj[0], 1)
+    b = line_gather(jnp.concatenate([b_query[0], b_value[0]], axis=1))
+    g_own = jnp.concatenate([grad_query, grad_value], axis=1)
+    g_other = to_place(g_own, 1)
+    weight_other = to_place(weight[:, 1::2], 1)
+
+    a_both = jnp.concatenate([a_proj[0], a_other], axis=1)
+    x_all = jnp.concatenate(x, axis=0)
+    hidden = sum_cores(dot(x_all, a_both, ((1,), (0,)))).astype(BF16)
+    count = tokens.shape[0]
+    rank2 = 2 * rank
+    hidden_own, hidden_other = [], []
+    for j in range(LINE):
+        block = hidden[j * count : (j + 1) * count]
+        mine = block[:, :rank2]
+        hidden_own.append(to_place(mine, 2 * j) if j else mine)
+        hidden_other.append(to_place(block[:, rank2:], 2 * j + 1))
+
+    b_all = jnp.concatenate(b, axis=0)
+    g_all = jnp.concatenate([g_own, g_other], axis=0)
+    slope_q = dot(g_all[:, :wide], b_all[:, :wide], ((1,), (1,)))
+    slope_v = dot(g_all[:, wide:], b_all[:, wide:], ((1,), (1,)))
+    slopes = sum_cores(jnp.stack([slope_q.reshape(-1, LINE, rank), slope_v.reshape(-1, LINE, rank)], axis=2))
+    slopes = slopes.reshape(-1, LINE, rank2)
+    weights = jnp.concatenate([weight[:, 0::2], weight_other], axis=0)
+    grad_hidden = (weights[:, :, None] * slopes).astype(BF16)
+    from_own, from_other = [], []
+    for j in range(LINE):
+        mine = grad_hidden[:count, j]
+        from_own.append(to_place(mine, 2 * j) if j else mine)
+        from_other.append(to_place(grad_hidden[count:, j], 2 * j + 1))
+    grad_cols = jnp.concatenate([jnp.concatenate(from_own, 0), jnp.concatenate(from_other, 0)], axis=1)
+    grad_a_both = dot(x_all, grad_cols, ((0,), (0,)))
+    grad_a = grad_a_both[:, :rank2] + to_place(grad_a_both[:, rank2:].astype(BF16), 1).astype(F32)
+
+    hid = jnp.concatenate([jnp.stack(hidden_own, 1), jnp.stack(hidden_other, 1)], axis=0).astype(F32)
+    weighted = (weights[:, :, None] * hid).astype(BF16)
+    weighted_q = weighted[:, :, :rank].reshape(-1, LINE * rank)
+    weighted_v = weighted[:, :, rank:].reshape(-1, LINE * rank)
+    grad_bq = dot(weighted_q, g_all[:, :wide], ((0,), (0,)))
+    grad_bv = dot(weighted_v, g_all[:, wide:], ((0,), (0,)))
+    grad_b = jnp.concatenate([grad_bq, grad_bv], axis=1)
+    grad_b_sum = grad_b[:rank]
+    for j in range(1, LINE):
+        grad_b_sum = grad_b_sum + to_place(grad_b[j * rank : (j + 1) * rank].astype(BF16), 2 * j).astype(F32)
+
+    out = jnp.concatenate(
+        [
+            dot(weighted_q, b_all[:, :wide], ((1,), (0,))),
+            dot(weighted_v, b_all[:, wide:], ((1,), (0,))),
+        ],
+        axis=1,
+    )
+    out = out[:count] + to_place(out[count:].astype(BF16), 1).astype(F32)
+
+    row_grad = jnp.sum(slopes * hid, axis=2)
+    row_grad = jnp.stack([row_grad[:count], to_place(row_grad[count:], 1)], axis=2).reshape(count, -1)
+    req_grad = jnp.sum(member[:, :, None] * row_grad[:, None, :], axis=0)
+    grad_mix = jnp.sum(jnp.where(picks, req_grad[:, None, :], 0.0), axis=2)
+    return (
+        out[:, :wide].astype(BF16),
+        out[:, wide:].astype(BF16),
+        grad_a.astype(BF16)[None],
+        grad_b_sum[:, :wide].astype(BF16)[None],
+        grad_b_sum[:, wide:].astype(BF16)[None],
+        grad_mix[None],
+    )
+
+
 def solution(mesh):
     in_specs = (
         P(("groups", "expert"), "tensor"),
@@ -171,4 +292,5 @@
         P(("groups", "expert"), None, "tensor"),
         P(("groups", "expert"), None, None),
     )
+    shards = pair_plan if mesh.shape["expert"] == LINE * PAIR else row_exchange
     return jax.shard_map(shards, mesh=mesh, in_specs=in_specs, out_specs=out_specs, check_vma=False)

time: 445 us -> 143 us (0.32)
  waiting for transfers between devices: 190 us -> 73.9 us
  blocking collectives: 107 us -> 0 us
  local copies, waits for them, and re-layouts: 53.1 us -> 5.43 us
  other arithmetic: 37 us -> 10.4 us
  starting transfers between devices: 26.7 us -> 47.8 us
  between operations: 14.4 us -> 1.15 us
  matrix products: 15.4 us -> 3.61 us
    all_to_all x5 -> x0, waiting for transfers between devices: 184 us -> none  [the longest x1 82.4 us: shards(): lax.all_to_all(x_rows, 'expert', split_axis=0, concat_axis=0, tiled=True)]
    all_to_all x2 -> x0, blocking collectives: 107 us -> none  [the longest x1 97.3 us: shards(): lax.all_to_all(query_rows, 'expert', split_axis=0, concat_axis=0, tiled=T...]
    ppermute x0 -> x35, waiting for transfers between devices: none -> 73.9 us  [the longest x25 39.2 us: to_place(): lax.ppermute(array, 'expert', [(i, i ^ place) for i in range(LINE * PAIR)])]
    ppermute x0 -> x35, starting transfers between devices: none -> 47.8 us  [the longest x25 37.8 us: to_place(): lax.ppermute(array, 'expert', [(i, i ^ place) for i in range(LINE * PAIR)])]
    all_to_all x5 -> x0, starting transfers between devices: 26.7 us -> none  [the longest x1 7.25 us: shards(): lax.all_to_all(value_rows, 'expert', split_axis=0, concat_axis=0, tiled=T...]
    scatter-add x2 -> x0, other arithmetic: 23.7 us -> none  [the longest x1 15.8 us: shards(): out_query = jnp.zeros((tok_count, feat_width), jnp.float32).at[flat_idx]....]
    gather x10 -> x0, local copies, waits for them, and re-layouts: 21.2 us -> none  [the longest x2 6.31 us: shards(): tokens[flat_idx]]
    reshape x6 -> x0, local copies, waits for them, and re-layouts: 17.5 us -> none  [the longest x1 5.46 us: shards(): up_query.reshape(slot_count, row_count, feat_width)]
  transfers between devices with their start and end apart: 6 -> 35, of which waited for: 6 -> 15; matrix products, arithmetic and copies ran while one was open for 13% -> 10% of each run, Pallas kernels for 0% -> 0%
where the time goes in v1:
time: 143 us; the launch traced here: 142 us
  waiting for transfers between devices  73.9 us (52%)
  starting transfers between devices  47.8 us (33%)
  other arithmetic  10.4 us (7%)
  local copies, waits for them, and re-layouts  5.43 us (4%)
  matrix products  3.61 us (3%)
    ppermute x25, waiting for transfers between devices, to_place(): lax.ppermute(array, 'expert', [(i, i ^ place) for i in range(LINE * PAIR)])  39.2 us
    ppermute x25, starting transfers between devices, to_place(): lax.ppermute(array, 'expert', [(i, i ^ place) for i in range(LINE * PAIR)])  37.8 us
    ppermute x2, waiting for transfers between devices, line_gather(): second_out = lax.ppermute(inner, 'expert', OUT)  21 us
    ppermute x2, waiting for transfers between devices, line_gather(): third_out = lax.ppermute(second_mid, 'expert', OUT)  13.2 us
    dot_general x8, matrix products, dot(): return lax.dot_general(a, b, (over, ((), ())), preferred_element_type=F32)  3.61 us
  transfers between devices with their start and end apart: 35, of which 15 were waited for; matrix products, arithmetic and copies ran while one was open for 10% of the time, Pallas kernels for 0%

profile of v1, /device:TPU:0, one launch (start us, length us, event | category | flops | bytes accessed | tf_op | source)
XLA Modules:
  0.0 142.3 jit_solution(8738596136740153529)
XLA Ops:
  0.6 3.1 %collective-permute-start.1 = (bf16[128,2048]{1,0:T(8,128)(2,1)}, bf16[128,2048]{1,0:T(8,128)(2,1)S(1)}, u32[]{:S(2)}, u32[]{:S(2)}) collective-permute-start(bf16[128,2048]{1,0:T(8,128)(2,1)} %param.10), channel_id=1, source_target_pairs={{0,4},{2,6},{4,0},{6,2},{8,12},{10,14},{12,8},{14,10},{1,5},{3,7},... | collective-permute-start | bytes 1572872 | tf_op jit(solution)/shard_map/ppermute | solution.py:160
  6.9 2.0 %collective-permute-start.21 = (bf16[128,2560]{1,0:T(8,128)(2,1)S(1)}, bf16[128,2560]{1,0:T(8,128)(2,1)S(1)}, u32[]{:S(2)}, u32[]{:S(2)}) collective-permute-start(bf16[128,2560]{1,0:T(8,128)(2,1)S(1)} %constant_dynamic-update-slice_fusion), channel_id=1, source_target_pairs={{0,2},{2,0},{4,6},{6,4},{8,10},{10,8},{12,14},{14,12},{1,3},{3,1},... | collective-permute-start | bytes 1966088 | tf_op jit(solution)/shard_map/ppermute | solution.py:160
  9.5 13.3 %collective-permute-done.15 = bf16[64,2560]{1,0:T(8,128)(2,1)S(1)} collective-permute-done((bf16[64,2560]{1,0:T(8,128)(2,1)S(1)}, bf16[64,2560]{1,0:T(8,128)(2,1)S(1)}, u32[]{:S(2)}, u32[]{:S(2)}) %collective-permute-start.15) | collective-permute-done | bytes 327712 | tf_op jit(solution)/shard_map/ppermute | solution.py:160
  23.6 1.5 %collective-permute-start.2 = (bf16[128,2048]{1,0:T(8,128)(2,1)}, bf16[128,2048]{1,0:T(8,128)(2,1)}, u32[]{:S(2)}, u32[]{:S(2)}) collective-permute-start(bf16[128,2048]{1,0:T(8,128)(2,1)} %param.10), channel_id=1, source_target_pairs={{4,8},{6,10},{8,4},{10,6},{5,9},{7,11},{9,5},{11,7},{20,24},{22,26... | collective-permute-start | bytes 1572872 | tf_op jit(solution)/shard_map/ppermute | solution.py:169
  25.0 1.5 %collective-permute-start.4 = (bf16[128,2048]{1,0:T(8,128)(2,1)S(1)}, bf16[128,2048]{1,0:T(8,128)(2,1)}, u32[]{:S(2)}, u32[]{:S(2)}) collective-permute-start(bf16[128,2048]{1,0:T(8,128)(2,1)S(1)} %collective-permute-done.1), channel_id=1, source_target_pairs={{4,8},{6,10},{8,4},{10,6},{5,9},{7,11},{9,5},{11,7},{20,24},{22,26... | collective-permute-start | bytes 1572872 | tf_op jit(solution)/shard_map/ppermute | solution.py:171
  28.4 1.3 collective-permute-start.19
  30.4 1.7 %collective-permute-start.6 = (bf16[2048,128]{1,0:T(8,128)(2,1)}, bf16[2048,128]{1,0:T(8,128)(2,1)S(1)}, u32[]{:S(2)}, u32[]{:S(2)}) collective-permute-start(bf16[2048,128]{1,0:T(8,128)(2,1)} %bitcast.107), channel_id=1, source_target_pairs={{0,2},{2,0},{4,6},{6,4},{8,10},{10,8},{12,14},{14,12},{1,3},{3,1},... | collective-permute-start | bytes 1572872 | tf_op jit(solution)/shard_map/ppermute | solution.py:160
  33.4 1.3 collective-permute-start.5
  34.7 9.8 %collective-permute-done.17 = bf16[64,2560]{1,0:T(8,128)(2,1)S(1)} collective-permute-done((bf16[64,2560]{1,0:T(8,128)(2,1)S(1)}, bf16[64,2560]{1,0:T(8,128)(2,1)S(1)}, u32[]{:S(2)}, u32[]{:S(2)}) %collective-permute-start.17) | collective-permute-done | bytes 327712 | tf_op jit(solution)/shard_map/ppermute | solution.py:170
  44.6 5.2 %collective-permute-done.19 = bf16[64,2560]{1,0:T(8,128)(2,1)S(1)} collective-permute-done((bf16[64,2560]{1,0:T(8,128)(2,1)S(1)}, bf16[64,2560]{1,0:T(8,128)(2,1)S(1)}, u32[]{:S(2)}, u32[]{:S(2)}) %collective-permute-start.19) | collective-permute-done | bytes 327712 | tf_op jit(solution)/shard_map/ppermute | solution.py:172
  51.1 11.2 %collective-permute-done.3 = bf16[128,2048]{1,0:T(8,128)(2,1)S(1)} collective-permute-done((bf16[128,2048]{1,0:T(8,128)(2,1)}, bf16[128,2048]{1,0:T(8,128)(2,1)S(1)}, u32[]{:S(2)}, u32[]{:S(2)}) %collective-permute-start.3) | collective-permute-done | bytes 524320 | tf_op jit(solution)/shard_map/ppermute | solution.py:170
  63.4 8.0 %collective-permute-done.5 = bf16[128,2048]{1,0:T(8,128)(2,1)S(1)} collective-permute-done((bf16[128,2048]{1,0:T(8,128)(2,1)}, bf16[128,2048]{1,0:T(8,128)(2,1)S(1)}, u32[]{:S(2)}, u32[]{:S(2)}) %collective-permute-start.5) | collective-permute-done | bytes 524320 | tf_op jit(solution)/shard_map/ppermute | solution.py:172
  75.6 2.3 %collective-permute-start.14 = (bf16[128,128]{0,1:T(8,128)(2,1)S(1)}, bf16[128,128]{0,1:T(8,128)(2,1)S(1)}, u32[]{:S(2)}, u32[]{:S(2)}) collective-permute-start(bf16[128,128]{0,1:T(8,128)(2,1)S(1)} %get-tuple-element.25), channel_id=1, source_target_pairs={{0,14},{2,12},{4,10},{6,8},{8,6},{10,4},{12,2},{14,0},{1,15},{3,13... | collective-permute-start | bytes 98312 | tf_op jit(solution)/shard_map/ppermute | solution.py:160
  77.9 3.9 %collective-permute-start.12 = (bf16[128,128]{0,1:T(8,128)(2,1)S(1)}, bf16[128,128]{0,1:T(8,128)(2,1)S(1)}, u32[]{:S(2)}, u32[]{:S(2)}) collective-permute-start(bf16[128,128]{0,1:T(8,128)(2,1)S(1)} %get-tuple-element.27), channel_id=1, source_target_pairs={{0,6},{2,4},{4,2},{6,0},{8,14},{10,12},{12,10},{14,8},{1,7},{3,5},... | collective-permute-start | bytes 98312 | tf_op jit(solution)/shard_map/ppermute | solution.py:160
  82.4 1.5 %collective-permute-start.10 = (bf16[128,128]{0,1:T(8,128)(2,1)S(1)}, bf16[128,128]{0,1:T(8,128)(2,1)S(1)}, u32[]{:S(2)}, u32[]{:S(2)}) collective-permute-start(bf16[128,128]{0,1:T(8,128)(2,1)S(1)} %get-tuple-element.29), channel_id=1, source_target_pairs={{0,12},{2,14},{4,8},{6,10},{8,4},{10,6},{12,0},{14,2},{1,13},{3,15... | collective-permute-start | bytes 98312 | tf_op jit(solution)/shard_map/ppermute | solution.py:160
  84.0 2.8 %collective-permute-start.8 = (bf16[128,128]{0,1:T(8,128)(2,1)S(1)}, bf16[128,128]{0,1:T(8,128)(2,1)S(1)}, u32[]{:S(2)}, u32[]{:S(2)}) collective-permute-start(bf16[128,128]{0,1:T(8,128)(2,1)S(1)} %get-tuple-element.31), channel_id=1, source_target_pairs={{0,4},{2,6},{4,0},{6,2},{8,12},{10,14},{12,8},{14,10},{1,5},{3,7},... | collective-permute-start | bytes 98312 | tf_op jit(solution)/shard_map/ppermute | solution.py:160
  86.8 1.3 collective-permute-done.10
  89.9 1.5 %collective-permute-start.34 = (f32[128,4]{0,1:T(4,128)S(1)}, f32[128,4]{0,1:T(4,128)S(1)}, u32[]{:S(2)}, u32[]{:S(2)}) collective-permute-start(f32[128,4]{0,1:T(4,128)S(1)} %get-tuple-element.35), channel_id=1, source_target_pairs={{0,2},{2,0},{4,6},{6,4},{8,10},{10,8},{12,14},{14,12},{1,3},{3,1},... | collective-permute-start | bytes 6152 | tf_op jit(solution)/shard_map/ppermute | solution.py:160
  91.5 2.0 %collective-permute-done.34 = f32[128,4]{0,1:T(4,128)S(1)} collective-permute-done((f32[128,4]{0,1:T(4,128)S(1)}, f32[128,4]{0,1:T(4,128)S(1)}, u32[]{:S(2)}, u32[]{:S(2)}) %collective-permute-start.34) | collective-permute-done | bytes 2080 | tf_op jit(solution)/shard_map/ppermute | solution.py:160
  93.8 1.5 %collective-permute-start = (f32[128,4]{0,1:T(4,128)S(1)}, f32[128,4]{0,1:T(4,128)S(1)}, u32[]{:S(2)}, u32[]{:S(2)}) collective-permute-start(f32[128,4]{0,1:T(4,128)S(1)} %slice.140), channel_id=1, source_target_pairs={{0,2},{2,0},{4,6},{6,4},{8,10},{10,8},{12,14},{14,12},{1,3},{3,1},... | collective-permute-start | bytes 6152 | tf_op jit(solution)/shard_map/ppermute | solution.py:160
  95.9 1.5 %collective-permute-done = f32[128,4]{0,1:T(4,128)S(1)} collective-permute-done((f32[128,4]{0,1:T(4,128)S(1)}, f32[128,4]{0,1:T(4,128)S(1)}, u32[]{:S(2)}, u32[]{:S(2)}) %collective-permute-start) | collective-permute-done | bytes 2080 | tf_op jit(solution)/shard_map/ppermute | solution.py:160
  98.6 3.0 %collective-permute-start.29 = (bf16[128,128]{0,1:T(8,128)(2,1)S(1)}, bf16[128,128]{0,1:T(8,128)(2,1)S(1)}, u32[]{:S(2)}, u32[]{:S(2)}) collective-permute-start(bf16[128,128]{0,1:T(8,128)(2,1)S(1)} %get-tuple-element.14), channel_id=1, source_target_pairs={{0,14},{2,12},{4,10},{6,8},{8,6},{10,4},{12,2},{14,0},{1,15},{3,13... | collective-permute-start | bytes 98312 | tf_op jit(solution)/shard_map/ppermute | solution.py:160
  102.7 2.2 %collective-permute-start.27 = (bf16[128,128]{0,1:T(8,128)(2,1)S(1)}, bf16[128,128]{0,1:T(8,128)(2,1)S(1)}, u32[]{:S(2)}, u32[]{:S(2)}) collective-permute-start(bf16[128,128]{0,1:T(8,128)(2,1)S(1)} %get-tuple-element.16), channel_id=1, source_target_pairs={{0,6},{2,4},{4,2},{6,0},{8,14},{10,12},{12,10},{14,8},{1,7},{3,5},... | collective-permute-start | bytes 98312 | tf_op jit(solution)/shard_map/ppermute | solution.py:160
  105.4 2.0 %collective-permute-start.25 = (bf16[128,128]{0,1:T(8,128)(2,1)S(1)}, bf16[128,128]{0,1:T(8,128)(2,1)S(1)}, u32[]{:S(2)}, u32[]{:S(2)}) collective-permute-start(bf16[128,128]{0,1:T(8,128)(2,1)S(1)} %get-tuple-element.18), channel_id=1, source_target_pairs={{0,12},{2,14},{4,8},{6,10},{8,4},{10,6},{12,0},{14,2},{1,13},{3,15... | collective-permute-start | bytes 98312 | tf_op jit(solution)/shard_map/ppermute | solution.py:160
  109.4 2.2 %collective-permute-start.23 = (bf16[128,128]{0,1:T(8,128)(2,1)S(1)}, bf16[128,128]{0,1:T(8,128)(2,1)S(1)}, u32[]{:S(2)}, u32[]{:S(2)}) collective-permute-start(bf16[128,128]{0,1:T(8,128)(2,1)S(1)} %get-tuple-element.20), channel_id=1, source_target_pairs={{0,4},{2,6},{4,0},{6,2},{8,12},{10,14},{12,8},{14,10},{1,5},{3,7},... | collective-permute-start | bytes 98312 | tf_op jit(solution)/shard_map/ppermute | solution.py:160
  111.6 2.0 %collective-permute-start.33 = (bf16[64,2560]{1,0:T(8,128)(2,1)S(1)}, bf16[64,2560]{1,0:T(8,128)(2,1)S(1)}, u32[]{:S(2)}, u32[]{:S(2)}) collective-permute-start(bf16[64,2560]{1,0:T(8,128)(2,1)S(1)} %get-tuple-element.11), channel_id=1, source_target_pairs={{0,12},{2,14},{4,8},{6,10},{8,4},{10,6},{12,0},{14,2},{1,13},{3,15... | collective-permute-start | bytes 983048 | tf_op jit(solution)/shard_map/ppermute | solution.py:160
  113.6 1.4 %collective-permute-start.32 = (bf16[64,2560]{1,0:T(8,128)(2,1)S(1)}, bf16[64,2560]{1,0:T(8,128)(2,1)S(1)}, u32[]{:S(2)}, u32[]{:S(2)}) collective-permute-start(bf16[64,2560]{1,0:T(8,128)(2,1)S(1)} %get-tuple-element.12), channel_id=1, source_target_pairs={{0,8},{2,10},{4,12},{6,14},{8,0},{10,2},{12,4},{14,6},{1,9},{3,11}... | collective-permute-start | bytes 983048 | tf_op jit(solution)/shard_map/ppermute | solution.py:160
  115.1 1.6 %collective-permute-done.24 = bf16[128,128]{0,1:T(8,128)(2,1)S(1)} collective-permute-done((bf16[128,128]{0,1:T(8,128)(2,1)S(1)}, bf16[128,128]{0,1:T(8,128)(2,1)S(1)}, u32[]{:S(2)}, u32[]{:S(2)}) %collective-permute-start.24) | collective-permute-done | bytes 32800 | tf_op jit(solution)/shard_map/ppermute | solution.py:160
  116.8 1.5 %collective-permute-start.20 = (bf16[128,2560]{1,0:T(8,128)(2,1)S(1)}, bf16[128,2560]{1,0:T(8,128)(2,1)S(1)}, u32[]{:S(2)}, u32[]{:S(2)}) collective-permute-start(bf16[128,2560]{1,0:T(8,128)(2,1)S(1)} %fusion.4), channel_id=1, source_target_pairs={{0,2},{2,0},{4,6},{6,4},{8,10},{10,8},{12,14},{14,12},{1,3},{3,1},... | collective-permute-start | bytes 1966088 | tf_op jit(solution)/shard_map/ppermute | solution.py:160
  119.7 1.5 %collective-permute-done.31 = bf16[64,2560]{1,0:T(8,128)(2,1)S(1)} collective-permute-done((bf16[64,2560]{1,0:T(8,128)(2,1)S(1)}, bf16[64,2560]{1,0:T(8,128)(2,1)S(1)}, u32[]{:S(2)}, u32[]{:S(2)}) %collective-permute-start.31) | collective-permute-done | bytes 327712 | tf_op jit(solution)/shard_map/ppermute | solution.py:160
  121.2 5.9 %collective-permute-done.33 = bf16[64,2560]{1,0:T(8,128)(2,1)S(1)} collective-permute-done((bf16[64,2560]{1,0:T(8,128)(2,1)S(1)}, bf16[64,2560]{1,0:T(8,128)(2,1)S(1)}, u32[]{:S(2)}, u32[]{:S(2)}) %collective-permute-start.33) | collective-permute-done | bytes 327712 | tf_op jit(solution)/shard_map/ppermute | solution.py:160
  127.1 11.2 %collective-permute-done.32 = bf16[64,2560]{1,0:T(8,128)(2,1)S(1)} collective-permute-done((bf16[64,2560]{1,0:T(8,128)(2,1)S(1)}, bf16[64,2560]{1,0:T(8,128)(2,1)S(1)}, u32[]{:S(2)}, u32[]{:S(2)}) %collective-permute-start.32) | collective-permute-done | bytes 327712 | tf_op jit(solution)/shard_map/ppermute | solution.py:160
  (119 shorter events, 28.8 us)
Async XLA Ops:
  0.6 24.4 %collective-permute-start.1 = (bf16[128,2048]{1,0:T(8,128)(2,1)}, bf16[128,2048]{1,0:T(8,128)(2,1)S(1)}, u32[]{:S(2)}, u32[]{:S(2)}) collective-permute-start(bf16[128,2048]{1,0:T(8,128)(2,1)} %param.10), channel_id=1, source_target_pairs={{0,4},{2,6},{4,0},{6,2},{8,12},{10,14},{12,8},{14,10},{1,5},{3,7},... | collective-permute-start | bytes 1572872 | tf_op jit(solution)/shard_map/ppermute | solution.py:160
  4.7 18.1 %collective-permute-start.15 = (bf16[64,2560]{1,0:T(8,128)(2,1)S(1)}, bf16[64,2560]{1,0:T(8,128)(2,1)S(1)}, u32[]{:S(2)}, u32[]{:S(2)}) collective-permute-start(bf16[64,2560]{1,0:T(8,128)(2,1)S(1)} %pad_maximum_fusion.7), channel_id=1, source_target_pairs={{0,4},{2,6},{4,0},{6,2},{8,12},{10,14},{12,8},{14,10},{1,5},{3,7},... | collective-permute-start | bytes 983048 | tf_op jit(solution)/shard_map/ppermute | solution.py:160
  6.9 25.2 %collective-permute-start.21 = (bf16[128,2560]{1,0:T(8,128)(2,1)S(1)}, bf16[128,2560]{1,0:T(8,128)(2,1)S(1)}, u32[]{:S(2)}, u32[]{:S(2)}) collective-permute-start(bf16[128,2560]{1,0:T(8,128)(2,1)S(1)} %constant_dynamic-update-slice_fusion), channel_id=1, source_target_pairs={{0,2},{2,0},{4,6},{6,4},{8,10},{10,8},{12,14},{14,12},{1,3},{3,1},... | collective-permute-start | bytes 1966088 | tf_op jit(solution)/shard_map/ppermute | solution.py:160
  8.9 18.3 %collective-permute-start.16 = (bf16[64,2560]{1,0:T(8,128)(2,1)S(1)}, bf16[64,2560]{1,0:T(8,128)(2,1)S(1)}, u32[]{:S(2)}, u32[]{:S(2)}) collective-permute-start(bf16[64,2560]{1,0:T(8,128)(2,1)S(1)} %pad_maximum_fusion.7), channel_id=1, source_target_pairs={{4,8},{6,10},{8,4},{10,6},{5,9},{7,11},{9,5},{11,7},{20,24},{22,26... | collective-permute-start | bytes 983048 | tf_op jit(solution)/shard_map/ppermute | solution.py:169
  22.9 5.5 %collective-permute-start.18 = (bf16[64,2560]{1,0:T(8,128)(2,1)S(1)}, bf16[64,2560]{1,0:T(8,128)(2,1)S(1)}, u32[]{:S(2)}, u32[]{:S(2)}) collective-permute-start(bf16[64,2560]{1,0:T(8,128)(2,1)S(1)} %collective-permute-done.15), channel_id=1, source_target_pairs={{4,8},{6,10},{8,4},{10,6},{5,9},{7,11},{9,5},{11,7},{20,24},{22,26... | collective-permute-start | bytes 983048 | tf_op jit(solution)/shard_map/ppermute | solution.py:171
  23.6 6.9 %collective-permute-start.2 = (bf16[128,2048]{1,0:T(8,128)(2,1)}, bf16[128,2048]{1,0:T(8,128)(2,1)}, u32[]{:S(2)}, u32[]{:S(2)}) collective-permute-start(bf16[128,2048]{1,0:T(8,128)(2,1)} %param.10), channel_id=1, source_target_pairs={{4,8},{6,10},{8,4},{10,6},{5,9},{7,11},{9,5},{11,7},{20,24},{22,26... | collective-permute-start | bytes 1572872 | tf_op jit(solution)/shard_map/ppermute | solution.py:169
  25.0 8.4 %collective-permute-start.4 = (bf16[128,2048]{1,0:T(8,128)(2,1)S(1)}, bf16[128,2048]{1,0:T(8,128)(2,1)}, u32[]{:S(2)}, u32[]{:S(2)}) collective-permute-start(bf16[128,2048]{1,0:T(8,128)(2,1)S(1)} %collective-permute-done.1), channel_id=1, source_target_pairs={{4,8},{6,10},{8,4},{10,6},{5,9},{7,11},{9,5},{11,7},{20,24},{22,26... | collective-permute-start | bytes 1572872 | tf_op jit(solution)/shard_map/ppermute | solution.py:171
  27.1 17.4 %collective-permute-start.17 = (bf16[64,2560]{1,0:T(8,128)(2,1)S(1)}, bf16[64,2560]{1,0:T(8,128)(2,1)S(1)}, u32[]{:S(2)}, u32[]{:S(2)}) collective-permute-start(bf16[64,2560]{1,0:T(8,128)(2,1)S(1)} %collective-permute-done.16), channel_id=1, source_target_pairs={{4,0},{6,2},{8,12},{10,14},{5,1},{7,3},{9,13},{11,15},{20,16},{22,... | collective-permute-start | bytes 983048 | tf_op jit(solution)/shard_map/ppermute | solution.py:170
  28.4 21.4 %collective-permute-start.19 = (bf16[64,2560]{1,0:T(8,128)(2,1)S(1)}, bf16[64,2560]{1,0:T(8,128)(2,1)S(1)}, u32[]{:S(2)}, u32[]{:S(2)}) collective-permute-start(bf16[64,2560]{1,0:T(8,128)(2,1)S(1)} %collective-permute-done.18), channel_id=1, source_target_pairs={{4,0},{6,2},{8,12},{10,14},{5,1},{7,3},{9,13},{11,15},{20,16},{22,... | collective-permute-start | bytes 983048 | tf_op jit(solution)/shard_map/ppermute | solution.py:172
  30.4 42.2 %collective-permute-start.6 = (bf16[2048,128]{1,0:T(8,128)(2,1)}, bf16[2048,128]{1,0:T(8,128)(2,1)S(1)}, u32[]{:S(2)}, u32[]{:S(2)}) collective-permute-start(bf16[2048,128]{1,0:T(8,128)(2,1)} %bitcast.107), channel_id=1, source_target_pairs={{0,2},{2,0},{4,6},{6,4},{8,10},{10,8},{12,14},{14,12},{1,3},{3,1},... | collective-permute-start | bytes 1572872 | tf_op jit(solution)/shard_map/ppermute | solution.py:160
  32.1 30.2 %collective-permute-start.3 = (bf16[128,2048]{1,0:T(8,128)(2,1)}, bf16[128,2048]{1,0:T(8,128)(2,1)S(1)}, u32[]{:S(2)}, u32[]{:S(2)}) collective-permute-start(bf16[128,2048]{1,0:T(8,128)(2,1)} %collective-permute-done.2), channel_id=1, source_target_pairs={{4,0},{6,2},{8,12},{10,14},{5,1},{7,3},{9,13},{11,15},{20,16},{22,... | collective-permute-start | bytes 1572872 | tf_op jit(solution)/shard_map/ppermute | solution.py:170
  33.4 38.0 %collective-permute-start.5 = (bf16[128,2048]{1,0:T(8,128)(2,1)}, bf16[128,2048]{1,0:T(8,128)(2,1)S(1)}, u32[]{:S(2)}, u32[]{:S(2)}) collective-permute-start(bf16[128,2048]{1,0:T(8,128)(2,1)} %collective-permute-done.4), channel_id=1, source_target_pairs={{4,0},{6,2},{8,12},{10,14},{5,1},{7,3},{9,13},{11,15},{20,16},{22,... | collective-permute-start | bytes 1572872 | tf_op jit(solution)/shard_map/ppermute | solution.py:172
  74.3 8.1 %collective-permute-start.22 = (f32[256,4,2,64]{0,3,2,1:T(8,128)S(1)}, f32[256,4,2,64]{0,3,2,1:T(8,128)S(1)}, u32[]{:S(2)}, u32[]{:S(2)}) collective-permute-start(f32[256,4,2,64]{0,3,2,1:T(8,128)S(1)} %pad_maximum_fusion.4), channel_id=1, source_target_pairs={{0,1},{1,0},{2,3},{3,2},{4,5},{5,4},{6,7},{7,6},{8,9},{9,8},{10,11... | collective-permute-start | bytes 1572872 | tf_op jit(solution)/shard_map/ppermute | solution.py:164
  75.6 8.4 %collective-permute-start.14 = (bf16[128,128]{0,1:T(8,128)(2,1)S(1)}, bf16[128,128]{0,1:T(8,128)(2,1)S(1)}, u32[]{:S(2)}, u32[]{:S(2)}) collective-permute-start(bf16[128,128]{0,1:T(8,128)(2,1)S(1)} %get-tuple-element.25), channel_id=1, source_target_pairs={{0,14},{2,12},{4,10},{6,8},{8,6},{10,4},{12,2},{14,0},{1,15},{3,13... | collective-permute-start | bytes 98312 | tf_op jit(solution)/shard_map/ppermute | solution.py:160
  77.9 6.1 %collective-permute-start.13 = (bf16[128,128]{0,1:T(8,128)(2,1)S(1)}, bf16[128,128]{0,1:T(8,128)(2,1)S(1)}, u32[]{:S(2)}, u32[]{:S(2)}) collective-permute-start(bf16[128,128]{0,1:T(8,128)(2,1)S(1)} %get-tuple-element.26), channel_id=1, source_target_pairs={{0,10},{2,8},{4,14},{6,12},{8,2},{10,0},{12,6},{14,4},{1,11},{3,9}... | collective-permute-start | bytes 98312 | tf_op jit(solution)/shard_map/ppermute | solution.py:160
  77.9 8.9 %collective-permute-start.12 = (bf16[128,128]{0,1:T(8,128)(2,1)S(1)}, bf16[128,128]{0,1:T(8,128)(2,1)S(1)}, u32[]{:S(2)}, u32[]{:S(2)}) collective-permute-start(bf16[128,128]{0,1:T(8,128)(2,1)S(1)} %get-tuple-element.27), channel_id=1, source_target_pairs={{0,6},{2,4},{4,2},{6,0},{8,14},{10,12},{12,10},{14,8},{1,7},{3,5},... | collective-permute-start | bytes 98312 | tf_op jit(solution)/shard_map/ppermute | solution.py:160
  81.8 5.0 %collective-permute-start.11 = (bf16[128,128]{0,1:T(8,128)(2,1)S(1)}, bf16[128,128]{0,1:T(8,128)(2,1)S(1)}, u32[]{:S(2)}, u32[]{:S(2)}) collective-permute-start(bf16[128,128]{0,1:T(8,128)(2,1)S(1)} %get-tuple-element.28), channel_id=1, source_target_pairs={{0,2},{2,0},{4,6},{6,4},{8,10},{10,8},{12,14},{14,12},{1,3},{3,1},... | collective-permute-start | bytes 98312 | tf_op jit(solution)/shard_map/ppermute | solution.py:160
  82.4 5.7 %collective-permute-start.10 = (bf16[128,128]{0,1:T(8,128)(2,1)S(1)}, bf16[128,128]{0,1:T(8,128)(2,1)S(1)}, u32[]{:S(2)}, u32[]{:S(2)}) collective-permute-start(bf16[128,128]{0,1:T(8,128)(2,1)S(1)} %get-tuple-element.29), channel_id=1, source_target_pairs={{0,12},{2,14},{4,8},{6,10},{8,4},{10,6},{12,0},{14,2},{1,13},{3,15... | collective-permute-start | bytes 98312 | tf_op jit(solution)/shard_map/ppermute | solution.py:160
  83.9 5.0 %collective-permute-start.9 = (bf16[128,128]{0,1:T(8,128)(2,1)S(1)}, bf16[128,128]{0,1:T(8,128)(2,1)S(1)}, u32[]{:S(2)}, u32[]{:S(2)}) collective-permute-start(bf16[128,128]{0,1:T(8,128)(2,1)S(1)} %get-tuple-element.30), channel_id=1, source_target_pairs={{0,8},{2,10},{4,12},{6,14},{8,0},{10,2},{12,4},{14,6},{1,9},{3,11}... | collective-permute-start | bytes 98312 | tf_op jit(solution)/shard_map/ppermute | solution.py:160
  84.0 5.1 %collective-permute-start.8 = (bf16[128,128]{0,1:T(8,128)(2,1)S(1)}, bf16[128,128]{0,1:T(8,128)(2,1)S(1)}, u32[]{:S(2)}, u32[]{:S(2)}) collective-permute-start(bf16[128,128]{0,1:T(8,128)(2,1)S(1)} %get-tuple-element.31), channel_id=1, source_target_pairs={{0,4},{2,6},{4,0},{6,2},{8,12},{10,14},{12,8},{14,10},{1,5},{3,7},... | collective-permute-start | bytes 98312 | tf_op jit(solution)/shard_map/ppermute | solution.py:160
  98.6 10.5 %collective-permute-start.29 = (bf16[128,128]{0,1:T(8,128)(2,1)S(1)}, bf16[128,128]{0,1:T(8,128)(2,1)S(1)}, u32[]{:S(2)}, u32[]{:S(2)}) collective-permute-start(bf16[128,128]{0,1:T(8,128)(2,1)S(1)} %get-tuple-element.14), channel_id=1, source_target_pairs={{0,14},{2,12},{4,10},{6,8},{8,6},{10,4},{12,2},{14,0},{1,15},{3,13... | collective-permute-start | bytes 98312 | tf_op jit(solution)/shard_map/ppermute | solution.py:160
  101.6 7.8 %collective-permute-start.28 = (bf16[128,128]{0,1:T(8,128)(2,1)S(1)}, bf16[128,128]{0,1:T(8,128)(2,1)S(1)}, u32[]{:S(2)}, u32[]{:S(2)}) collective-permute-start(bf16[128,128]{0,1:T(8,128)(2,1)S(1)} %get-tuple-element.15), channel_id=1, source_target_pairs={{0,10},{2,8},{4,14},{6,12},{8,2},{10,0},{12,6},{14,4},{1,11},{3,9}... | collective-permute-start | bytes 98312 | tf_op jit(solution)/shard_map/ppermute | solution.py:160
  102.7 8.9 %collective-permute-start.27 = (bf16[128,128]{0,1:T(8,128)(2,1)S(1)}, bf16[128,128]{0,1:T(8,128)(2,1)S(1)}, u32[]{:S(2)}, u32[]{:S(2)}) collective-permute-start(bf16[128,128]{0,1:T(8,128)(2,1)S(1)} %get-tuple-element.16), channel_id=1, source_target_pairs={{0,6},{2,4},{4,2},{6,0},{8,14},{10,12},{12,10},{14,8},{1,7},{3,5},... | collective-permute-start | bytes 98312 | tf_op jit(solution)/shard_map/ppermute | solution.py:160
  104.8 6.8 %collective-permute-start.26 = (bf16[128,128]{0,1:T(8,128)(2,1)S(1)}, bf16[128,128]{0,1:T(8,128)(2,1)S(1)}, u32[]{:S(2)}, u32[]{:S(2)}) collective-permute-start(bf16[128,128]{0,1:T(8,128)(2,1)S(1)} %get-tuple-element.17), channel_id=1, source_target_pairs={{0,2},{2,0},{4,6},{6,4},{8,10},{10,8},{12,14},{14,12},{1,3},{3,1},... | collective-permute-start | bytes 98312 | tf_op jit(solution)/shard_map/ppermute | solution.py:160
  105.4 8.2 %collective-permute-start.25 = (bf16[128,128]{0,1:T(8,128)(2,1)S(1)}, bf16[128,128]{0,1:T(8,128)(2,1)S(1)}, u32[]{:S(2)}, u32[]{:S(2)}) collective-permute-start(bf16[128,128]{0,1:T(8,128)(2,1)S(1)} %get-tuple-element.18), channel_id=1, source_target_pairs={{0,12},{2,14},{4,8},{6,10},{8,4},{10,6},{12,0},{14,2},{1,13},{3,15... | collective-permute-start | bytes 98312 | tf_op jit(solution)/shard_map/ppermute | solution.py:160
  109.1 7.7 %collective-permute-start.24 = (bf16[128,128]{0,1:T(8,128)(2,1)S(1)}, bf16[128,128]{0,1:T(8,128)(2,1)S(1)}, u32[]{:S(2)}, u32[]{:S(2)}) collective-permute-start(bf16[128,128]{0,1:T(8,128)(2,1)S(1)} %get-tuple-element.19), channel_id=1, source_target_pairs={{0,8},{2,10},{4,12},{6,14},{8,0},{10,2},{12,4},{14,6},{1,9},{3,11}... | collective-permute-start | bytes 98312 | tf_op jit(solution)/shard_map/ppermute | solution.py:160
  109.4 8.9 %collective-permute-start.23 = (bf16[128,128]{0,1:T(8,128)(2,1)S(1)}, bf16[128,128]{0,1:T(8,128)(2,1)S(1)}, u32[]{:S(2)}, u32[]{:S(2)}) collective-permute-start(bf16[128,128]{0,1:T(8,128)(2,1)S(1)} %get-tuple-element.20), channel_id=1, source_target_pairs={{0,4},{2,6},{4,0},{6,2},{8,12},{10,14},{12,8},{14,10},{1,5},{3,7},... | collective-permute-start | bytes 98312 | tf_op jit(solution)/shard_map/ppermute | solution.py:160
  111.6 9.6 %collective-permute-start.31 = (bf16[64,2560]{1,0:T(8,128)(2,1)S(1)}, bf16[64,2560]{1,0:T(8,128)(2,1)S(1)}, u32[]{:S(2)}, u32[]{:S(2)}) collective-permute-start(bf16[64,2560]{1,0:T(8,128)(2,1)S(1)} %get-tuple-element.10), channel_id=1, source_target_pairs={{0,4},{2,6},{4,0},{6,2},{8,12},{10,14},{12,8},{14,10},{1,5},{3,7},... | collective-permute-start | bytes 983048 | tf_op jit(solution)/shard_map/ppermute | solution.py:160
  111.6 15.4 %collective-permute-start.33 = (bf16[64,2560]{1,0:T(8,128)(2,1)S(1)}, bf16[64,2560]{1,0:T(8,128)(2,1)S(1)}, u32[]{:S(2)}, u32[]{:S(2)}) collective-permute-start(bf16[64,2560]{1,0:T(8,128)(2,1)S(1)} %get-tuple-element.11), channel_id=1, source_target_pairs={{0,12},{2,14},{4,8},{6,10},{8,4},{10,6},{12,0},{14,2},{1,13},{3,15... | collective-permute-start | bytes 983048 | tf_op jit(solution)/shard_map/ppermute | solution.py:160
  113.6 24.6 %collective-permute-start.32 = (bf16[64,2560]{1,0:T(8,128)(2,1)S(1)}, bf16[64,2560]{1,0:T(8,128)(2,1)S(1)}, u32[]{:S(2)}, u32[]{:S(2)}) collective-permute-start(bf16[64,2560]{1,0:T(8,128)(2,1)S(1)} %get-tuple-element.12), channel_id=1, source_target_pairs={{0,8},{2,10},{4,12},{6,14},{8,0},{10,2},{12,4},{14,6},{1,9},{3,11}... | collective-permute-start | bytes 983048 | tf_op jit(solution)/shard_map/ppermute | solution.py:160
  116.8 23.9 %collective-permute-start.20 = (bf16[128,2560]{1,0:T(8,128)(2,1)S(1)}, bf16[128,2560]{1,0:T(8,128)(2,1)S(1)}, u32[]{:S(2)}, u32[]{:S(2)}) collective-permute-start(bf16[128,2560]{1,0:T(8,128)(2,1)S(1)} %fusion.4), channel_id=1, source_target_pairs={{0,2},{2,0},{4,6},{6,4},{8,10},{10,8},{12,14},{14,12},{1,3},{3,1},... | collective-permute-start | bytes 1966088 | tf_op jit(solution)/shard_map/ppermute | solution.py:160
  119.1 20.6 %collective-permute-start.30 = (bf16[2048,128]{1,0:T(8,128)(2,1)S(1)}, bf16[2048,128]{1,0:T(8,128)(2,1)S(1)}, u32[]{:S(2)}, u32[]{:S(2)}) collective-permute-start(bf16[2048,128]{1,0:T(8,128)(2,1)S(1)} %slice.269), channel_id=1, source_target_pairs={{0,2},{2,0},{4,6},{6,4},{8,10},{10,8},{12,14},{14,12},{1,3},{3,1},... | collective-permute-start | bytes 1572872 | tf_op jit(solution)/shard_map/ppermute | solution.py:160
  (18 other events, 262.2 us)

commit v2 on v0

--- a/solution.py
+++ b/solution.py
@@ -1,12 +1,14 @@
 import jax
 import jax.numpy as jnp
 from jax import lax
+from jax.experimental import pallas as pl
+from jax.experimental.pallas import tpu as pltpu
 from jax.sharding import PartitionSpec as P
 
 REQ_MOST = 5
 
 
-def shards(
+def row_exchange(
     tokens,
     grad_query,
     grad_value,
@@ -150,6 +152,406 @@
     )
 
 
+LINE, PAIR = 4, 2
+F32, BF16 = jnp.float32, jnp.bfloat16
+MID = [(2, 4), (3, 5), (4, 2), (5, 3)]
+OUT = [(2, 0), (3, 1), (4, 6), (5, 7)]
+ROWS, COLS, SAME = ((0,), (0,)), ((1,), (1,)), ((1,), (0,))
+LANES = 128
+PREP_VMEM = 60
+COST = pl.CostEstimate(flops=0, bytes_accessed=0, transcendentals=0)
+
+
+def to_place(array, place):
+    return lax.ppermute(array, "expert", [(i, i ^ place) for i in range(LINE * PAIR)])
+
+
+def other_core(part):
+    return lax.ppermute(part, "tensor", [(0, 1), (1, 0)])
+
+
+def line_gather(own):
+    near = to_place(own, 2)
+    inner = lax.ppermute(own, "expert", MID)
+    second_out = lax.ppermute(inner, "expert", OUT)
+    second_mid = lax.ppermute(near, "expert", MID)
+    third_out = lax.ppermute(second_mid, "expert", OUT)
+    return near, second_out, second_mid, inner, third_out
+
+
+def dot(a, b, over):
+    return lax.dot_general(a, b, (over, ((), ())), preferred_element_type=F32)
+
+
+def call(kernel, outs, *ins, vmem=24):
+    shapes = [jax.ShapeDtypeStruct(shape, dtype) for shape, dtype in outs]
+    return pl.pallas_call(
+        kernel,
+        out_shape=shapes,
+        in_specs=[pl.BlockSpec(memory_space=pltpu.VMEM)] * len(ins),
+        out_specs=[pl.BlockSpec(memory_space=pltpu.VMEM)] * len(outs),
+        compiler_params=pltpu.CompilerParams(vmem_limit_bytes=vmem * 1024 * 1024),
+        cost_estimate=COST,
+    )(*ins)
+
+
+def members(request_row, requests):
+    tok = request_row.shape[1]
+    ids = lax.broadcasted_iota(jnp.int32, (requests, tok), 0)
+    return ids == jnp.broadcast_to(request_row, (requests, tok))
+
+
+def picked(me_ref, ra_ref, rc_ref, k, place):
+    found = (jnp.broadcast_to(ra_ref[0, k : k + 1, :], place.shape) ^ me_ref[0]) == place
+    return found & jnp.broadcast_to(rc_ref[...] > k, place.shape)
+
+
+def prepare(me_ref, tr, ra, rc, rm, bq, bv, gq, gv, x, a, pay_ref, gw_ref, a_ref, tr_ref, ra_ref, rc_ref, rm_ref, sems):
+    count, wide = x.shape
+    rank, narrow = bv.shape[1:]
+    full = wide + narrow
+    step = rank * narrow // wide
+    pairs = [
+        (tr, tr_ref),
+        (ra, ra_ref),
+        (rc, rc_ref),
+        (rm, rm_ref),
+        (x, pay_ref.at[pl.ds(0, count)]),
+        (bq.at[0], pay_ref.at[pl.ds(count, rank)]),
+        (gq, gw_ref.at[:, pl.ds(0, wide)]),
+        (gv, gw_ref.at[:, pl.ds(wide, narrow)]),
+        (a, a_ref),
+    ]
+    for i in range(rank // step):
+        dst = pay_ref.at[pl.ds(count + rank, step), pl.ds(i * narrow, narrow)]
+        pairs.append((bv.at[0, pl.ds(i * step, step)], dst))
+    copies = [pltpu.make_async_copy(src, dst, sems.at[i]) for i, (src, dst) in enumerate(pairs)]
+    for copy in copies:
+        copy.start()
+    for copy in copies[:4]:
+        copy.wait()
+    requests = ra_ref.shape[2]
+    place = lax.broadcasted_iota(jnp.int32, (LANES, requests), 0)
+    total = jnp.zeros((LANES, requests), F32)
+    for k in range(4):
+        mix = jnp.broadcast_to(rm_ref[0, k : k + 1, :].astype(F32), place.shape)
+        total = total + jnp.where(picked(me_ref, ra_ref, rc_ref, k, place), mix, 0.0)
+    high = total.astype(BF16)
+    low = (total - high.astype(F32)).astype(BF16)
+    member = jnp.where(members(tr_ref[...], requests), 1.0, 0.0).astype(BF16)
+    gw_ref[:, full : full + LANES] = dot(member, high, ((0,), (1,))).astype(BF16)
+    gw_ref[:, full + LANES :] = dot(member, low, ((0,), (1,))).astype(BF16)
+    for copy in copies[4:]:
+        copy.wait()
+
+
+def weight_of(gw_ref, place):
+    full = gw_ref.shape[1] - 2 * LANES
+    high = gw_ref[:, full : full + LANES][:, place : place + 1].astype(F32)
+    low = gw_ref[:, full + LANES :][:, place : place + 1].astype(F32)
+    return high + low
+
+
+def parts_of(pay_ref, narrow):
+    rows, wide = pay_ref.shape
+    blocks = wide // narrow
+    step = (rows - LANES) // (blocks + 1)
+    rank = blocks * step
+    count = rows - rank - step
+    last = pay_ref[count + rank :, :]
+    value = jnp.concatenate([last[:, i * narrow : (i + 1) * narrow] for i in range(blocks)], axis=0)
+    return pay_ref[:count, :], pay_ref[count : count + rank, :], value
+
+
+def products(pay_refs, a_ref, ax_ref, gw_ref, gx_ref, out_ref):
+    rank2 = a_ref.shape[1]
+    full = gw_ref.shape[1] - 2 * LANES
+    wide = pay_refs[0].shape[1]
+    for j, pay_ref in enumerate(pay_refs):
+        x, bq, bv = parts_of(pay_ref, full - wide)
+        rows = slice(j * x.shape[0], (j + 1) * x.shape[0])
+        out_ref[rows, :rank2] = dot(x, a_ref[...], SAME)
+        out_ref[rows, rank2 : 2 * rank2] = dot(x, ax_ref[...], SAME)
+        for i, g_ref in enumerate((gw_ref, gx_ref)):
+            part_q = dot(g_ref[:, :wide], bq, COLS)
+            part_v = dot(g_ref[:, wide:full], bv, COLS)
+            cols = slice((2 + i) * rank2, (3 + i) * rank2)
+            out_ref[rows, cols] = jnp.concatenate([part_q, part_v], axis=1)
+
+
+def products_early(own, near, out2, mid2, a_ref, ax_ref, gw_ref, gx_ref, out_ref, second_ref):
+    second_ref[...] = out2[...] + mid2[...]
+    products((own, near, second_ref), a_ref, ax_ref, gw_ref, gx_ref, out_ref)
+
+
+def products_late(inner, out3, a_ref, ax_ref, gw_ref, gx_ref, out_ref, third_ref):
+    third_ref[...] = inner[...] + out3[...]
+    products((third_ref,), a_ref, ax_ref, gw_ref, gx_ref, out_ref)
+
+
+def split_early(m_ref, r_ref, gw_ref, gx_ref, e0, e1, e2, sl_ref, c_ref, d_ref):
+    count = e0.shape[0]
+    rank2 = e0.shape[1] // 2
+    for j, e in enumerate((e0, e1, e2)):
+        rows = slice(j * count, (j + 1) * count)
+        cols = slice(j * rank2, (j + 1) * rank2)
+        total = m_ref[rows, :] + r_ref[rows, :]
+        e[...] = total[:, : 2 * rank2].astype(BF16)
+        sl_ref[rows, :] = total[:, 2 * rank2 :]
+        c_ref[:, cols] = (weight_of(gw_ref, 2 * j) * total[:, 2 * rank2 : 3 * rank2]).astype(BF16)
+        d_ref[:, cols] = (weight_of(gx_ref, 2 * j + 1) * total[:, 3 * rank2 :]).astype(BF16)
+
+
+def pack_early(e0, e1, e2, c_ref, d_ref, t_ref, q0, q1, q2):
+    rank2 = e0.shape[1] // 2
+    for j, (e, q) in enumerate(((e0, q0), (e1, q1), (e2, q2))):
+        cols = slice(j * rank2, (j + 1) * rank2)
+        t_ref[:, cols] = e[:, rank2:]
+        q[:, :rank2] = c_ref[:, cols]
+        q[:, rank2:] = d_ref[:, cols]
+
+
+def split_late(m_ref, r_ref, gw_ref, gx_ref, sl_ref, near_ref, far_ref):
+    rank2 = near_ref.shape[1] // 2
+    total = m_ref[...] + r_ref[...]
+    sl_ref[...] = total[:, 2 * rank2 :]
+    near_ref[:, :rank2] = total[:, :rank2].astype(BF16)
+    far_ref[:, :rank2] = total[:, rank2 : 2 * rank2].astype(BF16)
+    near_ref[:, rank2:] = (weight_of(gw_ref, 6) * total[:, 2 * rank2 : 3 * rank2]).astype(BF16)
+    far_ref[:, rank2:] = (weight_of(gx_ref, 7) * total[:, 3 * rank2 :]).astype(BF16)
+
+
+def grad_b_part(first, owns, others, gw_ref, gx_ref, wt_ref, p_refs):
+    count = gw_ref.shape[0]
+    rank2 = 2 * p_refs[0].shape[0]
+    rank = rank2 // 2
+    full = p_refs[0].shape[1]
+    wide = full - full // 5
+    for j, (own, other) in enumerate(zip(owns, others)):
+        cols = slice(j * rank2, (j + 1) * rank2)
+        own = weight_of(gw_ref, 2 * (first + j)) * own.astype(F32)
+        other = weight_of(gx_ref, 2 * (first + j) + 1) * other.astype(F32)
+        wt_ref[:count, cols] = own.astype(BF16)
+        wt_ref[count:, cols] = other.astype(BF16)
+    slots = len(p_refs)
+    left = [j * rank2 + i * rank for i in range(2) for j in range(slots)]
+    both = wt_ref[...]
+    both = jnp.concatenate([both[:, c : c + rank] for c in left], axis=1)
+    own, other = both[:count], both[count:]
+    half = slots * rank
+    part_q = dot(own[:, :half], gw_ref[:, :wide], ROWS) + dot(other[:, :half], gx_ref[:, :wide], ROWS)
+    part_v = dot(own[:, half:], gw_ref[:, wide:full], ROWS) + dot(other[:, half:], gx_ref[:, wide:full], ROWS)
+    for j, p_ref in enumerate(p_refs):
+        p_ref[:, :wide] = part_q[j * rank : (j + 1) * rank].astype(p_ref.dtype)
+        p_ref[:, wide:] = part_v[j * rank : (j + 1) * rank].astype(p_ref.dtype)
+
+
+def grad_b_early(e0, e1, e2, t_ref, gw_ref, gx_ref, wt_ref, p0, p1, p2):
+    rank2 = e0.shape[1] // 2
+    owns = [e[:, :rank2] for e in (e0, e1, e2)]
+    others = [t_ref[:, j * rank2 : (j + 1) * rank2] for j in range(3)]
+    grad_b_part(0, owns, others, gw_ref, gx_ref, wt_ref, (p0, p1, p2))
+
+
+def grad_b_late(near_ref, far_ref, gw_ref, gx_ref, wt_ref, p3):
+    rank2 = near_ref.shape[1] // 2
+    grad_b_part(3, (near_ref[:, :rank2],), (far_ref[:, :rank2],), gw_ref, gx_ref, wt_ref, (p3,))
+
+
+def grad_b_near(p0, p1, p2, sum_ref):
+    sum_ref[...] = p0[...] + p1[...].astype(F32) + p2[...].astype(F32)
+
+
+def grad_b_sum(near_ref, p3, q_ref, v_ref):
+    wide = q_ref.shape[2]
+    total = near_ref[...] + p3[...].astype(F32)
+    q_ref[0] = total[:, :wide].astype(BF16)
+    v_ref[0] = total[:, wide:].astype(BF16)
+
+
+def outputs_part(wt_ref, wt3_ref, b0, b1, b2, b3, s_ref, s3_ref, e0, e1, e2, t_ref, near, far, own_ref, sent_ref, rg_ref):
+    count, full = own_ref.shape
+    wide = b0.shape[1]
+    parts = [parts_of(b, full - wide) for b in (b0, b1, b2, b3)]
+    bq = jnp.concatenate([part[1] for part in parts], axis=0)
+    bv = jnp.concatenate([part[2] for part in parts], axis=0)
+    rank = bq.shape[0] // LINE
+    rank2 = 2 * rank
+    both = jnp.concatenate([wt_ref[...], wt3_ref[...]], axis=1)
+    q = jnp.concatenate([both[:, j * rank2 : j * rank2 + rank] for j in range(LINE)], axis=1)
+    v = jnp.concatenate([both[:, j * rank2 + rank : (j + 1) * rank2] for j in range(LINE)], axis=1)
+    out_q = dot(q, bq, SAME)
+    out_v = dot(v, bv, SAME)
+    own_ref[:, :wide] = out_q[:count]
+    own_ref[:, wide:] = out_v[:count]
+    sent_ref[:, :wide] = out_q[count:].astype(BF16)
+    sent_ref[:, wide:full] = out_v[count:].astype(BF16)
+    lane = lax.broadcasted_iota(jnp.int32, (count, LANES), 1)
+    owns = [e[:, :rank2] for e in (e0, e1, e2, near)]
+    others = [t_ref[:, j * rank2 : (j + 1) * rank2] for j in range(3)] + [far[:, :rank2]]
+    for i, hid in enumerate((owns, others)):
+        cols = slice(i * rank2, (i + 1) * rank2)
+        found = jnp.zeros((count, LANES), F32)
+        for j in range(LINE):
+            slope = s_ref[j * count : (j + 1) * count, cols] if j < 3 else s3_ref[:, cols]
+            grad = jnp.sum(slope * hid[j].astype(F32), axis=1, keepdims=True)
+            found = jnp.where(lane == 2 * j + i, jnp.broadcast_to(grad, found.shape), found)
+        if i == 0:
+            rg_ref[...] = found.astype(BF16)
+        else:
+            sent_ref[:, full:] = found.astype(BF16)
+
+
+def outputs_sum(me_ref, own_ref, sent_ref, rg_ref, tr_ref, ra_ref, rc_ref, q_ref, v_ref, mix_ref):
+    full = own_ref.shape[1]
+    wide = q_ref.shape[1]
+    total = own_ref[...] + sent_ref[:, :full].astype(F32)
+    q_ref[...] = total[:, :wide].astype(BF16)
+    v_ref[...] = total[:, wide:].astype(BF16)
+    requests = ra_ref.shape[2]
+    row_grad = rg_ref[...] + sent_ref[:, full:]
+    member = jnp.where(members(tr_ref[...], requests), 1.0, 0.0).astype(BF16)
+    req_grad = dot(row_grad, member, ((0,), (1,)))
+    place = lax.broadcasted_iota(jnp.int32, (LANES, requests), 0)
+    for k in range(4):
+        found = jnp.where(picked(me_ref, ra_ref, rc_ref, k, place), req_grad, 0.0)
+        mix_ref[0, k : k + 1, :] = jnp.sum(found, axis=0, keepdims=True)
+
+
+def pair_plan(
+    tokens,
+    grad_query,
+    grad_value,
+    a_proj,
+    b_query,
+    b_value,
+    token_request,
+    req_adapter,
+    req_count,
+    req_mix,
+):
+    rank = b_query.shape[1]
+    rank2 = 2 * rank
+    wide = grad_query.shape[1]
+    full = wide + grad_value.shape[1]
+    count = tokens.shape[0]
+    me = lax.axis_index("expert").astype(jnp.int32).reshape(1)
+    block = ((count, rank2), BF16)
+    b_block = ((rank, full), BF16)
+    adapters = jnp.swapaxes(req_adapter, 1, 2)
+    pair = ((count, 2 * rank2), BF16)
+    early = ((count, 3 * rank2), BF16)
+
+    own, gw, a_own = call_prepare(
+        me, token_request, adapters, req_count, jnp.swapaxes(req_mix, 1, 2),
+        b_query, b_value, grad_query, grad_value, tokens, a_proj[0],
+    )
+    payload = (own.shape, BF16)
+    near, inner = to_place(own, 2), lax.ppermute(own, "expert", MID)
+    a_other = to_place(a_proj[0], 1)
+    near, inner, a_other, gw = lax.optimization_barrier((near, inner, a_other, gw))
+    out2, mid2 = lax.ppermute(inner, "expert", OUT), lax.ppermute(near, "expert", MID)
+    gx = to_place(gw, 1)
+    out2, mid2, gx = lax.optimization_barrier((out2, mid2, gx))
+    out3 = lax.ppermute(mid2, "expert", OUT)
+
+    m, second = call(
+        products_early, [((3 * count, 4 * rank2), F32), payload], own, near, out2, mid2, a_own, a_other, gw, gx
+    )
+    e0, e1, e2, sl, c, d = call(
+        split_early, [pair] * 3 + [((3 * count, 2 * rank2), F32), early, early], m, other_core(m), gw, gx
+    )
+    e1, e2, d = to_place(e1, 2), to_place(e2, 4), to_place(d, 1)
+    t, q0, q1, q2 = call(pack_early, [early] + [pair] * 3, e0, e1, e2, c, d)
+    (out3,) = after(t, out3)
+    t, q1, q2 = to_place(t, 1), to_place(q1, 2), to_place(q2, 4)
+    m3, third = call(
+        products_late, [((count, 4 * rank2), F32), payload], inner, out3, a_own, a_other, gw, gx
+    )
+    (t,) = after(m3, t)
+    wt, p0, p1, p2 = call(
+        grad_b_early,
+        [((2 * count, 3 * rank2), BF16), ((rank, full), F32), b_block, b_block],
+        e0, e1, e2, t, gw, gx,
+    )
+    (m3,) = after(wt, m3)
+    p1, p2 = to_place(p1, 2), to_place(p2, 4)
+    sl3, z3, z7 = call(
+        split_late, [((count, 2 * rank2), F32), pair, pair], m3, other_core(m3), gw, gx
+    )
+    (q1,) = after(sl3, q1)
+    z3, z7 = to_place(z3, 6), to_place(z7, 7)
+    x1, x2, x3 = near[:count], second[:count], third[:count]
+    grad_a = dot(tokens, q0, ROWS) + dot(x1, q1, ROWS) + dot(x2, q2, ROWS)
+    (z3,) = after(grad_a, z3)
+    wt3, p3 = call(grad_b_late, [((2 * count, rank2), BF16), b_block], z3, z7, gw, gx)
+    p3 = to_place(p3, 6)
+    (wt,) = after(wt3, wt)
+    out_own, sent, rg = call(
+        outputs_part,
+        [((count, full), F32), ((count, full + LANES), BF16), ((count, LANES), BF16)],
+        wt, wt3, own, near, second, third, sl, sl3, e0, e1, e2, t, z3, z7,
+    )
+    sent = to_place(sent, 1)
+    (z7,) = after(out_own, z7)
+    grad_a_other = (grad_a[:, rank2:] + dot(x3, z7[:, rank2:], ROWS)).astype(BF16)
+    grad_a = grad_a[:, :rank2] + dot(x3, z3[:, rank2:], ROWS)
+    (p1,) = after(grad_a, p1)
+    (near_sum,) = call(grad_b_near, [((rank, full), F32)], p0, p1, p2)
+    (sent,) = after(near_sum, sent)
+    out_query, out_value, grad_mix = call_sum(
+        me, out_own, sent, rg, token_request, adapters, req_count, grad_query, grad_value
+    )
+    (p3,) = after(out_query, p3)
+    grad_bq, grad_bv = call(grad_b_sum, [(b_query.shape, BF16), (b_value.shape, BF16)], near_sum, p3)
+    (grad_a,) = after(grad_bq, grad_a)
+    grad_a = grad_a + to_place(grad_a_other, 1).astype(F32)
+    return out_query, out_value, grad_a.astype(BF16)[None], grad_bq, grad_bv, jnp.swapaxes(grad_mix, 1, 2)
+
+
+def after(earlier, *arrays):
+    return lax.optimization_barrier((*arrays, earlier))[:-1]
+
+
+def call_with_me(kernel, outs, *ins):
+    shapes = [jax.ShapeDtypeStruct(shape, dtype) for shape, dtype in outs]
+    return pl.pallas_call(
+        kernel,
+        out_shape=shapes,
+        in_specs=[pl.BlockSpec(memory_space=pltpu.SMEM)] + [pl.BlockSpec(memory_space=pltpu.VMEM)] * (len(ins) - 1),
+        out_specs=[pl.BlockSpec(memory_space=pltpu.VMEM)] * len(outs),
+        compiler_params=pltpu.CompilerParams(vmem_limit_bytes=24 * 1024 * 1024),
+        cost_estimate=COST,
+    )(*ins)
+
+
+def call_prepare(me, *ins):
+    request, adapters, counts, mix, b_query, b_value, grad_query, grad_value, x, a = ins
+    rank, wide = b_query.shape[1:]
+    narrow = b_value.shape[2]
+    step = rank * narrow // wide
+    outs = [
+        (x.shape[0] + rank + step, wide),
+        (grad_query.shape[0], wide + narrow + 2 * LANES),
+        a.shape,
+    ]
+    return pl.pallas_call(
+        prepare,
+        out_shape=[jax.ShapeDtypeStruct(shape, BF16) for shape in outs],
+        in_specs=[pl.BlockSpec(memory_space=pltpu.SMEM)] + [pl.BlockSpec(memory_space=pltpu.HBM)] * len(ins),
+        out_specs=[pl.BlockSpec(memory_space=pltpu.VMEM)] * len(outs),
+        scratch_shapes=[pltpu.VMEM(i.shape, i.dtype) for i in (request, adapters, counts, mix)]
+        + [pltpu.SemaphoreType.DMA((len(ins) - 1 + rank // step,))],
+        compiler_params=pltpu.CompilerParams(vmem_limit_bytes=PREP_VMEM * 1024 * 1024),
+        cost_estimate=COST,
+    )(me, *ins)
+
+
+def call_sum(me, own, sent, rg, token_request, adapters, req_count, grad_query, grad_value):
+    outs = [(grad_query.shape, BF16), (grad_value.shape, BF16), (adapters.shape, F32)]
+    return call_with_me(outputs_sum, outs, me, own, sent, rg, token_request, adapters, req_count)
+
+
 def solution(mesh):
     in_specs = (
         P(("groups", "expert"), "tensor"),
@@ -171,4 +573,5 @@
         P(("groups", "expert"), None, "tensor"),
         P(("groups", "expert"), None, None),
     )
+    shards = pair_plan if mesh.shape["expert"] == LINE * PAIR else row_exchange
     return jax.shard_map(shards, mesh=mesh, in_specs=in_specs, out_specs=out_specs, check_vma=False)

time: 445 us -> 133 us (0.30)
  waiting for transfers between devices: 190 us -> 81.8 us
  blocking collectives: 107 us -> 0 us
  local copies, waits for them, and re-layouts: 53.1 us -> 4.33 us
  other arithmetic: 37 us -> 0.1 us
  between operations: 14.4 us -> 0.89 us
  matrix products: 15.4 us -> 2.14 us
  Pallas kernels: 0 us -> 10.2 us
  starting transfers between devices: 26.7 us -> 33.1 us
    all_to_all x5 -> x0, waiting for transfers between devices: 184 us -> none  [the longest x1 82.4 us: shards(): lax.all_to_all(x_rows, 'expert', split_axis=0, concat_axis=0, tiled=True)]
    all_to_all x2 -> x0, blocking collectives: 107 us -> none  [the longest x1 97.3 us: shards(): lax.all_to_all(query_rows, 'expert', split_axis=0, concat_axis=0, tiled=T...]
    ppermute x0 -> x22, waiting for transfers between devices: none -> 81.8 us  [the longest x16 78.4 us: to_place(): lax.ppermute(array, 'expert', [(i, i ^ place) for i in range(LINE * PAIR)])]
    ppermute x0 -> x22, starting transfers between devices: none -> 33.1 us  [the longest x16 28.9 us: to_place(): lax.ppermute(array, 'expert', [(i, i ^ place) for i in range(LINE * PAIR)])]
    all_to_all x5 -> x0, starting transfers between devices: 26.7 us -> none  [the longest x1 7.25 us: shards(): lax.all_to_all(value_rows, 'expert', split_axis=0, concat_axis=0, tiled=T...]
    scatter-add x2 -> x0, other arithmetic: 23.7 us -> none  [the longest x1 15.8 us: shards(): out_query = jnp.zeros((tok_count, feat_width), jnp.float32).at[flat_idx]....]
    gather x10 -> x0, local copies, waits for them, and re-layouts: 21.2 us -> none  [the longest x2 6.31 us: shards(): tokens[flat_idx]]
    reshape x6 -> x0, local copies, waits for them, and re-layouts: 17.5 us -> none  [the longest x1 5.46 us: shards(): up_query.reshape(slot_count, row_count, feat_width)]
  transfers between devices with their start and end apart: 6 -> 22, of which waited for: 6 -> 12; matrix products, arithmetic and copies ran while one was open for 13% -> 2% of each run, Pallas kernels for 0% -> 3%
where the time goes in v2:
time: 133 us
  waiting for transfers between devices  81.8 us (62%)
  starting transfers between devices  33.1 us (25%)
  Pallas kernels  10.2 us (8%)
  local copies, waits for them, and re-layouts  4.33 us (3%)
  matrix products  2.14 us (2%)
    ppermute x16, waiting for transfers between devices, to_place(): lax.ppermute(array, 'expert', [(i, i ^ place) for i in range(LINE * PAIR)])  78.4 us
    ppermute x16, starting transfers between devices, to_place(): lax.ppermute(array, 'expert', [(i, i ^ place) for i in range(LINE * PAIR)])  28.9 us
    pallas_call x10, Pallas kernels, call(): pl.pallas_call(kernel, out_shape=shapes, in_specs=[pl.BlockSpec(memory_sp...  6.04 us
    unnamed x19, local copies, waits for them, and re-layouts  4.33 us
    pallas_call x1, Pallas kernels, call_prepare(): pl.pallas_call(prepare, out_shape=[jax.ShapeDtypeStruct(shape, BF16) for...  2.97 us
  transfers between devices with their start and end apart: 22, of which 12 were waited for; matrix products, arithmetic and copies ran while one was open for 2% of the time, Pallas kernels for 3%

profile of v2, /device:TPU:0, one launch (start us, length us, event | category | flops | bytes accessed | tf_op | source)
XLA Modules:
  0.0 132.5 jit_solution(985201664092412821)
XLA Ops:
  0.6 3.0 %shard_map.145 = (bf16[208,2048]{1,0:T(8,128)(2,1)}, bf16[128,2816]{1,0:T(8,128)(2,1)}, bf16[2048,128]{1,0:T(8,128)(2,1)}) custom-call(s32[1]{0:T(128)} %bitcast.me_ref, s32[1,128]{1,0:T(1,128)} %tr_ref.1, s32[1,4,32]{2,1,0:T(4,128)} %bitcast.17, s32[1,32]{1,0:T(1,128)} %rc_ref.1, bf16[1,4,32]{2,1,0:T(4,128)(2,1)} %bitcast.21, bf16[1,64,2048]{2,1,0:T(8,128)(2,1)} %bq.1, ...), custom_call_target="tpu_custom_call" | custom-call | tf_op jit(solution)/shard_map/pallas_call | solution.py:538
  4.3 5.9 %collective-permute-start = (bf16[208,2048]{1,0:T(8,128)(2,1)}, bf16[208,2048]{1,0:T(8,128)(2,1)S(1)}, u32[]{:S(2)}, u32[]{:S(2)}) collective-permute-start(bf16[208,2048]{1,0:T(8,128)(2,1)} %get-tuple-element.58.own.b0), channel_id=1, source_target_pairs={{0,4},{2,6},{4,0},{6,2},{8,12},{10,14},{12,8},{14,10},{1,5},{3,7},... | collective-permute-start | bytes 2555912 | tf_op jit(solution)/shard_map/ppermute | solution.py:166
  10.2 1.5 %collective-permute-start.2 = (bf16[2048,128]{1,0:T(8,128)(2,1)}, bf16[2048,128]{1,0:T(8,128)(2,1)S(1)}, u32[]{:S(2)}, u32[]{:S(2)}) collective-permute-start(bf16[2048,128]{1,0:T(8,128)(2,1)} %bitcast.20), channel_id=1, source_target_pairs={{0,2},{2,0},{4,6},{6,4},{8,10},{10,8},{12,14},{14,12},{1,3},{3,1},... | collective-permute-start | bytes 1572872 | tf_op jit(solution)/shard_map/ppermute | solution.py:166
  11.7 11.8 %collective-permute-done.2.ax_ref = bf16[2048,128]{1,0:T(8,128)(2,1)S(1)} collective-permute-done((bf16[2048,128]{1,0:T(8,128)(2,1)}, bf16[2048,128]{1,0:T(8,128)(2,1)S(1)}, u32[]{:S(2)}, u32[]{:S(2)}) %collective-permute-start.2) | collective-permute-done | bytes 524320 | tf_op jit(solution)/shard_map/ppermute | solution.py:166
  23.5 5.6 %collective-permute-done.near.b1 = bf16[208,2048]{1,0:T(8,128)(2,1)S(1)} collective-permute-done((bf16[208,2048]{1,0:T(8,128)(2,1)}, bf16[208,2048]{1,0:T(8,128)(2,1)S(1)}, u32[]{:S(2)}, u32[]{:S(2)}) %collective-permute-start) | collective-permute-done | bytes 852000 | tf_op jit(solution)/shard_map/ppermute | solution.py:166
  29.1 1.3 collective-permute-start.3
  31.1 1.6 %collective-permute-start.5 = (bf16[128,2816]{1,0:T(8,128)(2,1)}, bf16[128,2816]{1,0:T(8,128)(2,1)S(1)}, u32[]{:S(2)}, u32[]{:S(2)}) collective-permute-start(bf16[128,2816]{1,0:T(8,128)(2,1)} %get-tuple-element.62.gw_ref), channel_id=1, source_target_pairs={{0,2},{2,0},{4,6},{6,4},{8,10},{10,8},{12,14},{14,12},{1,3},{3,1},... | collective-permute-start | bytes 2162696 | tf_op jit(solution)/shard_map/ppermute | solution.py:166
  32.6 15.7 %collective-permute-done.5.gx_ref = bf16[128,2816]{1,0:T(8,128)(2,1)S(1)} collective-permute-done((bf16[128,2816]{1,0:T(8,128)(2,1)}, bf16[128,2816]{1,0:T(8,128)(2,1)S(1)}, u32[]{:S(2)}, u32[]{:S(2)}) %collective-permute-start.5) | collective-permute-done | bytes 720928 | tf_op jit(solution)/shard_map/ppermute | solution.py:166
  48.4 2.4 %collective-permute-done.3.out2 = bf16[208,2048]{1,0:T(8,128)(2,1)S(1)} collective-permute-done((bf16[208,2048]{1,0:T(8,128)(2,1)S(1)}, bf16[208,2048]{1,0:T(8,128)(2,1)S(1)}, u32[]{:S(2)}, u32[]{:S(2)}) %collective-permute-start.3) | collective-permute-done | bytes 852000 | tf_op jit(solution)/shard_map/ppermute | solution.py:453
  50.8 1.1 copy-done
  51.9 1.2 copy-done.2
  53.0 1.0 copy-done.4
  54.1 2.0 %shard_map.146 = (f32[384,512]{1,0:T(8,128)S(1)}, bf16[208,2048]{1,0:T(8,128)(2,1)S(1)}) custom-call(bf16[208,2048]{1,0:T(8,128)(2,1)S(1)} %copy-done.2, bf16[208,2048]{1,0:T(8,128)(2,1)S(1)} %collective-permute-done.near.b1, bf16[208,2048]{1,0:T(8,128)(2,1)S(1)} %collective-permute-done.3.out2, bf16[208,2048]{1,0:T(8,128)(2,1)S(1)} %collective-permute-done.4.mid2, ...), custom_call_target="tpu_custom_call" | custom-call | tf_op jit(solution)/shard_map/pallas_call | solution.py:188
  56.2 1.3 collective-permute-start.11
  57.5 1.0 collective-permute-done.6.r_ref
  58.7 1.6 %collective-permute-start.9 = (bf16[128,384]{1,0:T(8,128)(2,1)S(1)}, bf16[128,384]{1,0:T(8,128)(2,1)S(1)}, u32[]{:S(2)}, u32[]{:S(2)}) collective-permute-start(bf16[128,384]{1,0:T(8,128)(2,1)S(1)} %get-tuple-element.73), channel_id=1, source_target_pairs={{0,2},{2,0},{4,6},{6,4},{8,10},{10,8},{12,14},{14,12},{1,3},{3,1},... | collective-permute-start | bytes 294920 | tf_op jit(solution)/shard_map/ppermute | solution.py:166
  60.2 3.7 %collective-permute-start.7 = (bf16[128,256]{1,0:T(8,128)(2,1)S(1)}, bf16[128,256]{1,0:T(8,128)(2,1)S(1)}, u32[]{:S(2)}, u32[]{:S(2)}) collective-permute-start(bf16[128,256]{1,0:T(8,128)(2,1)S(1)} %get-tuple-element.70), channel_id=1, source_target_pairs={{0,4},{2,6},{4,0},{6,2},{8,12},{10,14},{12,8},{14,10},{1,5},{3,7},... | collective-permute-start | bytes 196616 | tf_op jit(solution)/shard_map/ppermute | solution.py:166
  64.0 19.6 %collective-permute-done.7.e1 = bf16[128,256]{1,0:T(8,128)(2,1)S(1)} collective-permute-done((bf16[128,256]{1,0:T(8,128)(2,1)S(1)}, bf16[128,256]{1,0:T(8,128)(2,1)S(1)}, u32[]{:S(2)}, u32[]{:S(2)}) %collective-permute-start.7) | collective-permute-done | bytes 65568 | tf_op jit(solution)/shard_map/ppermute | solution.py:166
  83.7 1.6 %collective-permute-start.10 = (bf16[128,384]{1,0:T(8,128)(2,1)S(1)}, bf16[128,384]{1,0:T(8,128)(2,1)S(1)}, u32[]{:S(2)}, u32[]{:S(2)}) collective-permute-start(bf16[128,384]{1,0:T(8,128)(2,1)S(1)} %get-tuple-element.74), channel_id=1, source_target_pairs={{0,2},{2,0},{4,6},{6,4},{8,10},{10,8},{12,14},{14,12},{1,3},{3,1},... | collective-permute-start | bytes 294920 | tf_op jit(solution)/shard_map/ppermute | solution.py:166
  85.2 1.9 %collective-permute-start.14 = (bf16[128,256]{1,0:T(8,128)(2,1)S(1)}, bf16[128,256]{1,0:T(8,128)(2,1)S(1)}, u32[]{:S(2)}, u32[]{:S(2)}) collective-permute-start(bf16[128,256]{1,0:T(8,128)(2,1)S(1)} %get-tuple-element.82), channel_id=1, source_target_pairs={{0,4},{2,6},{4,0},{6,2},{8,12},{10,14},{12,8},{14,10},{1,5},{3,7},... | collective-permute-start | bytes 196616 | tf_op jit(solution)/shard_map/ppermute | solution.py:166
  88.4 0.9 shard_map.150
  89.4 1.1 collective-permute-done.15
  91.1 2.1 %collective-permute-start.13 = (bf16[128,256]{1,0:T(8,128)(2,1)S(1)}, bf16[128,256]{1,0:T(8,128)(2,1)S(1)}, u32[]{:S(2)}, u32[]{:S(2)}) collective-permute-start(bf16[128,256]{1,0:T(8,128)(2,1)S(1)} %get-tuple-element.80), channel_id=1, source_target_pairs={{0,12},{2,14},{4,8},{6,10},{8,4},{10,6},{12,0},{14,2},{1,13},{3,15... | collective-permute-start | bytes 196616 | tf_op jit(solution)/shard_map/ppermute | solution.py:166
  93.2 2.6 %collective-permute-start.16 = (bf16[128,256]{1,0:T(8,128)(2,1)S(1)}, bf16[128,256]{1,0:T(8,128)(2,1)S(1)}, u32[]{:S(2)}, u32[]{:S(2)}) collective-permute-start(bf16[128,256]{1,0:T(8,128)(2,1)S(1)} %get-tuple-element.88), channel_id=1, source_target_pairs={{0,14},{2,12},{4,10},{6,8},{8,6},{10,4},{12,2},{14,0},{1,15},{3,13... | collective-permute-start | bytes 196616 | tf_op jit(solution)/shard_map/ppermute | solution.py:166
  97.2 2.9 %collective-permute-done.16.far_ref.far = bf16[128,256]{1,0:T(8,128)(2,1)S(1)} collective-permute-done((bf16[128,256]{1,0:T(8,128)(2,1)S(1)}, bf16[128,256]{1,0:T(8,128)(2,1)S(1)}, u32[]{:S(2)}, u32[]{:S(2)}) %collective-permute-start.16) | collective-permute-done | bytes 65568 | tf_op jit(solution)/shard_map/ppermute | solution.py:166
  102.3 1.4 %collective-permute-start.21 = (bf16[2048,128]{0,1:T(8,128)(2,1)S(1)}, bf16[2048,128]{0,1:T(8,128)(2,1)S(1)}, u32[]{:S(2)}, u32[]{:S(2)}) collective-permute-start(bf16[2048,128]{0,1:T(8,128)(2,1)S(1)} %fusion.2), channel_id=1, source_target_pairs={{0,2},{2,0},{4,6},{6,4},{8,10},{10,8},{12,14},{14,12},{1,3},{3,1},... | collective-permute-start | bytes 1572872 | tf_op jit(solution)/shard_map/ppermute | solution.py:166
  103.7 2.4 %collective-permute-start.19 = (bf16[64,2560]{1,0:T(8,128)(2,1)S(1)}, bf16[64,2560]{1,0:T(8,128)(2,1)S(1)}, u32[]{:S(2)}, u32[]{:S(2)}) collective-permute-start(bf16[64,2560]{1,0:T(8,128)(2,1)S(1)} %get-tuple-element.98), channel_id=1, source_target_pairs={{0,8},{2,10},{4,12},{6,14},{8,0},{10,2},{12,4},{14,6},{1,9},{3,11}... | collective-permute-start | bytes 983048 | tf_op jit(solution)/shard_map/ppermute | solution.py:166
  106.1 2.0 %collective-permute-start.20 = (bf16[64,2560]{1,0:T(8,128)(2,1)S(1)}, bf16[64,2560]{1,0:T(8,128)(2,1)S(1)}, u32[]{:S(2)}, u32[]{:S(2)}) collective-permute-start(bf16[64,2560]{1,0:T(8,128)(2,1)S(1)} %get-tuple-element.103), channel_id=1, source_target_pairs={{0,12},{2,14},{4,8},{6,10},{8,4},{10,6},{12,0},{14,2},{1,13},{3,15... | collective-permute-start | bytes 983048 | tf_op jit(solution)/shard_map/ppermute | solution.py:166
  108.5 8.9 %collective-permute-done.18.p1 = bf16[64,2560]{1,0:T(8,128)(2,1)S(1)} collective-permute-done((bf16[64,2560]{1,0:T(8,128)(2,1)S(1)}, bf16[64,2560]{1,0:T(8,128)(2,1)S(1)}, u32[]{:S(2)}, u32[]{:S(2)}) %collective-permute-start.18) | collective-permute-done | bytes 327712 | tf_op jit(solution)/shard_map/ppermute | solution.py:166
  117.4 11.9 %collective-permute-done.19.p2 = bf16[64,2560]{1,0:T(8,128)(2,1)S(1)} collective-permute-done((bf16[64,2560]{1,0:T(8,128)(2,1)S(1)}, bf16[64,2560]{1,0:T(8,128)(2,1)S(1)}, u32[]{:S(2)}, u32[]{:S(2)}) %collective-permute-start.19) | collective-permute-done | bytes 327712 | tf_op jit(solution)/shard_map/ppermute | solution.py:166
  129.4 1.2 shard_map.155
  131.5 1.0 copy.20
  (49 shorter events, 8.5 us)
Async XLA Ops:
  3.6 19.9 %collective-permute-start.1 = (bf16[208,2048]{1,0:T(8,128)(2,1)}, bf16[208,2048]{1,0:T(8,128)(2,1)S(1)}, u32[]{:S(2)}, u32[]{:S(2)}) collective-permute-start(bf16[208,2048]{1,0:T(8,128)(2,1)} %get-tuple-element.58.own.b0), channel_id=1, source_target_pairs={{4,8},{6,10},{8,4},{10,6},{5,9},{7,11},{9,5},{11,7},{20,24},{22,26... | collective-permute-start | bytes 2555912 | tf_op jit(solution)/shard_map/ppermute | solution.py:450
  4.3 24.7 %collective-permute-start = (bf16[208,2048]{1,0:T(8,128)(2,1)}, bf16[208,2048]{1,0:T(8,128)(2,1)S(1)}, u32[]{:S(2)}, u32[]{:S(2)}) collective-permute-start(bf16[208,2048]{1,0:T(8,128)(2,1)} %get-tuple-element.58.own.b0), channel_id=1, source_target_pairs={{0,4},{2,6},{4,0},{6,2},{8,12},{10,14},{12,8},{14,10},{1,5},{3,7},... | collective-permute-start | bytes 2555912 | tf_op jit(solution)/shard_map/ppermute | solution.py:166
  10.2 13.3 %collective-permute-start.2 = (bf16[2048,128]{1,0:T(8,128)(2,1)}, bf16[2048,128]{1,0:T(8,128)(2,1)S(1)}, u32[]{:S(2)}, u32[]{:S(2)}) collective-permute-start(bf16[2048,128]{1,0:T(8,128)(2,1)} %bitcast.20), channel_id=1, source_target_pairs={{0,2},{2,0},{4,6},{6,4},{8,10},{10,8},{12,14},{14,12},{1,3},{3,1},... | collective-permute-start | bytes 1572872 | tf_op jit(solution)/shard_map/ppermute | solution.py:166
  29.1 21.7 %collective-permute-start.3 = (bf16[208,2048]{1,0:T(8,128)(2,1)S(1)}, bf16[208,2048]{1,0:T(8,128)(2,1)S(1)}, u32[]{:S(2)}, u32[]{:S(2)}) collective-permute-start(bf16[208,2048]{1,0:T(8,128)(2,1)S(1)} %collective-permute-done.1.inner), channel_id=1, source_target_pairs={{4,0},{6,2},{8,12},{10,14},{5,1},{7,3},{9,13},{11,15},{20,16},{22,... | collective-permute-start | bytes 2555912 | tf_op jit(solution)/shard_map/ppermute | solution.py:453
  30.4 20.4 %collective-permute-start.4 = (bf16[208,2048]{1,0:T(8,128)(2,1)S(1)}, bf16[208,2048]{1,0:T(8,128)(2,1)S(1)}, u32[]{:S(2)}, u32[]{:S(2)}) collective-permute-start(bf16[208,2048]{1,0:T(8,128)(2,1)S(1)} %collective-permute-done.near.b1), channel_id=1, source_target_pairs={{4,8},{6,10},{8,4},{10,6},{5,9},{7,11},{9,5},{11,7},{20,24},{22,26... | collective-permute-start | bytes 2555912 | tf_op jit(solution)/shard_map/ppermute | solution.py:453
  31.1 17.3 %collective-permute-start.5 = (bf16[128,2816]{1,0:T(8,128)(2,1)}, bf16[128,2816]{1,0:T(8,128)(2,1)S(1)}, u32[]{:S(2)}, u32[]{:S(2)}) collective-permute-start(bf16[128,2816]{1,0:T(8,128)(2,1)} %get-tuple-element.62.gw_ref), channel_id=1, source_target_pairs={{0,2},{2,0},{4,6},{6,4},{8,10},{10,8},{12,14},{14,12},{1,3},{3,1},... | collective-permute-start | bytes 2162696 | tf_op jit(solution)/shard_map/ppermute | solution.py:166
  50.8 1.1 copy-start
  51.9 1.2 copy-start.2
  53.0 1.0 copy-start.4
  54.1 4.4 %copy-start.1 = (bf16[128,2816]{1,0:T(8,128)(2,1)S(1)}, bf16[128,2816]{1,0:T(8,128)(2,1)}, u32[]{:S(2)}) copy-start(bf16[128,2816]{1,0:T(8,128)(2,1)} %get-tuple-element.62.gw_ref) | copy-start | bytes 2162692
  56.1 2.4 %collective-permute-start.6 = (f32[384,512]{1,0:T(8,128)S(1)}, f32[384,512]{1,0:T(8,128)S(1)}, u32[]{:S(2)}, u32[]{:S(2)}) collective-permute-start(f32[384,512]{1,0:T(8,128)S(1)} %get-tuple-element.68.m_ref), channel_id=1, source_target_pairs={{0,1},{1,0},{2,3},{3,2},{4,5},{5,4},{6,7},{7,6},{8,9},{9,8},{10,11... | collective-permute-start | bytes 2359304 | tf_op jit(solution)/shard_map/ppermute | solution.py:170
  56.2 30.9 %collective-permute-start.11 = (bf16[208,2048]{1,0:T(8,128)(2,1)S(1)}, bf16[208,2048]{1,0:T(8,128)(2,1)S(1)}, u32[]{:S(2)}, u32[]{:S(2)}) collective-permute-start(bf16[208,2048]{1,0:T(8,128)(2,1)S(1)} %collective-permute-done.4.mid2), channel_id=1, source_target_pairs={{4,0},{6,2},{8,12},{10,14},{5,1},{7,3},{9,13},{11,15},{20,16},{22,... | collective-permute-start | bytes 2555912 | tf_op jit(solution)/shard_map/ppermute | solution.py:456
  58.7 24.9 %collective-permute-start.9 = (bf16[128,384]{1,0:T(8,128)(2,1)S(1)}, bf16[128,384]{1,0:T(8,128)(2,1)S(1)}, u32[]{:S(2)}, u32[]{:S(2)}) collective-permute-start(bf16[128,384]{1,0:T(8,128)(2,1)S(1)} %get-tuple-element.73), channel_id=1, source_target_pairs={{0,2},{2,0},{4,6},{6,4},{8,10},{10,8},{12,14},{14,12},{1,3},{3,1},... | collective-permute-start | bytes 294920 | tf_op jit(solution)/shard_map/ppermute | solution.py:166
  60.2 23.4 %collective-permute-start.7 = (bf16[128,256]{1,0:T(8,128)(2,1)S(1)}, bf16[128,256]{1,0:T(8,128)(2,1)S(1)}, u32[]{:S(2)}, u32[]{:S(2)}) collective-permute-start(bf16[128,256]{1,0:T(8,128)(2,1)S(1)} %get-tuple-element.70), channel_id=1, source_target_pairs={{0,4},{2,6},{4,0},{6,2},{8,12},{10,14},{12,8},{14,10},{1,5},{3,7},... | collective-permute-start | bytes 196616 | tf_op jit(solution)/shard_map/ppermute | solution.py:166
  64.0 19.7 %collective-permute-start.8 = (bf16[128,256]{1,0:T(8,128)(2,1)S(1)}, bf16[128,256]{1,0:T(8,128)(2,1)S(1)}, u32[]{:S(2)}, u32[]{:S(2)}) collective-permute-start(bf16[128,256]{1,0:T(8,128)(2,1)S(1)} %get-tuple-element.71), channel_id=1, source_target_pairs={{0,8},{2,10},{4,12},{6,14},{8,0},{10,2},{12,4},{14,6},{1,9},{3,11}... | collective-permute-start | bytes 196616 | tf_op jit(solution)/shard_map/ppermute | solution.py:166
  83.7 4.7 %collective-permute-start.10 = (bf16[128,384]{1,0:T(8,128)(2,1)S(1)}, bf16[128,384]{1,0:T(8,128)(2,1)S(1)}, u32[]{:S(2)}, u32[]{:S(2)}) collective-permute-start(bf16[128,384]{1,0:T(8,128)(2,1)S(1)} %get-tuple-element.74), channel_id=1, source_target_pairs={{0,2},{2,0},{4,6},{6,4},{8,10},{10,8},{12,14},{14,12},{1,3},{3,1},... | collective-permute-start | bytes 294920 | tf_op jit(solution)/shard_map/ppermute | solution.py:166
  85.2 5.2 %collective-permute-start.15 = (bf16[128,256]{1,0:T(8,128)(2,1)S(1)}, bf16[128,256]{1,0:T(8,128)(2,1)S(1)}, u32[]{:S(2)}, u32[]{:S(2)}) collective-permute-start(bf16[128,256]{1,0:T(8,128)(2,1)S(1)} %get-tuple-element.86), channel_id=1, source_target_pairs={{0,8},{2,10},{4,12},{6,14},{8,0},{10,2},{12,4},{14,6},{1,9},{3,11}... | collective-permute-start | bytes 196616 | tf_op jit(solution)/shard_map/ppermute | solution.py:166
  85.2 5.9 %collective-permute-start.14 = (bf16[128,256]{1,0:T(8,128)(2,1)S(1)}, bf16[128,256]{1,0:T(8,128)(2,1)S(1)}, u32[]{:S(2)}, u32[]{:S(2)}) collective-permute-start(bf16[128,256]{1,0:T(8,128)(2,1)S(1)} %get-tuple-element.82), channel_id=1, source_target_pairs={{0,4},{2,6},{4,0},{6,2},{8,12},{10,14},{12,8},{14,10},{1,5},{3,7},... | collective-permute-start | bytes 196616 | tf_op jit(solution)/shard_map/ppermute | solution.py:166
  89.3 1.7 %collective-permute-start.12 = (f32[128,512]{1,0:T(8,128)S(1)}, f32[128,512]{1,0:T(8,128)S(1)}, u32[]{:S(2)}, u32[]{:S(2)}) collective-permute-start(f32[128,512]{1,0:T(8,128)S(1)} %get-tuple-element.79.m_ref), channel_id=1, source_target_pairs={{0,1},{1,0},{2,3},{3,2},{4,5},{5,4},{6,7},{7,6},{8,9},{9,8},{10,11... | collective-permute-start | bytes 786440 | tf_op jit(solution)/shard_map/ppermute | solution.py:170
  91.0 5.4 %copy-start.8 = (bf16[128,2048]{1,0:T(8,128)(2,1)S(1)}, bf16[128,2048]{1,0:T(8,128)(2,1)}, u32[]{:S(2)}) copy-start(bf16[128,2048]{1,0:T(8,128)(2,1)} %x.1) | copy-start | bytes 1572868
  91.1 6.1 %collective-permute-start.13 = (bf16[128,256]{1,0:T(8,128)(2,1)S(1)}, bf16[128,256]{1,0:T(8,128)(2,1)S(1)}, u32[]{:S(2)}, u32[]{:S(2)}) collective-permute-start(bf16[128,256]{1,0:T(8,128)(2,1)S(1)} %get-tuple-element.80), channel_id=1, source_target_pairs={{0,12},{2,14},{4,8},{6,10},{8,4},{10,6},{12,0},{14,2},{1,13},{3,15... | collective-permute-start | bytes 196616 | tf_op jit(solution)/shard_map/ppermute | solution.py:166
  93.2 7.0 %collective-permute-start.16 = (bf16[128,256]{1,0:T(8,128)(2,1)S(1)}, bf16[128,256]{1,0:T(8,128)(2,1)S(1)}, u32[]{:S(2)}, u32[]{:S(2)}) collective-permute-start(bf16[128,256]{1,0:T(8,128)(2,1)S(1)} %get-tuple-element.88), channel_id=1, source_target_pairs={{0,14},{2,12},{4,10},{6,8},{8,6},{10,4},{12,2},{14,0},{1,15},{3,13... | collective-permute-start | bytes 196616 | tf_op jit(solution)/shard_map/ppermute | solution.py:166
  96.8 3.8 %copy-start.3 = (bf16[208,2048]{1,0:T(8,128)(2,1)S(1)}, bf16[208,2048]{1,0:T(8,128)(2,1)}, u32[]{:S(2)}) copy-start(bf16[208,2048]{1,0:T(8,128)(2,1)} %get-tuple-element.58.own.b0) | copy-start | bytes 2555908
  101.2 28.2 %collective-permute-start.17 = (bf16[128,2688]{1,0:T(8,128)(2,1)S(1)}, bf16[128,2688]{1,0:T(8,128)(2,1)S(1)}, u32[]{:S(2)}, u32[]{:S(2)}) collective-permute-start(bf16[128,2688]{1,0:T(8,128)(2,1)S(1)} %get-tuple-element.94), channel_id=1, source_target_pairs={{0,2},{2,0},{4,6},{6,4},{8,10},{10,8},{12,14},{14,12},{1,3},{3,1},... | collective-permute-start | bytes 2064392 | tf_op jit(solution)/shard_map/ppermute | solution.py:166
  102.3 29.1 %collective-permute-start.21 = (bf16[2048,128]{0,1:T(8,128)(2,1)S(1)}, bf16[2048,128]{0,1:T(8,128)(2,1)S(1)}, u32[]{:S(2)}, u32[]{:S(2)}) collective-permute-start(bf16[2048,128]{0,1:T(8,128)(2,1)S(1)} %fusion.2), channel_id=1, source_target_pairs={{0,2},{2,0},{4,6},{6,4},{8,10},{10,8},{12,14},{14,12},{1,3},{3,1},... | collective-permute-start | bytes 1572872 | tf_op jit(solution)/shard_map/ppermute | solution.py:166
  103.7 13.7 %collective-permute-start.18 = (bf16[64,2560]{1,0:T(8,128)(2,1)S(1)}, bf16[64,2560]{1,0:T(8,128)(2,1)S(1)}, u32[]{:S(2)}, u32[]{:S(2)}) collective-permute-start(bf16[64,2560]{1,0:T(8,128)(2,1)S(1)} %get-tuple-element.96), channel_id=1, source_target_pairs={{0,4},{2,6},{4,0},{6,2},{8,12},{10,14},{12,8},{14,10},{1,5},{3,7},... | collective-permute-start | bytes 983048 | tf_op jit(solution)/shard_map/ppermute | solution.py:166
  103.7 25.6 %collective-permute-start.19 = (bf16[64,2560]{1,0:T(8,128)(2,1)S(1)}, bf16[64,2560]{1,0:T(8,128)(2,1)S(1)}, u32[]{:S(2)}, u32[]{:S(2)}) collective-permute-start(bf16[64,2560]{1,0:T(8,128)(2,1)S(1)} %get-tuple-element.98), channel_id=1, source_target_pairs={{0,8},{2,10},{4,12},{6,14},{8,0},{10,2},{12,4},{14,6},{1,9},{3,11}... | collective-permute-start | bytes 983048 | tf_op jit(solution)/shard_map/ppermute | solution.py:166
  106.1 23.3 %copy-start.5 = (s32[1,32,4]{1,2,0:T(4,128)S(1)}, s32[1,32,4]{1,2,0:T(4,128)}, u32[]{:S(2)}) copy-start(s32[1,32,4]{1,2,0:T(4,128)} %param.17) | copy-start | bytes 1540
  106.1 23.4 %copy-start.6 = (s32[1,128]{1,0:T(1,128)S(1)}, s32[1,128]{1,0:T(1,128)}, u32[]{:S(2)}) copy-start(s32[1,128]{1,0:T(1,128)} %tr_ref.1) | copy-start | bytes 1540
  106.1 23.4 %copy-start.7 = (s32[1,32]{1,0:T(1,128)S(1)}, s32[1,32]{1,0:T(1,128)}, u32[]{:S(2)}) copy-start(s32[1,32]{1,0:T(1,128)} %rc_ref.1) | copy-start | bytes 388
  106.1 24.6 %collective-permute-start.20 = (bf16[64,2560]{1,0:T(8,128)(2,1)S(1)}, bf16[64,2560]{1,0:T(8,128)(2,1)S(1)}, u32[]{:S(2)}, u32[]{:S(2)}) collective-permute-start(bf16[64,2560]{1,0:T(8,128)(2,1)S(1)} %get-tuple-element.103), channel_id=1, source_target_pairs={{0,12},{2,14},{4,8},{6,10},{8,4},{10,6},{12,0},{14,2},{1,13},{3,15... | collective-permute-start | bytes 983048 | tf_op jit(solution)/shard_map/ppermute | solution.py:166

commit v3 on v2

--- a/solution.py
+++ b/solution.py
@@ -1,3 +1,5 @@
+import functools
+
 import jax
 import jax.numpy as jnp
 from jax import lax
@@ -158,8 +160,11 @@
 OUT = [(2, 0), (3, 1), (4, 6), (5, 7)]
 ROWS, COLS, SAME = ((0,), (0,)), ((1,), (1,)), ((1,), (0,))
 LANES = 128
-PREP_VMEM = 60
-COST = pl.CostEstimate(flops=0, bytes_accessed=0, transcendentals=0)
+PREP_VMEM = 24
+
+
+def cost(us):
+    return pl.CostEstimate(flops=0, bytes_accessed=int(us * 3.0e6), transcendentals=0)
 
 
 def to_place(array, place):
@@ -183,7 +188,7 @@
     return lax.dot_general(a, b, (over, ((), ())), preferred_element_type=F32)
 
 
-def call(kernel, outs, *ins, vmem=24):
+def call(kernel, outs, *ins, vmem=24, us=0):
     shapes = [jax.ShapeDtypeStruct(shape, dtype) for shape, dtype in outs]
     return pl.pallas_call(
         kernel,
@@ -191,7 +196,7 @@
         in_specs=[pl.BlockSpec(memory_space=pltpu.VMEM)] * len(ins),
         out_specs=[pl.BlockSpec(memory_space=pltpu.VMEM)] * len(outs),
         compiler_params=pltpu.CompilerParams(vmem_limit_bytes=vmem * 1024 * 1024),
-        cost_estimate=COST,
+        cost_estimate=cost(us),
     )(*ins)
 
 
@@ -206,8 +211,8 @@
     return found & jnp.broadcast_to(rc_ref[...] > k, place.shape)
 
 
-def prepare(me_ref, tr, ra, rc, rm, bq, bv, gq, gv, x, a, pay_ref, gw_ref, a_ref, tr_ref, ra_ref, rc_ref, rm_ref, sems):
-    count, wide = x.shape
+def prepare(me_ref, tr, ra, rc, rm, bq, bv, gq, gv, x, a, b_ref, gw_ref, x_ref, a_ref, tr_ref, ra_ref, rc_ref, rm_ref, sems):
+    wide = x.shape[1]
     rank, narrow = bv.shape[1:]
     full = wide + narrow
     step = rank * narrow // wide
@@ -216,14 +221,14 @@
         (ra, ra_ref),
         (rc, rc_ref),
         (rm, rm_ref),
-        (x, pay_ref.at[pl.ds(0, count)]),
-        (bq.at[0], pay_ref.at[pl.ds(count, rank)]),
+        (bq.at[0], b_ref.at[pl.ds(0, rank)]),
         (gq, gw_ref.at[:, pl.ds(0, wide)]),
         (gv, gw_ref.at[:, pl.ds(wide, narrow)]),
+        (x, x_ref),
         (a, a_ref),
     ]
     for i in range(rank // step):
-        dst = pay_ref.at[pl.ds(count + rank, step), pl.ds(i * narrow, narrow)]
+        dst = b_ref.at[pl.ds(rank, step), pl.ds(i * narrow, narrow)]
         pairs.append((bv.at[0, pl.ds(i * step, step)], dst))
     copies = [pltpu.make_async_copy(src, dst, sems.at[i]) for i, (src, dst) in enumerate(pairs)]
     for copy in copies:
@@ -252,54 +257,63 @@
     return high + low
 
 
-def parts_of(pay_ref, narrow):
-    rows, wide = pay_ref.shape
+def b_parts(b, narrow):
+    rows, wide = b.shape
     blocks = wide // narrow
-    step = (rows - LANES) // (blocks + 1)
-    rank = blocks * step
-    count = rows - rank - step
-    last = pay_ref[count + rank :, :]
+    step = rows // (blocks + 1)
+    last = b[blocks * step :, :]
     value = jnp.concatenate([last[:, i * narrow : (i + 1) * narrow] for i in range(blocks)], axis=0)
-    return pay_ref[:count, :], pay_ref[count : count + rank, :], value
-
-
-def products(pay_refs, a_ref, ax_ref, gw_ref, gx_ref, out_ref):
+    return b[: blocks * step, :], value
+
+
+def hidden_of(x, rows, a_ref, ax_ref, out_ref):
     rank2 = a_ref.shape[1]
+    out_ref[rows, :rank2] = dot(x, a_ref[...], SAME)
+    out_ref[rows, rank2 : 2 * rank2] = dot(x, ax_ref[...], SAME)
+
+
+def slopes_of(b, rows, first, gw_ref, gx_ref, out_ref):
     full = gw_ref.shape[1] - 2 * LANES
-    wide = pay_refs[0].shape[1]
-    for j, pay_ref in enumerate(pay_refs):
-        x, bq, bv = parts_of(pay_ref, full - wide)
-        rows = slice(j * x.shape[0], (j + 1) * x.shape[0])
-        out_ref[rows, :rank2] = dot(x, a_ref[...], SAME)
-        out_ref[rows, rank2 : 2 * rank2] = dot(x, ax_ref[...], SAME)
-        for i, g_ref in enumerate((gw_ref, gx_ref)):
-            part_q = dot(g_ref[:, :wide], bq, COLS)
-            part_v = dot(g_ref[:, wide:full], bv, COLS)
-            cols = slice((2 + i) * rank2, (3 + i) * rank2)
-            out_ref[rows, cols] = jnp.concatenate([part_q, part_v], axis=1)
-
-
-def products_early(own, near, out2, mid2, a_ref, ax_ref, gw_ref, gx_ref, out_ref, second_ref):
-    second_ref[...] = out2[...] + mid2[...]
-    products((own, near, second_ref), a_ref, ax_ref, gw_ref, gx_ref, out_ref)
-
-
-def products_late(inner, out3, a_ref, ax_ref, gw_ref, gx_ref, out_ref, third_ref):
-    third_ref[...] = inner[...] + out3[...]
-    products((third_ref,), a_ref, ax_ref, gw_ref, gx_ref, out_ref)
-
-
-def split_early(m_ref, r_ref, gw_ref, gx_ref, e0, e1, e2, sl_ref, c_ref, d_ref):
+    wide = b.shape[1]
+    bq, bv = b_parts(b, full - wide)
+    rank2 = 2 * bq.shape[0]
+    for i, g_ref in enumerate((gw_ref, gx_ref)):
+        part_q = dot(g_ref[:, :wide], bq, COLS)
+        part_v = dot(g_ref[:, wide:full], bv, COLS)
+        cols = slice(first + i * rank2, first + (i + 1) * rank2)
+        out_ref[rows, cols] = jnp.concatenate([part_q, part_v], axis=1)
+
+
+def products_early(x0, x1, xo, xm, b0, b1, bo, bm, a_ref, ax_ref, gw_ref, gx_ref, h_ref, s_ref, x2_ref, b2_ref):
+    count = x2_ref.shape[0]
+    x2_ref[...] = xo[...] + xm[...]
+    b2_ref[...] = bo[...] + bm[...]
+    for j, (x, b) in enumerate(((x0, b0), (x1, b1), (x2_ref, b2_ref))):
+        rows = slice(j * count, (j + 1) * count)
+        hidden_of(x[...], rows, a_ref, ax_ref, h_ref)
+        slopes_of(b[...], rows, 0, gw_ref, gx_ref, s_ref)
+
+
+def products_late(xi, xo, bi, bo, a_ref, ax_ref, gw_ref, gx_ref, out_ref, x3_ref, b3_ref):
+    rank2 = a_ref.shape[1]
+    x3_ref[...] = xi[...] + xo[...]
+    b3_ref[...] = bi[...] + bo[...]
+    rows = slice(0, x3_ref.shape[0])
+    hidden_of(x3_ref[...], rows, a_ref, ax_ref, out_ref)
+    slopes_of(b3_ref[...], rows, 2 * rank2, gw_ref, gx_ref, out_ref)
+
+
+def split_early(h_ref, hr_ref, s_ref, sr_ref, gw_ref, gx_ref, e0, e1, e2, sl_ref, c_ref, d_ref):
     count = e0.shape[0]
     rank2 = e0.shape[1] // 2
     for j, e in enumerate((e0, e1, e2)):
         rows = slice(j * count, (j + 1) * count)
         cols = slice(j * rank2, (j + 1) * rank2)
-        total = m_ref[rows, :] + r_ref[rows, :]
-        e[...] = total[:, : 2 * rank2].astype(BF16)
-        sl_ref[rows, :] = total[:, 2 * rank2 :]
-        c_ref[:, cols] = (weight_of(gw_ref, 2 * j) * total[:, 2 * rank2 : 3 * rank2]).astype(BF16)
-        d_ref[:, cols] = (weight_of(gx_ref, 2 * j + 1) * total[:, 3 * rank2 :]).astype(BF16)
+        e[...] = (h_ref[rows, :] + hr_ref[rows, :]).astype(BF16)
+        total = s_ref[rows, :] + sr_ref[rows, :]
+        sl_ref[rows, :] = total
+        c_ref[:, cols] = (weight_of(gw_ref, 2 * j) * total[:, :rank2]).astype(BF16)
+        d_ref[:, cols] = (weight_of(gx_ref, 2 * j + 1) * total[:, rank2:]).astype(BF16)
 
 
 def pack_early(e0, e1, e2, c_ref, d_ref, t_ref, q0, q1, q2):
@@ -321,12 +335,11 @@
     far_ref[:, rank2:] = (weight_of(gx_ref, 7) * total[:, 3 * rank2 :]).astype(BF16)
 
 
-def grad_b_part(first, owns, others, gw_ref, gx_ref, wt_ref, p_refs):
+def grad_b_part(wide, first, owns, others, gw_ref, gx_ref, wt_ref, p_refs):
     count = gw_ref.shape[0]
     rank2 = 2 * p_refs[0].shape[0]
     rank = rank2 // 2
     full = p_refs[0].shape[1]
-    wide = full - full // 5
     for j, (own, other) in enumerate(zip(owns, others)):
         cols = slice(j * rank2, (j + 1) * rank2)
         own = weight_of(gw_ref, 2 * (first + j)) * own.astype(F32)
@@ -346,16 +359,16 @@
         p_ref[:, wide:] = part_v[j * rank : (j + 1) * rank].astype(p_ref.dtype)
 
 
-def grad_b_early(e0, e1, e2, t_ref, gw_ref, gx_ref, wt_ref, p0, p1, p2):
+def grad_b_early(wide, e0, e1, e2, t_ref, gw_ref, gx_ref, wt_ref, p0, p1, p2):
     rank2 = e0.shape[1] // 2
     owns = [e[:, :rank2] for e in (e0, e1, e2)]
     others = [t_ref[:, j * rank2 : (j + 1) * rank2] for j in range(3)]
-    grad_b_part(0, owns, others, gw_ref, gx_ref, wt_ref, (p0, p1, p2))
-
-
-def grad_b_late(near_ref, far_ref, gw_ref, gx_ref, wt_ref, p3):
+    grad_b_part(wide, 0, owns, others, gw_ref, gx_ref, wt_ref, (p0, p1, p2))
+
+
+def grad_b_late(wide, near_ref, far_ref, gw_ref, gx_ref, wt_ref, p3):
     rank2 = near_ref.shape[1] // 2
-    grad_b_part(3, (near_ref[:, :rank2],), (far_ref[:, :rank2],), gw_ref, gx_ref, wt_ref, (p3,))
+    grad_b_part(wide, 3, (near_ref[:, :rank2],), (far_ref[:, :rank2],), gw_ref, gx_ref, wt_ref, (p3,))
 
 
 def grad_b_near(p0, p1, p2, sum_ref):
@@ -372,9 +385,9 @@
 def outputs_part(wt_ref, wt3_ref, b0, b1, b2, b3, s_ref, s3_ref, e0, e1, e2, t_ref, near, far, own_ref, sent_ref, rg_ref):
     count, full = own_ref.shape
     wide = b0.shape[1]
-    parts = [parts_of(b, full - wide) for b in (b0, b1, b2, b3)]
-    bq = jnp.concatenate([part[1] for part in parts], axis=0)
-    bv = jnp.concatenate([part[2] for part in parts], axis=0)
+    parts = [b_parts(b[...], full - wide) for b in (b0, b1, b2, b3)]
+    bq = jnp.concatenate([part[0] for part in parts], axis=0)
+    bv = jnp.concatenate([part[1] for part in parts], axis=0)
     rank = bq.shape[0] // LINE
     rank2 = 2 * rank
     both = jnp.concatenate([wt_ref[...], wt3_ref[...]], axis=1)
@@ -438,64 +451,74 @@
     me = lax.axis_index("expert").astype(jnp.int32).reshape(1)
     block = ((count, rank2), BF16)
     b_block = ((rank, full), BF16)
+    x_block = (tokens.shape, BF16)
     adapters = jnp.swapaxes(req_adapter, 1, 2)
     pair = ((count, 2 * rank2), BF16)
     early = ((count, 3 * rank2), BF16)
 
-    own, gw, a_own = call_prepare(
+    x1, xi = to_place(tokens, 2), lax.ppermute(tokens, "expert", MID)
+    a_other = to_place(a_proj[0], 1)
+    b0, gw, x0, a_own = call_prepare(
         me, token_request, adapters, req_count, jnp.swapaxes(req_mix, 1, 2),
         b_query, b_value, grad_query, grad_value, tokens, a_proj[0],
     )
-    payload = (own.shape, BF16)
-    near, inner = to_place(own, 2), lax.ppermute(own, "expert", MID)
-    a_other = to_place(a_proj[0], 1)
-    near, inner, a_other, gw = lax.optimization_barrier((near, inner, a_other, gw))
-    out2, mid2 = lax.ppermute(inner, "expert", OUT), lax.ppermute(near, "expert", MID)
+    b1, bi = to_place(b0, 2), lax.ppermute(b0, "expert", MID)
+    x1, xi, a_other = lax.optimization_barrier((x1, xi, a_other))
+    xo, xm = lax.ppermute(xi, "expert", OUT), lax.ppermute(x1, "expert", MID)
+    bo, bm = lax.ppermute(bi, "expert", OUT), lax.ppermute(b1, "expert", MID)
     gx = to_place(gw, 1)
-    out2, mid2, gx = lax.optimization_barrier((out2, mid2, gx))
-    out3 = lax.ppermute(mid2, "expert", OUT)
-
-    m, second = call(
-        products_early, [((3 * count, 4 * rank2), F32), payload], own, near, out2, mid2, a_own, a_other, gw, gx
+    xo3 = lax.ppermute(xm, "expert", OUT)
+    bo3 = lax.ppermute(bm, "expert", OUT)
+
+    wide_block = (b0.shape, BF16)
+    m, ms, x2, b2 = call(
+        products_early,
+        [((3 * count, 2 * rank2), F32), ((3 * count, 2 * rank2), F32), x_block, wide_block],
+        x0, x1, xo, xm, b0, b1, bo, bm, a_own, a_other, gw, gx,
     )
     e0, e1, e2, sl, c, d = call(
-        split_early, [pair] * 3 + [((3 * count, 2 * rank2), F32), early, early], m, other_core(m), gw, gx
+        split_early,
+        [pair] * 3 + [((3 * count, 2 * rank2), F32), early, early],
+        m, other_core(m), ms, other_core(ms), gw, gx,
     )
     e1, e2, d = to_place(e1, 2), to_place(e2, 4), to_place(d, 1)
+    (xo3,) = after(e0, xo3)
+    m3, x3, b3 = call(
+        products_late,
+        [((count, 4 * rank2), F32), x_block, wide_block],
+        xi, xo3, bi, bo3, a_own, a_other, gw, gx,
+    )
+    (c,) = after(m3, c)
     t, q0, q1, q2 = call(pack_early, [early] + [pair] * 3, e0, e1, e2, c, d)
-    (out3,) = after(t, out3)
     t, q1, q2 = to_place(t, 1), to_place(q1, 2), to_place(q2, 4)
-    m3, third = call(
-        products_late, [((count, 4 * rank2), F32), payload], inner, out3, a_own, a_other, gw, gx
-    )
-    (t,) = after(m3, t)
+    m3 = after(q0, m3)[0]
+    sl3, z3, z7 = call(
+        split_late, [((count, 2 * rank2), F32), pair, pair], m3, other_core(m3), gw, gx
+    )
+    z3, z7 = to_place(z3, 6), to_place(z7, 7)
+    (t,) = after(sl3, t)
     wt, p0, p1, p2 = call(
-        grad_b_early,
+        functools.partial(grad_b_early, wide),
         [((2 * count, 3 * rank2), BF16), ((rank, full), F32), b_block, b_block],
         e0, e1, e2, t, gw, gx,
     )
-    (m3,) = after(wt, m3)
+    (q1,) = after(wt, q1)
     p1, p2 = to_place(p1, 2), to_place(p2, 4)
-    sl3, z3, z7 = call(
-        split_late, [((count, 2 * rank2), F32), pair, pair], m3, other_core(m3), gw, gx
-    )
-    (q1,) = after(sl3, q1)
-    z3, z7 = to_place(z3, 6), to_place(z7, 7)
-    x1, x2, x3 = near[:count], second[:count], third[:count]
-    grad_a = dot(tokens, q0, ROWS) + dot(x1, q1, ROWS) + dot(x2, q2, ROWS)
+    x1s, x2s, x3s = x1, x2, x3
+    grad_a = dot(x0, q0, ROWS) + dot(x1s, q1, ROWS) + dot(x2s, q2, ROWS)
     (z3,) = after(grad_a, z3)
-    wt3, p3 = call(grad_b_late, [((2 * count, rank2), BF16), b_block], z3, z7, gw, gx)
+    wt3, p3 = call(functools.partial(grad_b_late, wide), [((2 * count, rank2), BF16), b_block], z3, z7, gw, gx)
     p3 = to_place(p3, 6)
     (wt,) = after(wt3, wt)
     out_own, sent, rg = call(
         outputs_part,
         [((count, full), F32), ((count, full + LANES), BF16), ((count, LANES), BF16)],
-        wt, wt3, own, near, second, third, sl, sl3, e0, e1, e2, t, z3, z7,
+        wt, wt3, b0, b1, b2, b3, sl, sl3, e0, e1, e2, t, z3, z7,
     )
     sent = to_place(sent, 1)
     (z7,) = after(out_own, z7)
-    grad_a_other = (grad_a[:, rank2:] + dot(x3, z7[:, rank2:], ROWS)).astype(BF16)
-    grad_a = grad_a[:, :rank2] + dot(x3, z3[:, rank2:], ROWS)
+    grad_a_other = (grad_a[:, rank2:] + dot(x3s, z7[:, rank2:], ROWS)).astype(BF16)
+    grad_a = grad_a[:, :rank2] + dot(x3s, z3[:, rank2:], ROWS)
     (p1,) = after(grad_a, p1)
     (near_sum,) = call(grad_b_near, [((rank, full), F32)], p0, p1, p2)
     (sent,) = after(near_sum, sent)
@@ -513,7 +536,7 @@
     return lax.optimization_barrier((*arrays, earlier))[:-1]
 
 
-def call_with_me(kernel, outs, *ins):
+def call_with_me(kernel, outs, *ins, us=0):
     shapes = [jax.ShapeDtypeStruct(shape, dtype) for shape, dtype in outs]
     return pl.pallas_call(
         kernel,
@@ -521,7 +544,7 @@
         in_specs=[pl.BlockSpec(memory_space=pltpu.SMEM)] + [pl.BlockSpec(memory_space=pltpu.VMEM)] * (len(ins) - 1),
         out_specs=[pl.BlockSpec(memory_space=pltpu.VMEM)] * len(outs),
         compiler_params=pltpu.CompilerParams(vmem_limit_bytes=24 * 1024 * 1024),
-        cost_estimate=COST,
+        cost_estimate=cost(us),
     )(*ins)
 
 
@@ -531,8 +554,9 @@
     narrow = b_value.shape[2]
     step = rank * narrow // wide
     outs = [
-        (x.shape[0] + rank + step, wide),
+        (rank + step, wide),
         (grad_query.shape[0], wide + narrow + 2 * LANES),
+        x.shape,
         a.shape,
     ]
     return pl.pallas_call(
@@ -543,13 +567,13 @@
         scratch_shapes=[pltpu.VMEM(i.shape, i.dtype) for i in (request, adapters, counts, mix)]
         + [pltpu.SemaphoreType.DMA((len(ins) - 1 + rank // step,))],
         compiler_params=pltpu.CompilerParams(vmem_limit_bytes=PREP_VMEM * 1024 * 1024),
-        cost_estimate=COST,
+        cost_estimate=cost(0),
     )(me, *ins)
 
 
 def call_sum(me, own, sent, rg, token_request, adapters, req_count, grad_query, grad_value):
     outs = [(grad_query.shape, BF16), (grad_value.shape, BF16), (adapters.shape, F32)]
-    return call_with_me(outputs_sum, outs, me, own, sent, rg, token_request, adapters, req_count)
+    return call_with_me(outputs_sum, outs, me, own, sent, rg, token_request, adapters, req_count, us=0)
 
 
 def solution(mesh):

time: 133 us -> 116 us (0.87)
  waiting for transfers between devices: 81.8 us -> 56.4 us
  starting transfers between devices: 33.1 us -> 38.5 us
  local copies, waits for them, and re-layouts: 4.33 us -> 8.5 us
  Pallas kernels: 10.2 us -> 7.74 us
    ppermute x16 -> x17, waiting for transfers between devices: 78.4 us -> 30.6 us  [to_place(): lax.ppermute(array, 'expert', [(i, i ^ place) for i in range(LINE * PAIR)])]
    ppermute x4 -> x8, waiting for transfers between devices: 2.41 us -> 25.3 us  [the longest x2 16.3 us: pair_plan(): bo, bm = (lax.ppermute(bi, 'expert', OUT), lax.ppermute(b1, 'expert', MID))]
    unnamed x19 -> x26, local copies, waits for them, and re-layouts: 4.33 us -> 8.5 us
    ppermute x4 -> x8, starting transfers between devices: 4 us -> 7.86 us  [the longest x2 1.98 us: pair_plan(): xo, xm = (lax.ppermute(xi, 'expert', OUT), lax.ppermute(x1, 'expert', MID))]
    pallas_call x1, Pallas kernels: 2.97 us -> 0.52 us  [call_prepare(): pl.pallas_call(prepare, out_shape=[jax.ShapeDtypeStruct(shape, BF16) for...]
    ppermute x16 -> x17, starting transfers between devices: 28.9 us -> 30.1 us  [to_place(): lax.ppermute(array, 'expert', [(i, i ^ place) for i in range(LINE * PAIR)])]
  transfers between devices with their start and end apart: 22 -> 28, of which waited for: 12 -> 11; matrix products, arithmetic and copies ran while one was open for 2% -> 2% of each run, Pallas kernels for 3% -> 6%
where the time goes in v3:
time: 116 us; the launch traced here: 115 us
  waiting for transfers between devices  56.4 us (49%)
  starting transfers between devices  38.5 us (33%)
  local copies, waits for them, and re-layouts  8.5 us (7%)
  Pallas kernels  7.74 us (7%)
  matrix products  2.11 us (2%)
    ppermute x17, waiting for transfers between devices, to_place(): lax.ppermute(array, 'expert', [(i, i ^ place) for i in range(LINE * PAIR)])  30.6 us
    ppermute x17, starting transfers between devices, to_place(): lax.ppermute(array, 'expert', [(i, i ^ place) for i in range(LINE * PAIR)])  30.1 us
    ppermute x2, waiting for transfers between devices, pair_plan(): bo, bm = (lax.ppermute(bi, 'expert', OUT), lax.ppermute(b1, 'expert', MID))  16.3 us
    unnamed x26, local copies, waits for them, and re-layouts  8.5 us
    ppermute x1, waiting for transfers between devices, pair_plan(): bo3 = lax.ppermute(bm, 'expert', OUT)  7.48 us
    pallas_call x10, Pallas kernels, call(): pl.pallas_call(kernel, out_shape=shapes, in_specs=[pl.BlockSpec(memory_sp...  6.01 us
  transfers between devices with their start and end apart: 28, of which 11 were waited for; matrix products, arithmetic and copies ran while one was open for 2% of the time, Pallas kernels for 6%

profile of v3, /device:TPU:0, one launch (start us, length us, event | category | flops | bytes accessed | tf_op | source)
XLA Modules:
  0.0 115.1 jit_solution(2094082542083317096)
XLA Ops:
  0.6 3.0 %collective-permute-start.2 = (bf16[2048,128]{1,0:T(8,128)(2,1)}, bf16[2048,128]{1,0:T(8,128)(2,1)S(1)}, u32[]{:S(2)}, u32[]{:S(2)}) collective-permute-start(bf16[2048,128]{1,0:T(8,128)(2,1)} %bitcast.15), channel_id=1, source_target_pairs={{0,2},{2,0},{4,6},{6,4},{8,10},{10,8},{12,14},{14,12},{1,3},{3,1},... | collective-permute-start | bytes 1572872 | tf_op jit(solution)/shard_map/ppermute | solution.py:171
  4.3 4.4 %collective-permute-start = (bf16[128,2048]{1,0:T(8,128)(2,1)}, bf16[128,2048]{1,0:T(8,128)(2,1)S(1)}, u32[]{:S(2)}, u32[]{:S(2)}) collective-permute-start(bf16[128,2048]{1,0:T(8,128)(2,1)} %x.1), channel_id=1, source_target_pairs={{0,4},{2,6},{4,0},{6,2},{8,12},{10,14},{12,8},{14,10},{1,5},{3,7},... | collective-permute-start | bytes 1572872 | tf_op jit(solution)/shard_map/ppermute | solution.py:171
  8.8 1.0 copy-done
  9.8 1.0 copy-done.1
  10.8 1.0 copy-done.2
  11.9 0.9 copy-done.3
  19.1 1.8 %collective-permute-start.5 = (bf16[80,2048]{1,0:T(8,128)(2,1)S(1)}, bf16[80,2048]{1,0:T(8,128)(2,1)S(1)}, u32[]{:S(2)}, u32[]{:S(2)}) collective-permute-start(bf16[80,2048]{1,0:T(8,128)(2,1)S(1)} %get-tuple-element.62.b0), channel_id=1, source_target_pairs={{0,4},{2,6},{4,0},{6,2},{8,12},{10,14},{12,8},{14,10},{1,5},{3,7},... | collective-permute-start | bytes 983048 | tf_op jit(solution)/shard_map/ppermute | solution.py:171
  21.5 1.3 %collective-permute-start.3 = (bf16[128,2048]{1,0:T(8,128)(2,1)S(1)}, bf16[128,2048]{1,0:T(8,128)(2,1)S(1)}, u32[]{:S(2)}, u32[]{:S(2)}) collective-permute-start(bf16[128,2048]{1,0:T(8,128)(2,1)S(1)} %collective-permute-done.1.xi), channel_id=1, source_target_pairs={{4,0},{6,2},{8,12},{10,14},{5,1},{7,3},{9,13},{11,15},{20,16},{22,... | collective-permute-start | bytes 1572872 | tf_op jit(solution)/shard_map/ppermute | solution.py:467
  22.8 1.3 %collective-permute-start.7 = (bf16[80,2048]{1,0:T(8,128)(2,1)S(1)}, bf16[80,2048]{1,0:T(8,128)(2,1)S(1)}, u32[]{:S(2)}, u32[]{:S(2)}) collective-permute-start(bf16[80,2048]{1,0:T(8,128)(2,1)S(1)} %collective-permute-done.6.bi), channel_id=1, source_target_pairs={{4,0},{6,2},{8,12},{10,14},{5,1},{7,3},{9,13},{11,15},{20,16},{22,... | collective-permute-start | bytes 983048 | tf_op jit(solution)/shard_map/ppermute | solution.py:468
  24.1 5.6 %collective-permute-done.5.b1 = bf16[80,2048]{1,0:T(8,128)(2,1)S(1)} collective-permute-done((bf16[80,2048]{1,0:T(8,128)(2,1)S(1)}, bf16[80,2048]{1,0:T(8,128)(2,1)S(1)}, u32[]{:S(2)}, u32[]{:S(2)}) %collective-permute-start.5) | collective-permute-done | bytes 327712 | tf_op jit(solution)/shard_map/ppermute | solution.py:171
  30.5 1.3 %collective-permute-start.14 = (bf16[128,2048]{1,0:T(8,128)(2,1)S(1)}, bf16[128,2048]{1,0:T(8,128)(2,1)S(1)}, u32[]{:S(2)}, u32[]{:S(2)}) collective-permute-start(bf16[128,2048]{1,0:T(8,128)(2,1)S(1)} %collective-permute-done.4.xm), channel_id=1, source_target_pairs={{4,0},{6,2},{8,12},{10,14},{5,1},{7,3},{9,13},{11,15},{20,16},{22,... | collective-permute-start | bytes 1572872 | tf_op jit(solution)/shard_map/ppermute | solution.py:470
  31.8 16.3 %collective-permute-done.7.bo = bf16[80,2048]{1,0:T(8,128)(2,1)S(1)} collective-permute-done((bf16[80,2048]{1,0:T(8,128)(2,1)S(1)}, bf16[80,2048]{1,0:T(8,128)(2,1)S(1)}, u32[]{:S(2)}, u32[]{:S(2)}) %collective-permute-start.7) | collective-permute-done | bytes 327712 | tf_op jit(solution)/shard_map/ppermute | solution.py:468
  48.1 2.0 %shard_map.146 = (f32[384,256]{1,0:T(8,128)S(1)}, f32[384,256]{1,0:T(8,128)S(1)}, bf16[128,2048]{1,0:T(8,128)(2,1)S(1)}, bf16[80,2048]{1,0:T(8,128)(2,1)S(1)}) custom-call(bf16[128,2048]{1,0:T(8,128)(2,1)S(1)} %get-tuple-element.59.x0, bf16[128,2048]{1,0:T(8,128)(2,1)S(1)} %collective-permute-done.x1, bf16[128,2048]{1,0:T(8,128)(2,1)S(1)} %collective-permute-done.3.xo, ...), custom_call_target="tpu_custom_call" | custom-call | tf_op jit(solution)/shard_map/pallas_call | solution.py:193
  50.7 1.3 %collective-permute-start.15 = (bf16[80,2048]{1,0:T(8,128)(2,1)S(1)}, bf16[80,2048]{1,0:T(8,128)(2,1)S(1)}, u32[]{:S(2)}, u32[]{:S(2)}) collective-permute-start(bf16[80,2048]{1,0:T(8,128)(2,1)S(1)} %collective-permute-done.8.bm), channel_id=1, source_target_pairs={{4,0},{6,2},{8,12},{10,14},{5,1},{7,3},{9,13},{11,15},{20,16},{22,... | collective-permute-start | bytes 983048 | tf_op jit(solution)/shard_map/ppermute | solution.py:471
  52.6 1.6 %collective-permute-start.16 = (bf16[128,384]{1,0:T(8,128)(2,1)S(1)}, bf16[128,384]{1,0:T(8,128)(2,1)S(1)}, u32[]{:S(2)}, u32[]{:S(2)}) collective-permute-start(bf16[128,384]{1,0:T(8,128)(2,1)S(1)} %get-tuple-element.75), channel_id=1, source_target_pairs={{0,2},{2,0},{4,6},{6,4},{8,10},{10,8},{12,14},{14,12},{1,3},{3,1},... | collective-permute-start | bytes 294920 | tf_op jit(solution)/shard_map/ppermute | solution.py:171
  54.2 2.2 %collective-permute-start.12 = (bf16[128,256]{1,0:T(8,128)(2,1)S(1)}, bf16[128,256]{1,0:T(8,128)(2,1)S(1)}, u32[]{:S(2)}, u32[]{:S(2)}) collective-permute-start(bf16[128,256]{1,0:T(8,128)(2,1)S(1)} %get-tuple-element.69), channel_id=1, source_target_pairs={{0,4},{2,6},{4,0},{6,2},{8,12},{10,14},{12,8},{14,10},{1,5},{3,7},... | collective-permute-start | bytes 196616 | tf_op jit(solution)/shard_map/ppermute | solution.py:171
  57.1 1.5 %collective-permute-done.14.xo = bf16[128,2048]{1,0:T(8,128)(2,1)S(1)} collective-permute-done((bf16[128,2048]{1,0:T(8,128)(2,1)S(1)}, bf16[128,2048]{1,0:T(8,128)(2,1)S(1)}, u32[]{:S(2)}, u32[]{:S(2)}) %collective-permute-start.14) | collective-permute-done | bytes 524320 | tf_op jit(solution)/shard_map/ppermute | solution.py:470
  58.6 7.5 %collective-permute-done.15.bo = bf16[80,2048]{1,0:T(8,128)(2,1)S(1)} collective-permute-done((bf16[80,2048]{1,0:T(8,128)(2,1)S(1)}, bf16[80,2048]{1,0:T(8,128)(2,1)S(1)}, u32[]{:S(2)}, u32[]{:S(2)}) %collective-permute-start.15) | collective-permute-done | bytes 327712 | tf_op jit(solution)/shard_map/ppermute | solution.py:471
  67.6 2.5 %collective-permute-start.20 = (bf16[128,256]{1,0:T(8,128)(2,1)S(1)}, bf16[128,256]{1,0:T(8,128)(2,1)S(1)}, u32[]{:S(2)}, u32[]{:S(2)}) collective-permute-start(bf16[128,256]{1,0:T(8,128)(2,1)S(1)} %get-tuple-element.83), channel_id=1, source_target_pairs={{0,4},{2,6},{4,0},{6,2},{8,12},{10,14},{12,8},{14,10},{1,5},{3,7},... | collective-permute-start | bytes 196616 | tf_op jit(solution)/shard_map/ppermute | solution.py:171
  70.1 1.5 %collective-permute-start.17 = (bf16[128,384]{1,0:T(8,128)(2,1)S(1)}, bf16[128,384]{1,0:T(8,128)(2,1)S(1)}, u32[]{:S(2)}, u32[]{:S(2)}) collective-permute-start(bf16[128,384]{1,0:T(8,128)(2,1)S(1)} %get-tuple-element.76), channel_id=1, source_target_pairs={{0,2},{2,0},{4,6},{6,4},{8,10},{10,8},{12,14},{14,12},{1,3},{3,1},... | collective-permute-start | bytes 294920 | tf_op jit(solution)/shard_map/ppermute | solution.py:171
  71.6 1.0 collective-permute-done.21
  73.2 1.5 %collective-permute-done.17.t_ref = bf16[128,384]{1,0:T(8,128)(2,1)S(1)} collective-permute-done((bf16[128,384]{1,0:T(8,128)(2,1)S(1)}, bf16[128,384]{1,0:T(8,128)(2,1)S(1)}, u32[]{:S(2)}, u32[]{:S(2)}) %collective-permute-start.17) | collective-permute-done | bytes 98336 | tf_op jit(solution)/shard_map/ppermute | solution.py:171
  74.7 1.4 %collective-permute-start.19 = (bf16[128,256]{1,0:T(8,128)(2,1)S(1)}, bf16[128,256]{1,0:T(8,128)(2,1)S(1)}, u32[]{:S(2)}, u32[]{:S(2)}) collective-permute-start(bf16[128,256]{1,0:T(8,128)(2,1)S(1)} %get-tuple-element.82), channel_id=1, source_target_pairs={{0,12},{2,14},{4,8},{6,10},{8,4},{10,6},{12,0},{14,2},{1,13},{3,15... | collective-permute-start | bytes 196616 | tf_op jit(solution)/shard_map/ppermute | solution.py:171
  76.1 3.4 %collective-permute-start.22 = (bf16[128,256]{1,0:T(8,128)(2,1)S(1)}, bf16[128,256]{1,0:T(8,128)(2,1)S(1)}, u32[]{:S(2)}, u32[]{:S(2)}) collective-permute-start(bf16[128,256]{1,0:T(8,128)(2,1)S(1)} %get-tuple-element.88), channel_id=1, source_target_pairs={{0,14},{2,12},{4,10},{6,8},{8,6},{10,4},{12,2},{14,0},{1,15},{3,13... | collective-permute-start | bytes 196616 | tf_op jit(solution)/shard_map/ppermute | solution.py:171
  79.4 0.9 shard_map.151
  81.4 1.6 %collective-permute-done.22.far_ref.far = bf16[128,256]{1,0:T(8,128)(2,1)S(1)} collective-permute-done((bf16[128,256]{1,0:T(8,128)(2,1)S(1)}, bf16[128,256]{1,0:T(8,128)(2,1)S(1)}, u32[]{:S(2)}, u32[]{:S(2)}) %collective-permute-start.22) | collective-permute-done | bytes 65568 | tf_op jit(solution)/shard_map/ppermute | solution.py:171
  84.1 1.6 %collective-permute-start.23 = (bf16[128,2688]{1,0:T(8,128)(2,1)S(1)}, bf16[128,2688]{1,0:T(8,128)(2,1)S(1)}, u32[]{:S(2)}, u32[]{:S(2)}) collective-permute-start(bf16[128,2688]{1,0:T(8,128)(2,1)S(1)} %get-tuple-element.95), channel_id=1, source_target_pairs={{0,2},{2,0},{4,6},{6,4},{8,10},{10,8},{12,14},{14,12},{1,3},{3,1},... | collective-permute-start | bytes 2064392 | tf_op jit(solution)/shard_map/ppermute | solution.py:171
  86.6 3.0 %collective-permute-start.25 = (bf16[64,2560]{1,0:T(8,128)(2,1)S(1)}, bf16[64,2560]{1,0:T(8,128)(2,1)S(1)}, u32[]{:S(2)}, u32[]{:S(2)}) collective-permute-start(bf16[64,2560]{1,0:T(8,128)(2,1)S(1)} %get-tuple-element.100), channel_id=1, source_target_pairs={{0,8},{2,10},{4,12},{6,14},{8,0},{10,2},{12,4},{14,6},{1,9},{3,11}... | collective-permute-start | bytes 983048 | tf_op jit(solution)/shard_map/ppermute | solution.py:171
  89.6 1.4 %collective-permute-start.26 = (bf16[64,2560]{1,0:T(8,128)(2,1)S(1)}, bf16[64,2560]{1,0:T(8,128)(2,1)S(1)}, u32[]{:S(2)}, u32[]{:S(2)}) collective-permute-start(bf16[64,2560]{1,0:T(8,128)(2,1)S(1)} %get-tuple-element.105), channel_id=1, source_target_pairs={{0,12},{2,14},{4,8},{6,10},{8,4},{10,6},{12,0},{14,2},{1,13},{3,15... | collective-permute-start | bytes 983048 | tf_op jit(solution)/shard_map/ppermute | solution.py:171
  91.3 7.2 %collective-permute-done.24.p1 = bf16[64,2560]{1,0:T(8,128)(2,1)S(1)} collective-permute-done((bf16[64,2560]{1,0:T(8,128)(2,1)S(1)}, bf16[64,2560]{1,0:T(8,128)(2,1)S(1)}, u32[]{:S(2)}, u32[]{:S(2)}) %collective-permute-start.24) | collective-permute-done | bytes 327712 | tf_op jit(solution)/shard_map/ppermute | solution.py:171
  98.5 13.6 %collective-permute-done.25.p2 = bf16[64,2560]{1,0:T(8,128)(2,1)S(1)} collective-permute-done((bf16[64,2560]{1,0:T(8,128)(2,1)S(1)}, bf16[64,2560]{1,0:T(8,128)(2,1)S(1)}, u32[]{:S(2)}, u32[]{:S(2)}) %collective-permute-start.25) | collective-permute-done | bytes 327712 | tf_op jit(solution)/shard_map/ppermute | solution.py:171
  112.2 1.2 %shard_map.155 = (bf16[128,2048]{1,0:T(8,128)(2,1)}, bf16[128,512]{1,0:T(8,128)(2,1)}, f32[1,4,32]{2,1,0:T(4,128)}) custom-call(s32[1]{0:T(128)} %bitcast.me_ref, f32[128,2560]{1,0:T(8,128)S(1)} %get-tuple-element.94.own_ref, bf16[128,2688]{1,0:T(8,128)(2,1)S(1)} %collective-permute-done.23.sent_ref, bf16[128,128]{1,0:T(8,128)(2,1)S(1)} %get-tuple-element.102.rg_ref, ...), custom_call_target="tpu_custom_call" | custom-call | tf_op jit(solution)/shard_map/pallas_call | solution.py:541
  (68 shorter events, 17.3 us)
Async XLA Ops:
  0.6 18.4 %collective-permute-start.2 = (bf16[2048,128]{1,0:T(8,128)(2,1)}, bf16[2048,128]{1,0:T(8,128)(2,1)S(1)}, u32[]{:S(2)}, u32[]{:S(2)}) collective-permute-start(bf16[2048,128]{1,0:T(8,128)(2,1)} %bitcast.15), channel_id=1, source_target_pairs={{0,2},{2,0},{4,6},{6,4},{8,10},{10,8},{12,14},{14,12},{1,3},{3,1},... | collective-permute-start | bytes 1572872 | tf_op jit(solution)/shard_map/ppermute | solution.py:171
  3.6 17.2 %collective-permute-start.1 = (bf16[128,2048]{1,0:T(8,128)(2,1)}, bf16[128,2048]{1,0:T(8,128)(2,1)S(1)}, u32[]{:S(2)}, u32[]{:S(2)}) collective-permute-start(bf16[128,2048]{1,0:T(8,128)(2,1)} %x.1), channel_id=1, source_target_pairs={{4,8},{6,10},{8,4},{10,6},{5,9},{7,11},{9,5},{11,7},{20,24},{22,26... | collective-permute-start | bytes 1572872 | tf_op jit(solution)/shard_map/ppermute | solution.py:459
  4.3 16.5 %collective-permute-start = (bf16[128,2048]{1,0:T(8,128)(2,1)}, bf16[128,2048]{1,0:T(8,128)(2,1)S(1)}, u32[]{:S(2)}, u32[]{:S(2)}) collective-permute-start(bf16[128,2048]{1,0:T(8,128)(2,1)} %x.1), channel_id=1, source_target_pairs={{0,4},{2,6},{4,0},{6,2},{8,12},{10,14},{12,8},{14,10},{1,5},{3,7},... | collective-permute-start | bytes 1572872 | tf_op jit(solution)/shard_map/ppermute | solution.py:171
  8.8 1.0 copy-start
  17.8 30.3 %collective-permute-start.9 = (bf16[128,2816]{1,0:T(8,128)(2,1)S(1)}, bf16[128,2816]{1,0:T(8,128)(2,1)S(1)}, u32[]{:S(2)}, u32[]{:S(2)}) collective-permute-start(bf16[128,2816]{1,0:T(8,128)(2,1)S(1)} %get-tuple-element.65.gw_ref), channel_id=1, source_target_pairs={{0,2},{2,0},{4,6},{6,4},{8,10},{10,8},{12,14},{14,12},{1,3},{3,1},... | collective-permute-start | bytes 2162696 | tf_op jit(solution)/shard_map/ppermute | solution.py:171
  18.4 4.4 %collective-permute-start.6 = (bf16[80,2048]{1,0:T(8,128)(2,1)S(1)}, bf16[80,2048]{1,0:T(8,128)(2,1)S(1)}, u32[]{:S(2)}, u32[]{:S(2)}) collective-permute-start(bf16[80,2048]{1,0:T(8,128)(2,1)S(1)} %get-tuple-element.62.b0), channel_id=1, source_target_pairs={{4,8},{6,10},{8,4},{10,6},{5,9},{7,11},{9,5},{11,7},{20,24},{22,26... | collective-permute-start | bytes 983048 | tf_op jit(solution)/shard_map/ppermute | solution.py:465
  19.1 10.7 %collective-permute-start.5 = (bf16[80,2048]{1,0:T(8,128)(2,1)S(1)}, bf16[80,2048]{1,0:T(8,128)(2,1)S(1)}, u32[]{:S(2)}, u32[]{:S(2)}) collective-permute-start(bf16[80,2048]{1,0:T(8,128)(2,1)S(1)} %get-tuple-element.62.b0), channel_id=1, source_target_pairs={{0,4},{2,6},{4,0},{6,2},{8,12},{10,14},{12,8},{14,10},{1,5},{3,7},... | collective-permute-start | bytes 983048 | tf_op jit(solution)/shard_map/ppermute | solution.py:171
  20.8 9.6 %collective-permute-start.4 = (bf16[128,2048]{1,0:T(8,128)(2,1)S(1)}, bf16[128,2048]{1,0:T(8,128)(2,1)S(1)}, u32[]{:S(2)}, u32[]{:S(2)}) collective-permute-start(bf16[128,2048]{1,0:T(8,128)(2,1)S(1)} %collective-permute-done.x1), channel_id=1, source_target_pairs={{4,8},{6,10},{8,4},{10,6},{5,9},{7,11},{9,5},{11,7},{20,24},{22,26... | collective-permute-start | bytes 1572872 | tf_op jit(solution)/shard_map/ppermute | solution.py:467
  21.5 26.5 %collective-permute-start.3 = (bf16[128,2048]{1,0:T(8,128)(2,1)S(1)}, bf16[128,2048]{1,0:T(8,128)(2,1)S(1)}, u32[]{:S(2)}, u32[]{:S(2)}) collective-permute-start(bf16[128,2048]{1,0:T(8,128)(2,1)S(1)} %collective-permute-done.1.xi), channel_id=1, source_target_pairs={{4,0},{6,2},{8,12},{10,14},{5,1},{7,3},{9,13},{11,15},{20,16},{22,... | collective-permute-start | bytes 1572872 | tf_op jit(solution)/shard_map/ppermute | solution.py:467
  22.8 25.2 %collective-permute-start.7 = (bf16[80,2048]{1,0:T(8,128)(2,1)S(1)}, bf16[80,2048]{1,0:T(8,128)(2,1)S(1)}, u32[]{:S(2)}, u32[]{:S(2)}) collective-permute-start(bf16[80,2048]{1,0:T(8,128)(2,1)S(1)} %collective-permute-done.6.bi), channel_id=1, source_target_pairs={{4,0},{6,2},{8,12},{10,14},{5,1},{7,3},{9,13},{11,15},{20,16},{22,... | collective-permute-start | bytes 983048 | tf_op jit(solution)/shard_map/ppermute | solution.py:468
  29.8 18.3 %collective-permute-start.8 = (bf16[80,2048]{1,0:T(8,128)(2,1)S(1)}, bf16[80,2048]{1,0:T(8,128)(2,1)S(1)}, u32[]{:S(2)}, u32[]{:S(2)}) collective-permute-start(bf16[80,2048]{1,0:T(8,128)(2,1)S(1)} %collective-permute-done.5.b1), channel_id=1, source_target_pairs={{4,8},{6,10},{8,4},{10,6},{5,9},{7,11},{9,5},{11,7},{20,24},{22,26... | collective-permute-start | bytes 983048 | tf_op jit(solution)/shard_map/ppermute | solution.py:468
  30.5 28.1 %collective-permute-start.14 = (bf16[128,2048]{1,0:T(8,128)(2,1)S(1)}, bf16[128,2048]{1,0:T(8,128)(2,1)S(1)}, u32[]{:S(2)}, u32[]{:S(2)}) collective-permute-start(bf16[128,2048]{1,0:T(8,128)(2,1)S(1)} %collective-permute-done.4.xm), channel_id=1, source_target_pairs={{4,0},{6,2},{8,12},{10,14},{5,1},{7,3},{9,13},{11,15},{20,16},{22,... | collective-permute-start | bytes 1572872 | tf_op jit(solution)/shard_map/ppermute | solution.py:470
  50.1 1.9 %collective-permute-start.10 = (f32[384,256]{1,0:T(8,128)S(1)}, f32[384,256]{1,0:T(8,128)S(1)}, u32[]{:S(2)}, u32[]{:S(2)}) collective-permute-start(f32[384,256]{1,0:T(8,128)S(1)} %get-tuple-element.66.h_ref), channel_id=1, source_target_pairs={{0,1},{1,0},{2,3},{3,2},{4,5},{5,4},{6,7},{7,6},{8,9},{9,8},{10,11... | collective-permute-start | bytes 1179656 | tf_op jit(solution)/shard_map/ppermute | solution.py:175
  50.2 2.3 %collective-permute-start.11 = (f32[384,256]{1,0:T(8,128)S(1)}, f32[384,256]{1,0:T(8,128)S(1)}, u32[]{:S(2)}, u32[]{:S(2)}) collective-permute-start(f32[384,256]{1,0:T(8,128)S(1)} %get-tuple-element.67.s_ref), channel_id=1, source_target_pairs={{0,1},{1,0},{2,3},{3,2},{4,5},{5,4},{6,7},{7,6},{8,9},{9,8},{10,11... | collective-permute-start | bytes 1179656 | tf_op jit(solution)/shard_map/ppermute | solution.py:175
  50.7 15.4 %collective-permute-start.15 = (bf16[80,2048]{1,0:T(8,128)(2,1)S(1)}, bf16[80,2048]{1,0:T(8,128)(2,1)S(1)}, u32[]{:S(2)}, u32[]{:S(2)}) collective-permute-start(bf16[80,2048]{1,0:T(8,128)(2,1)S(1)} %collective-permute-done.8.bm), channel_id=1, source_target_pairs={{4,0},{6,2},{8,12},{10,14},{5,1},{7,3},{9,13},{11,15},{20,16},{22,... | collective-permute-start | bytes 983048 | tf_op jit(solution)/shard_map/ppermute | solution.py:471
  52.6 14.3 %collective-permute-start.16 = (bf16[128,384]{1,0:T(8,128)(2,1)S(1)}, bf16[128,384]{1,0:T(8,128)(2,1)S(1)}, u32[]{:S(2)}, u32[]{:S(2)}) collective-permute-start(bf16[128,384]{1,0:T(8,128)(2,1)S(1)} %get-tuple-element.75), channel_id=1, source_target_pairs={{0,2},{2,0},{4,6},{6,4},{8,10},{10,8},{12,14},{14,12},{1,3},{3,1},... | collective-permute-start | bytes 294920 | tf_op jit(solution)/shard_map/ppermute | solution.py:171
  54.2 12.7 %collective-permute-start.12 = (bf16[128,256]{1,0:T(8,128)(2,1)S(1)}, bf16[128,256]{1,0:T(8,128)(2,1)S(1)}, u32[]{:S(2)}, u32[]{:S(2)}) collective-permute-start(bf16[128,256]{1,0:T(8,128)(2,1)S(1)} %get-tuple-element.69), channel_id=1, source_target_pairs={{0,4},{2,6},{4,0},{6,2},{8,12},{10,14},{12,8},{14,10},{1,5},{3,7},... | collective-permute-start | bytes 196616 | tf_op jit(solution)/shard_map/ppermute | solution.py:171
  56.4 10.5 %collective-permute-start.13 = (bf16[128,256]{1,0:T(8,128)(2,1)S(1)}, bf16[128,256]{1,0:T(8,128)(2,1)S(1)}, u32[]{:S(2)}, u32[]{:S(2)}) collective-permute-start(bf16[128,256]{1,0:T(8,128)(2,1)S(1)} %get-tuple-element.70), channel_id=1, source_target_pairs={{0,8},{2,10},{4,12},{6,14},{8,0},{10,2},{12,4},{14,6},{1,9},{3,11}... | collective-permute-start | bytes 196616 | tf_op jit(solution)/shard_map/ppermute | solution.py:171
  67.0 5.5 %collective-permute-start.21 = (bf16[128,256]{1,0:T(8,128)(2,1)S(1)}, bf16[128,256]{1,0:T(8,128)(2,1)S(1)}, u32[]{:S(2)}, u32[]{:S(2)}) collective-permute-start(bf16[128,256]{1,0:T(8,128)(2,1)S(1)} %get-tuple-element.86), channel_id=1, source_target_pairs={{0,8},{2,10},{4,12},{6,14},{8,0},{10,2},{12,4},{14,6},{1,9},{3,11}... | collective-permute-start | bytes 196616 | tf_op jit(solution)/shard_map/ppermute | solution.py:171
  67.6 12.8 %collective-permute-start.20 = (bf16[128,256]{1,0:T(8,128)(2,1)S(1)}, bf16[128,256]{1,0:T(8,128)(2,1)S(1)}, u32[]{:S(2)}, u32[]{:S(2)}) collective-permute-start(bf16[128,256]{1,0:T(8,128)(2,1)S(1)} %get-tuple-element.83), channel_id=1, source_target_pairs={{0,4},{2,6},{4,0},{6,2},{8,12},{10,14},{12,8},{14,10},{1,5},{3,7},... | collective-permute-start | bytes 196616 | tf_op jit(solution)/shard_map/ppermute | solution.py:171
  70.1 4.6 %collective-permute-start.17 = (bf16[128,384]{1,0:T(8,128)(2,1)S(1)}, bf16[128,384]{1,0:T(8,128)(2,1)S(1)}, u32[]{:S(2)}, u32[]{:S(2)}) collective-permute-start(bf16[128,384]{1,0:T(8,128)(2,1)S(1)} %get-tuple-element.76), channel_id=1, source_target_pairs={{0,2},{2,0},{4,6},{6,4},{8,10},{10,8},{12,14},{14,12},{1,3},{3,1},... | collective-permute-start | bytes 294920 | tf_op jit(solution)/shard_map/ppermute | solution.py:171
  71.6 1.5 %collective-permute-start.18 = (f32[128,512]{1,0:T(8,128)S(1)}, f32[128,512]{1,0:T(8,128)S(1)}, u32[]{:S(2)}, u32[]{:S(2)}) collective-permute-start(f32[128,512]{1,0:T(8,128)S(1)} %get-tuple-element.78.m_ref), channel_id=1, source_target_pairs={{0,1},{1,0},{2,3},{3,2},{4,5},{5,4},{6,7},{7,6},{8,9},{9,8},{10,11... | collective-permute-start | bytes 786440 | tf_op jit(solution)/shard_map/ppermute | solution.py:175
  74.7 6.7 %collective-permute-start.19 = (bf16[128,256]{1,0:T(8,128)(2,1)S(1)}, bf16[128,256]{1,0:T(8,128)(2,1)S(1)}, u32[]{:S(2)}, u32[]{:S(2)}) collective-permute-start(bf16[128,256]{1,0:T(8,128)(2,1)S(1)} %get-tuple-element.82), channel_id=1, source_target_pairs={{0,12},{2,14},{4,8},{6,10},{8,4},{10,6},{12,0},{14,2},{1,13},{3,15... | collective-permute-start | bytes 196616 | tf_op jit(solution)/shard_map/ppermute | solution.py:171
  76.1 7.0 %collective-permute-start.22 = (bf16[128,256]{1,0:T(8,128)(2,1)S(1)}, bf16[128,256]{1,0:T(8,128)(2,1)S(1)}, u32[]{:S(2)}, u32[]{:S(2)}) collective-permute-start(bf16[128,256]{1,0:T(8,128)(2,1)S(1)} %get-tuple-element.88), channel_id=1, source_target_pairs={{0,14},{2,12},{4,10},{6,8},{8,6},{10,4},{12,2},{14,0},{1,15},{3,13... | collective-permute-start | bytes 196616 | tf_op jit(solution)/shard_map/ppermute | solution.py:171
  84.1 28.1 %collective-permute-start.23 = (bf16[128,2688]{1,0:T(8,128)(2,1)S(1)}, bf16[128,2688]{1,0:T(8,128)(2,1)S(1)}, u32[]{:S(2)}, u32[]{:S(2)}) collective-permute-start(bf16[128,2688]{1,0:T(8,128)(2,1)S(1)} %get-tuple-element.95), channel_id=1, source_target_pairs={{0,2},{2,0},{4,6},{6,4},{8,10},{10,8},{12,14},{14,12},{1,3},{3,1},... | collective-permute-start | bytes 2064392 | tf_op jit(solution)/shard_map/ppermute | solution.py:171
  86.0 28.2 %collective-permute-start.27 = (bf16[2048,128]{1,0:T(8,128)(2,1)S(1)}, bf16[2048,128]{1,0:T(8,128)(2,1)S(1)}, u32[]{:S(2)}, u32[]{:S(2)}) collective-permute-start(bf16[2048,128]{1,0:T(8,128)(2,1)S(1)} %fusion.1), channel_id=1, source_target_pairs={{0,2},{2,0},{4,6},{6,4},{8,10},{10,8},{12,14},{14,12},{1,3},{3,1},... | collective-permute-start | bytes 1572872 | tf_op jit(solution)/shard_map/ppermute | solution.py:171
  86.6 11.9 %collective-permute-start.24 = (bf16[64,2560]{1,0:T(8,128)(2,1)S(1)}, bf16[64,2560]{1,0:T(8,128)(2,1)S(1)}, u32[]{:S(2)}, u32[]{:S(2)}) collective-permute-start(bf16[64,2560]{1,0:T(8,128)(2,1)S(1)} %get-tuple-element.97), channel_id=1, source_target_pairs={{0,4},{2,6},{4,0},{6,2},{8,12},{10,14},{12,8},{14,10},{1,5},{3,7},... | collective-permute-start | bytes 983048 | tf_op jit(solution)/shard_map/ppermute | solution.py:171
  86.6 25.5 %collective-permute-start.25 = (bf16[64,2560]{1,0:T(8,128)(2,1)S(1)}, bf16[64,2560]{1,0:T(8,128)(2,1)S(1)}, u32[]{:S(2)}, u32[]{:S(2)}) collective-permute-start(bf16[64,2560]{1,0:T(8,128)(2,1)S(1)} %get-tuple-element.100), channel_id=1, source_target_pairs={{0,8},{2,10},{4,12},{6,14},{8,0},{10,2},{12,4},{14,6},{1,9},{3,11}... | collective-permute-start | bytes 983048 | tf_op jit(solution)/shard_map/ppermute | solution.py:171
  89.6 22.6 %copy-start.7 = (s32[1,32,4]{1,2,0:T(4,128)S(1)}, s32[1,32,4]{1,2,0:T(4,128)}, u32[]{:S(2)}) copy-start(s32[1,32,4]{1,2,0:T(4,128)} %param.17) | copy-start | bytes 1540
  89.6 22.6 %copy-start.9 = (s32[1,128]{1,0:T(1,128)S(1)}, s32[1,128]{1,0:T(1,128)}, u32[]{:S(2)}) copy-start(s32[1,128]{1,0:T(1,128)} %tr_ref.1) | copy-start | bytes 1540
  89.6 22.6 %copy-start.11 = (s32[1,32]{1,0:T(1,128)S(1)}, s32[1,32]{1,0:T(1,128)}, u32[]{:S(2)}) copy-start(s32[1,32]{1,0:T(1,128)} %rc_ref.1) | copy-start | bytes 388
  89.6 23.8 %collective-permute-start.26 = (bf16[64,2560]{1,0:T(8,128)(2,1)S(1)}, bf16[64,2560]{1,0:T(8,128)(2,1)S(1)}, u32[]{:S(2)}, u32[]{:S(2)}) collective-permute-start(bf16[64,2560]{1,0:T(8,128)(2,1)S(1)} %get-tuple-element.105), channel_id=1, source_target_pairs={{0,12},{2,14},{4,8},{6,10},{8,4},{10,6},{12,0},{14,2},{1,13},{3,15... | collective-permute-start | bytes 983048 | tf_op jit(solution)/shard_map/ppermute | solution.py:171
  (9 other events, 7.4 us)

commit v4 on v3

--- a/solution.py
+++ b/solution.py
@@ -280,8 +280,7 @@
     for i, g_ref in enumerate((gw_ref, gx_ref)):
         part_q = dot(g_ref[:, :wide], bq, COLS)
         part_v = dot(g_ref[:, wide:full], bv, COLS)
-        cols = slice(first + i * rank2, first + (i + 1) * rank2)
-        out_ref[rows, cols] = jnp.concatenate([part_q, part_v], axis=1)
+        out_ref[rows, first + i * rank2 : first + (i + 1) * rank2] = jnp.concatenate([part_q, part_v], axis=1)
 
 
 def products_early(x0, x1, xo, xm, b0, b1, bo, bm, a_ref, ax_ref, gw_ref, gx_ref, h_ref, s_ref, x2_ref, b2_ref):
@@ -295,59 +294,55 @@
 
 
 def products_late(xi, xo, bi, bo, a_ref, ax_ref, gw_ref, gx_ref, out_ref, x3_ref, b3_ref):
-    rank2 = a_ref.shape[1]
     x3_ref[...] = xi[...] + xo[...]
     b3_ref[...] = bi[...] + bo[...]
     rows = slice(0, x3_ref.shape[0])
     hidden_of(x3_ref[...], rows, a_ref, ax_ref, out_ref)
-    slopes_of(b3_ref[...], rows, 2 * rank2, gw_ref, gx_ref, out_ref)
-
-
-def split_early(h_ref, hr_ref, s_ref, sr_ref, gw_ref, gx_ref, e0, e1, e2, sl_ref, c_ref, d_ref):
-    count = e0.shape[0]
-    rank2 = e0.shape[1] // 2
-    for j, e in enumerate((e0, e1, e2)):
+    slopes_of(b3_ref[...], rows, 2 * a_ref.shape[1], gw_ref, gx_ref, out_ref)
+
+
+def split_early(m_ref, mr_ref, s_ref, sr_ref, gw_ref, gx_ref, sl_ref, near_ref, far_ref):
+    count = gw_ref.shape[0]
+    both = m_ref.shape[1]
+    for j in range(LINE - 1):
         rows = slice(j * count, (j + 1) * count)
-        cols = slice(j * rank2, (j + 1) * rank2)
-        e[...] = (h_ref[rows, :] + hr_ref[rows, :]).astype(BF16)
-        total = s_ref[rows, :] + sr_ref[rows, :]
-        sl_ref[rows, :] = total
-        c_ref[:, cols] = (weight_of(gw_ref, 2 * j) * total[:, :rank2]).astype(BF16)
-        d_ref[:, cols] = (weight_of(gx_ref, 2 * j + 1) * total[:, rank2:]).astype(BF16)
-
-
-def pack_early(e0, e1, e2, c_ref, d_ref, t_ref, q0, q1, q2):
-    rank2 = e0.shape[1] // 2
-    for j, (e, q) in enumerate(((e0, q0), (e1, q1), (e2, q2))):
-        cols = slice(j * rank2, (j + 1) * rank2)
-        t_ref[:, cols] = e[:, rank2:]
-        q[:, :rank2] = c_ref[:, cols]
-        q[:, rank2:] = d_ref[:, cols]
+        cols = pl.ds(j * both, both)
+        slope = s_ref[rows, :] + sr_ref[rows, :]
+        sl_ref[rows, :] = slope
+        blocks = near_ref.at[:, cols], far_ref.at[:, cols]
+        fill_blocks(j, m_ref[rows, :] + mr_ref[rows, :], slope, gw_ref, gx_ref, *blocks)
+
+
+def pack_slots(near_ref, far_ref, *out_refs):
+    rank2 = out_refs[0].shape[1] // 4
+    for j, out_ref in enumerate(out_refs):
+        for half in range(2):
+            first = (2 * j + half) * rank2
+            out_ref[:, 2 * half * rank2 : (2 * half + 1) * rank2] = near_ref[:, first : first + rank2]
+            out_ref[:, (2 * half + 1) * rank2 : (2 * half + 2) * rank2] = far_ref[:, first : first + rank2]
 
 
 def split_late(m_ref, r_ref, gw_ref, gx_ref, sl_ref, near_ref, far_ref):
+    total = m_ref[...] + r_ref[...]
+    half = total.shape[1] // 2
+    sl_ref[...] = total[:, half:]
+    fill_blocks(LINE - 1, total[:, :half], total[:, half:], gw_ref, gx_ref, near_ref, far_ref)
+
+
+def fill_blocks(j, hidden, slope, gw_ref, gx_ref, near_ref, far_ref):
     rank2 = near_ref.shape[1] // 2
-    total = m_ref[...] + r_ref[...]
-    sl_ref[...] = total[:, 2 * rank2 :]
-    near_ref[:, :rank2] = total[:, :rank2].astype(BF16)
-    far_ref[:, :rank2] = total[:, rank2 : 2 * rank2].astype(BF16)
-    near_ref[:, rank2:] = (weight_of(gw_ref, 6) * total[:, 2 * rank2 : 3 * rank2]).astype(BF16)
-    far_ref[:, rank2:] = (weight_of(gx_ref, 7) * total[:, 3 * rank2 :]).astype(BF16)
-
-
-def grad_b_part(wide, first, owns, others, gw_ref, gx_ref, wt_ref, p_refs):
+    hidden = hidden.astype(BF16)
+    near_ref[:, :rank2] = hidden[:, :rank2]
+    far_ref[:, :rank2] = hidden[:, rank2:]
+    near_ref[:, rank2:] = (weight_of(gw_ref, 2 * j) * slope[:, :rank2]).astype(BF16)
+    far_ref[:, rank2:] = (weight_of(gx_ref, 2 * j + 1) * slope[:, rank2:]).astype(BF16)
+
+
+def grad_b_parts(wide, wt_ref, gw_ref, gx_ref, *p_refs):
     count = gw_ref.shape[0]
-    rank2 = 2 * p_refs[0].shape[0]
-    rank = rank2 // 2
-    full = p_refs[0].shape[1]
-    for j, (own, other) in enumerate(zip(owns, others)):
-        cols = slice(j * rank2, (j + 1) * rank2)
-        own = weight_of(gw_ref, 2 * (first + j)) * own.astype(F32)
-        other = weight_of(gx_ref, 2 * (first + j) + 1) * other.astype(F32)
-        wt_ref[:count, cols] = own.astype(BF16)
-        wt_ref[count:, cols] = other.astype(BF16)
+    rank, full = p_refs[0].shape
     slots = len(p_refs)
-    left = [j * rank2 + i * rank for i in range(2) for j in range(slots)]
+    left = [(2 * j + i) * rank for i in range(2) for j in range(slots)]
     both = wt_ref[...]
     both = jnp.concatenate([both[:, c : c + rank] for c in left], axis=1)
     own, other = both[:count], both[count:]
@@ -359,30 +354,16 @@
         p_ref[:, wide:] = part_v[j * rank : (j + 1) * rank].astype(p_ref.dtype)
 
 
-def grad_b_early(wide, e0, e1, e2, t_ref, gw_ref, gx_ref, wt_ref, p0, p1, p2):
-    rank2 = e0.shape[1] // 2
-    owns = [e[:, :rank2] for e in (e0, e1, e2)]
-    others = [t_ref[:, j * rank2 : (j + 1) * rank2] for j in range(3)]
-    grad_b_part(wide, 0, owns, others, gw_ref, gx_ref, wt_ref, (p0, p1, p2))
-
-
-def grad_b_late(wide, near_ref, far_ref, gw_ref, gx_ref, wt_ref, p3):
-    rank2 = near_ref.shape[1] // 2
-    grad_b_part(wide, 3, (near_ref[:, :rank2],), (far_ref[:, :rank2],), gw_ref, gx_ref, wt_ref, (p3,))
-
-
-def grad_b_near(p0, p1, p2, sum_ref):
-    sum_ref[...] = p0[...] + p1[...].astype(F32) + p2[...].astype(F32)
-
-
-def grad_b_sum(near_ref, p3, q_ref, v_ref):
+def grad_b_sum(p0, p1, p2, p3, q_ref, v_ref):
     wide = q_ref.shape[2]
-    total = near_ref[...] + p3[...].astype(F32)
+    total = p0[...] + p1[...].astype(F32) + p2[...].astype(F32) + p3[...].astype(F32)
     q_ref[0] = total[:, :wide].astype(BF16)
     v_ref[0] = total[:, wide:].astype(BF16)
 
 
-def outputs_part(wt_ref, wt3_ref, b0, b1, b2, b3, s_ref, s3_ref, e0, e1, e2, t_ref, near, far, own_ref, sent_ref, rg_ref):
+def outputs_part(
+    c0, c1, c2, n3, f3, gw_ref, gx_ref, b0, b1, b2, b3, s_ref, s3_ref, own_ref, sent_ref, rg_ref, wt_ref
+):
     count, full = own_ref.shape
     wide = b0.shape[1]
     parts = [b_parts(b[...], full - wide) for b in (b0, b1, b2, b3)]
@@ -390,7 +371,15 @@
     bv = jnp.concatenate([part[1] for part in parts], axis=0)
     rank = bq.shape[0] // LINE
     rank2 = 2 * rank
-    both = jnp.concatenate([wt_ref[...], wt3_ref[...]], axis=1)
+    owns = [c[:, :rank2] for c in (c0, c1, c2, n3)]
+    others = [c[:, rank2 : 2 * rank2] for c in (c0, c1, c2)] + [f3[:, :rank2]]
+    for j in range(LINE):
+        cols = slice(j * rank2, (j + 1) * rank2)
+        own = weight_of(gw_ref, 2 * j) * owns[j].astype(F32)
+        other = weight_of(gx_ref, 2 * j + 1) * others[j].astype(F32)
+        wt_ref[:count, cols] = own.astype(BF16)
+        wt_ref[count:, cols] = other.astype(BF16)
+    both = wt_ref[...]
     q = jnp.concatenate([both[:, j * rank2 : j * rank2 + rank] for j in range(LINE)], axis=1)
     v = jnp.concatenate([both[:, j * rank2 + rank : (j + 1) * rank2] for j in range(LINE)], axis=1)
     out_q = dot(q, bq, SAME)
@@ -400,14 +389,12 @@
     sent_ref[:, :wide] = out_q[count:].astype(BF16)
     sent_ref[:, wide:full] = out_v[count:].astype(BF16)
     lane = lax.broadcasted_iota(jnp.int32, (count, LANES), 1)
-    owns = [e[:, :rank2] for e in (e0, e1, e2, near)]
-    others = [t_ref[:, j * rank2 : (j + 1) * rank2] for j in range(3)] + [far[:, :rank2]]
-    for i, hid in enumerate((owns, others)):
+    for i, blocks in enumerate((owns, others)):
         cols = slice(i * rank2, (i + 1) * rank2)
         found = jnp.zeros((count, LANES), F32)
-        for j in range(LINE):
+        for j, block in enumerate(blocks):
             slope = s_ref[j * count : (j + 1) * count, cols] if j < 3 else s3_ref[:, cols]
-            grad = jnp.sum(slope * hid[j].astype(F32), axis=1, keepdims=True)
+            grad = jnp.sum(slope * block.astype(F32), axis=1, keepdims=True)
             found = jnp.where(lane == 2 * j + i, jnp.broadcast_to(grad, found.shape), found)
         if i == 0:
             rg_ref[...] = found.astype(BF16)
@@ -476,59 +463,54 @@
         [((3 * count, 2 * rank2), F32), ((3 * count, 2 * rank2), F32), x_block, wide_block],
         x0, x1, xo, xm, b0, b1, bo, bm, a_own, a_other, gw, gx,
     )
-    e0, e1, e2, sl, c, d = call(
+    sl, near, far = call(
         split_early,
-        [pair] * 3 + [((3 * count, 2 * rank2), F32), early, early],
+        [((3 * count, 2 * rank2), F32), ((count, 6 * rank2), BF16), ((count, 6 * rank2), BF16)],
         m, other_core(m), ms, other_core(ms), gw, gx,
     )
-    e1, e2, d = to_place(e1, 2), to_place(e2, 4), to_place(d, 1)
-    (xo3,) = after(e0, xo3)
-    m3, x3, b3 = call(
+    near, far, xo3 = lax.optimization_barrier((near, far, xo3))
+    far = to_place(far, 1)
+    (bo3,) = after(far, bo3)
+    c0, c1, c2 = call(pack_slots, [((count, 4 * rank2), BF16)] * 3, near, far)
+    c1, c2 = to_place(c1, 2), to_place(c2, 4)
+    h3, x3, b3 = call(
         products_late,
         [((count, 4 * rank2), F32), x_block, wide_block],
         xi, xo3, bi, bo3, a_own, a_other, gw, gx,
     )
-    (c,) = after(m3, c)
-    t, q0, q1, q2 = call(pack_early, [early] + [pair] * 3, e0, e1, e2, c, d)
-    t, q1, q2 = to_place(t, 1), to_place(q1, 2), to_place(q2, 4)
-    m3 = after(q0, m3)[0]
-    sl3, z3, z7 = call(
-        split_late, [((count, 2 * rank2), F32), pair, pair], m3, other_core(m3), gw, gx
-    )
-    z3, z7 = to_place(z3, 6), to_place(z7, 7)
-    (t,) = after(sl3, t)
-    wt, p0, p1, p2 = call(
-        functools.partial(grad_b_early, wide),
-        [((2 * count, 3 * rank2), BF16), ((rank, full), F32), b_block, b_block],
-        e0, e1, e2, t, gw, gx,
-    )
-    (q1,) = after(wt, q1)
-    p1, p2 = to_place(p1, 2), to_place(p2, 4)
-    x1s, x2s, x3s = x1, x2, x3
-    grad_a = dot(x0, q0, ROWS) + dot(x1s, q1, ROWS) + dot(x2s, q2, ROWS)
-    (z3,) = after(grad_a, z3)
-    wt3, p3 = call(functools.partial(grad_b_late, wide), [((2 * count, rank2), BF16), b_block], z3, z7, gw, gx)
-    p3 = to_place(p3, 6)
-    (wt,) = after(wt3, wt)
-    out_own, sent, rg = call(
+    rh = other_core(h3)
+    c1, c2 = after(h3, c1, c2)
+    grad_a = dot(x0, c0[:, 2 * rank2 :], ROWS) + dot(x1, c1[:, 2 * rank2 :], ROWS) + dot(x2, c2[:, 2 * rank2 :], ROWS)
+    rh, grad_a = lax.optimization_barrier((rh, grad_a))
+    sl3, n3, f3 = call(
+        split_late,
+        [((count, 2 * rank2), F32), pair, pair],
+        h3, rh, gw, gx,
+    )
+    n3, f3 = to_place(n3, 6), to_place(f3, 7)
+    out_own, sent, rg, wt = call(
         outputs_part,
-        [((count, full), F32), ((count, full + LANES), BF16), ((count, LANES), BF16)],
-        wt, wt3, b0, b1, b2, b3, sl, sl3, e0, e1, e2, t, z3, z7,
+        [((count, full), F32), ((count, full + LANES), BF16), ((count, LANES), BF16), ((2 * count, LINE * rank2), BF16)],
+        c0, c1, c2, n3, f3, gw, gx, b0, b1, b2, b3, sl, sl3,
     )
     sent = to_place(sent, 1)
-    (z7,) = after(out_own, z7)
-    grad_a_other = (grad_a[:, rank2:] + dot(x3s, z7[:, rank2:], ROWS)).astype(BF16)
-    grad_a = grad_a[:, :rank2] + dot(x3s, z3[:, rank2:], ROWS)
-    (p1,) = after(grad_a, p1)
-    (near_sum,) = call(grad_b_near, [((rank, full), F32)], p0, p1, p2)
-    (sent,) = after(near_sum, sent)
+    (f3s,) = after(out_own, f3)
+    grad_a_other = (grad_a[:, rank2:] + dot(x3, f3s[:, rank2:], ROWS)).astype(BF16)
+    (wt,) = after(grad_a_other, wt)
+    p0, p1, p2, p3 = call(
+        functools.partial(grad_b_parts, wide), [((rank, full), F32)] + [b_block] * 3, wt, gw, gx
+    )
+    p1, p2, p3 = to_place(p1, 2), to_place(p2, 4), to_place(p3, 6)
+    (n3s,) = after(p0, n3)
+    grad_a = grad_a[:, :rank2] + dot(x3, n3s[:, rank2:], ROWS)
+    (sent,) = after(grad_a, sent)
     out_query, out_value, grad_mix = call_sum(
         me, out_own, sent, rg, token_request, adapters, req_count, grad_query, grad_value
     )
-    (p3,) = after(out_query, p3)
-    grad_bq, grad_bv = call(grad_b_sum, [(b_query.shape, BF16), (b_value.shape, BF16)], near_sum, p3)
-    (grad_a,) = after(grad_bq, grad_a)
+    (grad_a,) = after(out_query, grad_a)
     grad_a = grad_a + to_place(grad_a_other, 1).astype(F32)
+    (p1,) = after(grad_a, p1)
+    grad_bq, grad_bv = call(grad_b_sum, [(b_query.shape, BF16), (b_value.shape, BF16)], p0, p1, p2, p3)
     return out_query, out_value, grad_a.astype(BF16)[None], grad_bq, grad_bv, jnp.swapaxes(grad_mix, 1, 2)
 
 

time: 116 us -> 111 us (0.957)
  starting transfers between devices: 38.5 us -> 32.9 us
    ppermute x1, waiting for transfers between devices: 7.48 us -> 0.38 us  [pair_plan(): bo3 = lax.ppermute(bm, 'expert', OUT)]
    ppermute x17 -> x14, starting transfers between devices: 30.1 us -> 24.4 us  [to_place(): lax.ppermute(array, 'expert', [(i, i ^ place) for i in range(LINE * PAIR)])]
    ppermute x1, waiting for transfers between devices: 1.52 us -> 6.27 us  [pair_plan(): xo3 = lax.ppermute(xm, 'expert', OUT)]
    ppermute x17 -> x14, waiting for transfers between devices: 30.6 us -> 32.4 us  [to_place(): lax.ppermute(array, 'expert', [(i, i ^ place) for i in range(LINE * PAIR)])]
    pallas_call x10 -> x8, Pallas kernels: 6.01 us -> 5.8 us  [call(): pl.pallas_call(kernel, out_shape=shapes, in_specs=[pl.BlockSpec(memory_sp...]
  transfers between devices with their start and end apart: 28 -> 25, of which waited for: 11 -> 12; matrix products, arithmetic and copies ran while one was open for 2% -> 3% of each run, Pallas kernels for 6% -> 5%
where the time goes in v4:
time: 111 us; the launch traced here: 109 us
  waiting for transfers between devices  56.3 us (51%)
  starting transfers between devices  32.9 us (30%)
  local copies, waits for them, and re-layouts  8.49 us (8%)
  Pallas kernels  7.52 us (7%)
  matrix products  2.06 us (2%)
    ppermute x14, waiting for transfers between devices, to_place(): lax.ppermute(array, 'expert', [(i, i ^ place) for i in range(LINE * PAIR)])  32.4 us
    ppermute x14, starting transfers between devices, to_place(): lax.ppermute(array, 'expert', [(i, i ^ place) for i in range(LINE * PAIR)])  24.4 us
    ppermute x2, waiting for transfers between devices, pair_plan(): bo, bm = (lax.ppermute(bi, 'expert', OUT), lax.ppermute(b1, 'expert', MID))  16.8 us
    unnamed x26, local copies, waits for them, and re-layouts  8.49 us
    ppermute x1, waiting for transfers between devices, pair_plan(): xo3 = lax.ppermute(xm, 'expert', OUT)  6.27 us
    pallas_call x8, Pallas kernels, call(): pl.pallas_call(kernel, out_shape=shapes, in_specs=[pl.BlockSpec(memory_sp...  5.8 us
  transfers between devices with their start and end apart: 25, of which 12 were waited for; matrix products, arithmetic and copies ran while one was open for 3% of the time, Pallas kernels for 5%

profile of v4, /device:TPU:0, one launch (start us, length us, event | category | flops | bytes accessed | tf_op | source)
XLA Modules:
  0.0 109.1 jit_solution(220032317847910739)
XLA Ops:
  0.6 3.0 %collective-permute-start.2 = (bf16[2048,128]{1,0:T(8,128)(2,1)}, bf16[2048,128]{1,0:T(8,128)(2,1)S(1)}, u32[]{:S(2)}, u32[]{:S(2)}) collective-permute-start(bf16[2048,128]{1,0:T(8,128)(2,1)} %bitcast.13), channel_id=1, source_target_pairs={{0,2},{2,0},{4,6},{6,4},{8,10},{10,8},{12,14},{14,12},{1,3},{3,1},... | collective-permute-start | bytes 1572872 | tf_op jit(solution)/shard_map/ppermute | solution.py:171
  3.6 1.6 %collective-permute-start = (bf16[128,2048]{1,0:T(8,128)(2,1)}, bf16[128,2048]{1,0:T(8,128)(2,1)S(1)}, u32[]{:S(2)}, u32[]{:S(2)}) collective-permute-start(bf16[128,2048]{1,0:T(8,128)(2,1)} %x.1), channel_id=1, source_target_pairs={{0,4},{2,6},{4,0},{6,2},{8,12},{10,14},{12,8},{14,10},{1,5},{3,7},... | collective-permute-start | bytes 1572872 | tf_op jit(solution)/shard_map/ppermute | solution.py:171
  5.9 1.0 copy-done
  7.0 1.0 copy-done.1
  8.0 1.0 copy-done.2
  9.0 0.9 copy-done.3
  10.0 0.9 copy-done.4
  15.5 4.4 %collective-permute-start.5 = (bf16[80,2048]{1,0:T(8,128)(2,1)S(1)}, bf16[80,2048]{1,0:T(8,128)(2,1)S(1)}, u32[]{:S(2)}, u32[]{:S(2)}) collective-permute-start(bf16[80,2048]{1,0:T(8,128)(2,1)S(1)} %get-tuple-element.59.b0), channel_id=1, source_target_pairs={{0,4},{2,6},{4,0},{6,2},{8,12},{10,14},{12,8},{14,10},{1,5},{3,7},... | collective-permute-start | bytes 983048 | tf_op jit(solution)/shard_map/ppermute | solution.py:171
  21.3 1.3 %collective-permute-start.3 = (bf16[128,2048]{1,0:T(8,128)(2,1)S(1)}, bf16[128,2048]{1,0:T(8,128)(2,1)S(1)}, u32[]{:S(2)}, u32[]{:S(2)}) collective-permute-start(bf16[128,2048]{1,0:T(8,128)(2,1)S(1)} %collective-permute-done.1.xi), channel_id=1, source_target_pairs={{4,0},{6,2},{8,12},{10,14},{5,1},{7,3},{9,13},{11,15},{20,16},{22,... | collective-permute-start | bytes 1572872 | tf_op jit(solution)/shard_map/ppermute | solution.py:454
  22.6 4.2 %collective-permute-done.5.b1 = bf16[80,2048]{1,0:T(8,128)(2,1)S(1)} collective-permute-done((bf16[80,2048]{1,0:T(8,128)(2,1)S(1)}, bf16[80,2048]{1,0:T(8,128)(2,1)S(1)}, u32[]{:S(2)}, u32[]{:S(2)}) %collective-permute-start.5) | collective-permute-done | bytes 327712 | tf_op jit(solution)/shard_map/ppermute | solution.py:171
  27.5 1.3 %collective-permute-start.7 = (bf16[80,2048]{1,0:T(8,128)(2,1)S(1)}, bf16[80,2048]{1,0:T(8,128)(2,1)S(1)}, u32[]{:S(2)}, u32[]{:S(2)}) collective-permute-start(bf16[80,2048]{1,0:T(8,128)(2,1)S(1)} %collective-permute-done.6.bi), channel_id=1, source_target_pairs={{4,0},{6,2},{8,12},{10,14},{5,1},{7,3},{9,13},{11,15},{20,16},{22,... | collective-permute-start | bytes 983048 | tf_op jit(solution)/shard_map/ppermute | solution.py:455
  28.8 1.3 %collective-permute-start.12 = (bf16[128,2048]{1,0:T(8,128)(2,1)S(1)}, bf16[128,2048]{1,0:T(8,128)(2,1)S(1)}, u32[]{:S(2)}, u32[]{:S(2)}) collective-permute-start(bf16[128,2048]{1,0:T(8,128)(2,1)S(1)} %collective-permute-done.4.xm), channel_id=1, source_target_pairs={{4,0},{6,2},{8,12},{10,14},{5,1},{7,3},{9,13},{11,15},{20,16},{22,... | collective-permute-start | bytes 1572872 | tf_op jit(solution)/shard_map/ppermute | solution.py:457
  30.2 16.8 %collective-permute-done.7.bo = bf16[80,2048]{1,0:T(8,128)(2,1)S(1)} collective-permute-done((bf16[80,2048]{1,0:T(8,128)(2,1)S(1)}, bf16[80,2048]{1,0:T(8,128)(2,1)S(1)}, u32[]{:S(2)}, u32[]{:S(2)}) %collective-permute-start.7) | collective-permute-done | bytes 327712 | tf_op jit(solution)/shard_map/ppermute | solution.py:455
  46.9 2.0 %shard_map.146 = (f32[384,256]{1,0:T(8,128)S(1)}, f32[384,256]{1,0:T(8,128)S(1)}, bf16[128,2048]{1,0:T(8,128)(2,1)S(1)}, bf16[80,2048]{1,0:T(8,128)(2,1)S(1)}) custom-call(bf16[128,2048]{1,0:T(8,128)(2,1)S(1)} %get-tuple-element.56.x0, bf16[128,2048]{1,0:T(8,128)(2,1)S(1)} %collective-permute-done.x1, bf16[128,2048]{1,0:T(8,128)(2,1)S(1)} %collective-permute-done.3.xo, ...), custom_call_target="tpu_custom_call" | custom-call | tf_op jit(solution)/shard_map/pallas_call | solution.py:193
  49.5 1.3 %collective-permute-start.16 = (bf16[80,2048]{1,0:T(8,128)(2,1)S(1)}, bf16[80,2048]{1,0:T(8,128)(2,1)S(1)}, u32[]{:S(2)}, u32[]{:S(2)}) collective-permute-start(bf16[80,2048]{1,0:T(8,128)(2,1)S(1)} %collective-permute-done.8.bm), channel_id=1, source_target_pairs={{4,0},{6,2},{8,12},{10,14},{5,1},{7,3},{9,13},{11,15},{20,16},{22,... | collective-permute-start | bytes 983048 | tf_op jit(solution)/shard_map/ppermute | solution.py:458
  51.5 6.3 %collective-permute-done.12.xo = bf16[128,2048]{1,0:T(8,128)(2,1)S(1)} collective-permute-done((bf16[128,2048]{1,0:T(8,128)(2,1)S(1)}, bf16[128,2048]{1,0:T(8,128)(2,1)S(1)}, u32[]{:S(2)}, u32[]{:S(2)}) %collective-permute-start.12) | collective-permute-done | bytes 524320 | tf_op jit(solution)/shard_map/ppermute | solution.py:457
  57.8 1.5 %collective-permute-start.13 = (bf16[128,768]{1,0:T(8,128)(2,1)S(1)}, bf16[128,768]{1,0:T(8,128)(2,1)S(1)}, u32[]{:S(2)}, u32[]{:S(2)}) collective-permute-start(bf16[128,768]{1,0:T(8,128)(2,1)S(1)} %get-tuple-element.68), channel_id=1, source_target_pairs={{0,2},{2,0},{4,6},{6,4},{8,10},{10,8},{12,14},{14,12},{1,3},{3,1},... | collective-permute-start | bytes 589832 | tf_op jit(solution)/shard_map/ppermute | solution.py:171
  59.3 4.2 %collective-permute-done.13.far_ref = bf16[128,768]{1,0:T(8,128)(2,1)S(1)} collective-permute-done((bf16[128,768]{1,0:T(8,128)(2,1)S(1)}, bf16[128,768]{1,0:T(8,128)(2,1)S(1)}, u32[]{:S(2)}, u32[]{:S(2)}) %collective-permute-start.13) | collective-permute-done | bytes 196640 | tf_op jit(solution)/shard_map/ppermute | solution.py:171
  63.6 1.8 %collective-permute-start.15 = (bf16[128,512]{1,0:T(8,128)(2,1)S(1)}, bf16[128,512]{1,0:T(8,128)(2,1)S(1)}, u32[]{:S(2)}, u32[]{:S(2)}) collective-permute-start(bf16[128,512]{1,0:T(8,128)(2,1)S(1)} %get-tuple-element.71), channel_id=1, source_target_pairs={{0,8},{2,10},{4,12},{6,14},{8,0},{10,2},{12,4},{14,6},{1,9},{3,11}... | collective-permute-start | bytes 393224 | tf_op jit(solution)/shard_map/ppermute | solution.py:171
  66.7 3.2 %collective-permute-done.14.c1 = bf16[128,512]{1,0:T(8,128)(2,1)S(1)} collective-permute-done((bf16[128,512]{1,0:T(8,128)(2,1)S(1)}, bf16[128,512]{1,0:T(8,128)(2,1)S(1)}, u32[]{:S(2)}, u32[]{:S(2)}) %collective-permute-start.14) | collective-permute-done | bytes 131104 | tf_op jit(solution)/shard_map/ppermute | solution.py:171
  71.5 2.5 %collective-permute-start.18 = (bf16[128,256]{1,0:T(8,128)(2,1)S(1)}, bf16[128,256]{1,0:T(8,128)(2,1)S(1)}, u32[]{:S(2)}, u32[]{:S(2)}) collective-permute-start(bf16[128,256]{1,0:T(8,128)(2,1)S(1)} %get-tuple-element.79), channel_id=1, source_target_pairs={{0,12},{2,14},{4,8},{6,10},{8,4},{10,6},{12,0},{14,2},{1,13},{3,15... | collective-permute-start | bytes 196616 | tf_op jit(solution)/shard_map/ppermute | solution.py:171
  74.0 2.3 %collective-permute-start.19 = (bf16[128,256]{1,0:T(8,128)(2,1)S(1)}, bf16[128,256]{1,0:T(8,128)(2,1)S(1)}, u32[]{:S(2)}, u32[]{:S(2)}) collective-permute-start(bf16[128,256]{1,0:T(8,128)(2,1)S(1)} %get-tuple-element.80), channel_id=1, source_target_pairs={{0,14},{2,12},{4,10},{6,8},{8,6},{10,4},{12,2},{14,0},{1,15},{3,13... | collective-permute-start | bytes 196616 | tf_op jit(solution)/shard_map/ppermute | solution.py:171
  76.3 1.4 %collective-permute-done.18.n3 = bf16[128,256]{1,0:T(8,128)(2,1)S(1)} collective-permute-done((bf16[128,256]{1,0:T(8,128)(2,1)S(1)}, bf16[128,256]{1,0:T(8,128)(2,1)S(1)}, u32[]{:S(2)}, u32[]{:S(2)}) %collective-permute-start.18) | collective-permute-done | bytes 65568 | tf_op jit(solution)/shard_map/ppermute | solution.py:171
  77.7 3.4 %collective-permute-done.19.f3 = bf16[128,256]{1,0:T(8,128)(2,1)S(1)} collective-permute-done((bf16[128,256]{1,0:T(8,128)(2,1)S(1)}, bf16[128,256]{1,0:T(8,128)(2,1)S(1)}, u32[]{:S(2)}, u32[]{:S(2)}) %collective-permute-start.19) | collective-permute-done | bytes 65568 | tf_op jit(solution)/shard_map/ppermute | solution.py:171
  81.9 1.6 %collective-permute-start.20 = (bf16[128,2688]{1,0:T(8,128)(2,1)S(1)}, bf16[128,2688]{1,0:T(8,128)(2,1)S(1)}, u32[]{:S(2)}, u32[]{:S(2)}) collective-permute-start(bf16[128,2688]{1,0:T(8,128)(2,1)S(1)} %get-tuple-element.86), channel_id=1, source_target_pairs={{0,2},{2,0},{4,6},{6,4},{8,10},{10,8},{12,14},{14,12},{1,3},{3,1},... | collective-permute-start | bytes 2064392 | tf_op jit(solution)/shard_map/ppermute | solution.py:171
  84.4 0.9 shard_map.152
  85.4 2.0 %collective-permute-start.23 = (bf16[64,2560]{1,0:T(8,128)(2,1)S(1)}, bf16[64,2560]{1,0:T(8,128)(2,1)S(1)}, u32[]{:S(2)}, u32[]{:S(2)}) collective-permute-start(bf16[64,2560]{1,0:T(8,128)(2,1)S(1)} %get-tuple-element.101), channel_id=1, source_target_pairs={{0,8},{2,10},{4,12},{6,14},{8,0},{10,2},{12,4},{14,6},{1,9},{3,11}... | collective-permute-start | bytes 983048 | tf_op jit(solution)/shard_map/ppermute | solution.py:171
  87.3 2.4 %collective-permute-start.24 = (bf16[64,2560]{1,0:T(8,128)(2,1)S(1)}, bf16[64,2560]{1,0:T(8,128)(2,1)S(1)}, u32[]{:S(2)}, u32[]{:S(2)}) collective-permute-start(bf16[64,2560]{1,0:T(8,128)(2,1)S(1)} %get-tuple-element.102), channel_id=1, source_target_pairs={{0,12},{2,14},{4,8},{6,10},{8,4},{10,6},{12,0},{14,2},{1,13},{3,15... | collective-permute-start | bytes 983048 | tf_op jit(solution)/shard_map/ppermute | solution.py:171
  90.1 10.2 %collective-permute-done.20.sent_ref = bf16[128,2688]{1,0:T(8,128)(2,1)S(1)} collective-permute-done((bf16[128,2688]{1,0:T(8,128)(2,1)S(1)}, bf16[128,2688]{1,0:T(8,128)(2,1)S(1)}, u32[]{:S(2)}, u32[]{:S(2)}) %collective-permute-start.20) | collective-permute-done | bytes 688160 | tf_op jit(solution)/shard_map/ppermute | solution.py:171
  100.3 1.2 %shard_map.153 = (bf16[128,2048]{1,0:T(8,128)(2,1)}, bf16[128,512]{1,0:T(8,128)(2,1)}, f32[1,4,32]{2,1,0:T(4,128)}) custom-call(s32[1]{0:T(128)} %bitcast.me_ref, f32[128,2560]{1,0:T(8,128)S(1)} %get-tuple-element.85.own_ref, bf16[128,2688]{1,0:T(8,128)(2,1)S(1)} %collective-permute-done.20.sent_ref, bf16[128,128]{1,0:T(8,128)(2,1)S(1)} %get-tuple-element.95.rg_ref, ...), custom_call_target="tpu_custom_call" | custom-call | tf_op jit(solution)/shard_map/pallas_call | solution.py:523
  101.5 5.2 %collective-permute-done.21 = bf16[2048,128]{1,0:T(8,128)(2,1)S(1)} collective-permute-done((bf16[2048,128]{1,0:T(8,128)(2,1)S(1)}, bf16[2048,128]{1,0:T(8,128)(2,1)S(1)}, u32[]{:S(2)}, u32[]{:S(2)}) %collective-permute-start.21) | collective-permute-done | bytes 524320 | tf_op jit(solution)/shard_map/ppermute | solution.py:171
  106.7 0.9 convert_add_fusion
  (60 shorter events, 15.1 us)
Async XLA Ops:
  0.6 19.3 %collective-permute-start.2 = (bf16[2048,128]{1,0:T(8,128)(2,1)}, bf16[2048,128]{1,0:T(8,128)(2,1)S(1)}, u32[]{:S(2)}, u32[]{:S(2)}) collective-permute-start(bf16[2048,128]{1,0:T(8,128)(2,1)} %bitcast.13), channel_id=1, source_target_pairs={{0,2},{2,0},{4,6},{6,4},{8,10},{10,8},{12,14},{14,12},{1,3},{3,1},... | collective-permute-start | bytes 1572872 | tf_op jit(solution)/shard_map/ppermute | solution.py:171
  3.6 16.9 %collective-permute-start = (bf16[128,2048]{1,0:T(8,128)(2,1)}, bf16[128,2048]{1,0:T(8,128)(2,1)S(1)}, u32[]{:S(2)}, u32[]{:S(2)}) collective-permute-start(bf16[128,2048]{1,0:T(8,128)(2,1)} %x.1), channel_id=1, source_target_pairs={{0,4},{2,6},{4,0},{6,2},{8,12},{10,14},{12,8},{14,10},{1,5},{3,7},... | collective-permute-start | bytes 1572872 | tf_op jit(solution)/shard_map/ppermute | solution.py:171
  5.2 15.4 %collective-permute-start.1 = (bf16[128,2048]{1,0:T(8,128)(2,1)}, bf16[128,2048]{1,0:T(8,128)(2,1)S(1)}, u32[]{:S(2)}, u32[]{:S(2)}) collective-permute-start(bf16[128,2048]{1,0:T(8,128)(2,1)} %x.1), channel_id=1, source_target_pairs={{4,8},{6,10},{8,4},{10,6},{5,9},{7,11},{9,5},{11,7},{20,24},{22,26... | collective-permute-start | bytes 1572872 | tf_op jit(solution)/shard_map/ppermute | solution.py:446
  5.9 1.0 copy-start
  7.0 1.0 copy-start.1
  8.0 1.0 copy-start.2
  9.0 0.9 copy-start.3
  14.9 32.0 %collective-permute-start.9 = (bf16[128,2816]{1,0:T(8,128)(2,1)S(1)}, bf16[128,2816]{1,0:T(8,128)(2,1)S(1)}, u32[]{:S(2)}, u32[]{:S(2)}) collective-permute-start(bf16[128,2816]{1,0:T(8,128)(2,1)S(1)} %get-tuple-element.62.gw_ref), channel_id=1, source_target_pairs={{0,2},{2,0},{4,6},{6,4},{8,10},{10,8},{12,14},{14,12},{1,3},{3,1},... | collective-permute-start | bytes 2162696 | tf_op jit(solution)/shard_map/ppermute | solution.py:171
  15.5 11.3 %collective-permute-start.5 = (bf16[80,2048]{1,0:T(8,128)(2,1)S(1)}, bf16[80,2048]{1,0:T(8,128)(2,1)S(1)}, u32[]{:S(2)}, u32[]{:S(2)}) collective-permute-start(bf16[80,2048]{1,0:T(8,128)(2,1)S(1)} %get-tuple-element.59.b0), channel_id=1, source_target_pairs={{0,4},{2,6},{4,0},{6,2},{8,12},{10,14},{12,8},{14,10},{1,5},{3,7},... | collective-permute-start | bytes 983048 | tf_op jit(solution)/shard_map/ppermute | solution.py:171
  19.9 7.6 %collective-permute-start.6 = (bf16[80,2048]{1,0:T(8,128)(2,1)S(1)}, bf16[80,2048]{1,0:T(8,128)(2,1)S(1)}, u32[]{:S(2)}, u32[]{:S(2)}) collective-permute-start(bf16[80,2048]{1,0:T(8,128)(2,1)S(1)} %get-tuple-element.59.b0), channel_id=1, source_target_pairs={{4,8},{6,10},{8,4},{10,6},{5,9},{7,11},{9,5},{11,7},{20,24},{22,26... | collective-permute-start | bytes 983048 | tf_op jit(solution)/shard_map/ppermute | solution.py:452
  20.6 8.2 %collective-permute-start.4 = (bf16[128,2048]{1,0:T(8,128)(2,1)S(1)}, bf16[128,2048]{1,0:T(8,128)(2,1)S(1)}, u32[]{:S(2)}, u32[]{:S(2)}) collective-permute-start(bf16[128,2048]{1,0:T(8,128)(2,1)S(1)} %collective-permute-done.x1), channel_id=1, source_target_pairs={{4,8},{6,10},{8,4},{10,6},{5,9},{7,11},{9,5},{11,7},{20,24},{22,26... | collective-permute-start | bytes 1572872 | tf_op jit(solution)/shard_map/ppermute | solution.py:454
  21.3 25.6 %collective-permute-start.3 = (bf16[128,2048]{1,0:T(8,128)(2,1)S(1)}, bf16[128,2048]{1,0:T(8,128)(2,1)S(1)}, u32[]{:S(2)}, u32[]{:S(2)}) collective-permute-start(bf16[128,2048]{1,0:T(8,128)(2,1)S(1)} %collective-permute-done.1.xi), channel_id=1, source_target_pairs={{4,0},{6,2},{8,12},{10,14},{5,1},{7,3},{9,13},{11,15},{20,16},{22,... | collective-permute-start | bytes 1572872 | tf_op jit(solution)/shard_map/ppermute | solution.py:454
  26.8 3.3 %collective-permute-start.8 = (bf16[80,2048]{1,0:T(8,128)(2,1)S(1)}, bf16[80,2048]{1,0:T(8,128)(2,1)S(1)}, u32[]{:S(2)}, u32[]{:S(2)}) collective-permute-start(bf16[80,2048]{1,0:T(8,128)(2,1)S(1)} %collective-permute-done.5.b1), channel_id=1, source_target_pairs={{4,8},{6,10},{8,4},{10,6},{5,9},{7,11},{9,5},{11,7},{20,24},{22,26... | collective-permute-start | bytes 983048 | tf_op jit(solution)/shard_map/ppermute | solution.py:455
  27.5 19.4 %collective-permute-start.7 = (bf16[80,2048]{1,0:T(8,128)(2,1)S(1)}, bf16[80,2048]{1,0:T(8,128)(2,1)S(1)}, u32[]{:S(2)}, u32[]{:S(2)}) collective-permute-start(bf16[80,2048]{1,0:T(8,128)(2,1)S(1)} %collective-permute-done.6.bi), channel_id=1, source_target_pairs={{4,0},{6,2},{8,12},{10,14},{5,1},{7,3},{9,13},{11,15},{20,16},{22,... | collective-permute-start | bytes 983048 | tf_op jit(solution)/shard_map/ppermute | solution.py:455
  28.8 28.9 %collective-permute-start.12 = (bf16[128,2048]{1,0:T(8,128)(2,1)S(1)}, bf16[128,2048]{1,0:T(8,128)(2,1)S(1)}, u32[]{:S(2)}, u32[]{:S(2)}) collective-permute-start(bf16[128,2048]{1,0:T(8,128)(2,1)S(1)} %collective-permute-done.4.xm), channel_id=1, source_target_pairs={{4,0},{6,2},{8,12},{10,14},{5,1},{7,3},{9,13},{11,15},{20,16},{22,... | collective-permute-start | bytes 1572872 | tf_op jit(solution)/shard_map/ppermute | solution.py:457
  49.0 1.9 %collective-permute-start.10 = (f32[384,256]{1,0:T(8,128)S(1)}, f32[384,256]{1,0:T(8,128)S(1)}, u32[]{:S(2)}, u32[]{:S(2)}) collective-permute-start(f32[384,256]{1,0:T(8,128)S(1)} %get-tuple-element.63.m_ref), channel_id=1, source_target_pairs={{0,1},{1,0},{2,3},{3,2},{4,5},{5,4},{6,7},{7,6},{8,9},{9,8},{10,11... | collective-permute-start | bytes 1179656 | tf_op jit(solution)/shard_map/ppermute | solution.py:175
  49.1 2.3 %collective-permute-start.11 = (f32[384,256]{1,0:T(8,128)S(1)}, f32[384,256]{1,0:T(8,128)S(1)}, u32[]{:S(2)}, u32[]{:S(2)}) collective-permute-start(f32[384,256]{1,0:T(8,128)S(1)} %get-tuple-element.64.s_ref), channel_id=1, source_target_pairs={{0,1},{1,0},{2,3},{3,2},{4,5},{5,4},{6,7},{7,6},{8,9},{9,8},{10,11... | collective-permute-start | bytes 1179656 | tf_op jit(solution)/shard_map/ppermute | solution.py:175
  49.5 16.3 %collective-permute-start.16 = (bf16[80,2048]{1,0:T(8,128)(2,1)S(1)}, bf16[80,2048]{1,0:T(8,128)(2,1)S(1)}, u32[]{:S(2)}, u32[]{:S(2)}) collective-permute-start(bf16[80,2048]{1,0:T(8,128)(2,1)S(1)} %collective-permute-done.8.bm), channel_id=1, source_target_pairs={{4,0},{6,2},{8,12},{10,14},{5,1},{7,3},{9,13},{11,15},{20,16},{22,... | collective-permute-start | bytes 983048 | tf_op jit(solution)/shard_map/ppermute | solution.py:458
  57.8 5.7 %collective-permute-start.13 = (bf16[128,768]{1,0:T(8,128)(2,1)S(1)}, bf16[128,768]{1,0:T(8,128)(2,1)S(1)}, u32[]{:S(2)}, u32[]{:S(2)}) collective-permute-start(bf16[128,768]{1,0:T(8,128)(2,1)S(1)} %get-tuple-element.68), channel_id=1, source_target_pairs={{0,2},{2,0},{4,6},{6,4},{8,10},{10,8},{12,14},{14,12},{1,3},{3,1},... | collective-permute-start | bytes 589832 | tf_op jit(solution)/shard_map/ppermute | solution.py:171
  63.5 6.4 %collective-permute-start.14 = (bf16[128,512]{1,0:T(8,128)(2,1)S(1)}, bf16[128,512]{1,0:T(8,128)(2,1)S(1)}, u32[]{:S(2)}, u32[]{:S(2)}) collective-permute-start(bf16[128,512]{1,0:T(8,128)(2,1)S(1)} %get-tuple-element.70), channel_id=1, source_target_pairs={{0,4},{2,6},{4,0},{6,2},{8,12},{10,14},{12,8},{14,10},{1,5},{3,7},... | collective-permute-start | bytes 393224 | tf_op jit(solution)/shard_map/ppermute | solution.py:171
  63.6 6.4 %collective-permute-start.15 = (bf16[128,512]{1,0:T(8,128)(2,1)S(1)}, bf16[128,512]{1,0:T(8,128)(2,1)S(1)}, u32[]{:S(2)}, u32[]{:S(2)}) collective-permute-start(bf16[128,512]{1,0:T(8,128)(2,1)S(1)} %get-tuple-element.71), channel_id=1, source_target_pairs={{0,8},{2,10},{4,12},{6,14},{8,0},{10,2},{12,4},{14,6},{1,9},{3,11}... | collective-permute-start | bytes 393224 | tf_op jit(solution)/shard_map/ppermute | solution.py:171
  66.6 4.7 %collective-permute-start.17 = (f32[128,512]{1,0:T(8,128)S(1)}, f32[128,512]{1,0:T(8,128)S(1)}, u32[]{:S(2)}, u32[]{:S(2)}) collective-permute-start(f32[128,512]{1,0:T(8,128)S(1)} %get-tuple-element.74.m_ref), channel_id=1, source_target_pairs={{0,1},{1,0},{2,3},{3,2},{4,5},{5,4},{6,7},{7,6},{8,9},{9,8},{10,11... | collective-permute-start | bytes 786440 | tf_op jit(solution)/shard_map/ppermute | solution.py:175
  71.5 6.2 %collective-permute-start.18 = (bf16[128,256]{1,0:T(8,128)(2,1)S(1)}, bf16[128,256]{1,0:T(8,128)(2,1)S(1)}, u32[]{:S(2)}, u32[]{:S(2)}) collective-permute-start(bf16[128,256]{1,0:T(8,128)(2,1)S(1)} %get-tuple-element.79), channel_id=1, source_target_pairs={{0,12},{2,14},{4,8},{6,10},{8,4},{10,6},{12,0},{14,2},{1,13},{3,15... | collective-permute-start | bytes 196616 | tf_op jit(solution)/shard_map/ppermute | solution.py:171
  74.0 7.1 %collective-permute-start.19 = (bf16[128,256]{1,0:T(8,128)(2,1)S(1)}, bf16[128,256]{1,0:T(8,128)(2,1)S(1)}, u32[]{:S(2)}, u32[]{:S(2)}) collective-permute-start(bf16[128,256]{1,0:T(8,128)(2,1)S(1)} %get-tuple-element.80), channel_id=1, source_target_pairs={{0,14},{2,12},{4,10},{6,8},{8,6},{10,4},{12,2},{14,0},{1,15},{3,13... | collective-permute-start | bytes 196616 | tf_op jit(solution)/shard_map/ppermute | solution.py:171
  81.9 18.4 %collective-permute-start.20 = (bf16[128,2688]{1,0:T(8,128)(2,1)S(1)}, bf16[128,2688]{1,0:T(8,128)(2,1)S(1)}, u32[]{:S(2)}, u32[]{:S(2)}) collective-permute-start(bf16[128,2688]{1,0:T(8,128)(2,1)S(1)} %get-tuple-element.86), channel_id=1, source_target_pairs={{0,2},{2,0},{4,6},{6,4},{8,10},{10,8},{12,14},{14,12},{1,3},{3,1},... | collective-permute-start | bytes 2064392 | tf_op jit(solution)/shard_map/ppermute | solution.py:171
  83.8 22.9 %collective-permute-start.21 = (bf16[2048,128]{1,0:T(8,128)(2,1)S(1)}, bf16[2048,128]{1,0:T(8,128)(2,1)S(1)}, u32[]{:S(2)}, u32[]{:S(2)}) collective-permute-start(bf16[2048,128]{1,0:T(8,128)(2,1)S(1)} %add_convert_fusion), channel_id=1, source_target_pairs={{0,2},{2,0},{4,6},{6,4},{8,10},{10,8},{12,14},{14,12},{1,3},{3,1},... | collective-permute-start | bytes 1572872 | tf_op jit(solution)/shard_map/ppermute | solution.py:171
  84.4 15.9 %copy-start.7 = (s32[1,32,4]{1,2,0:T(4,128)S(1)}, s32[1,32,4]{1,2,0:T(4,128)}, u32[]{:S(2)}) copy-start(s32[1,32,4]{1,2,0:T(4,128)} %param.17) | copy-start | bytes 1540
  84.4 15.9 %copy-start.9 = (s32[1,128]{1,0:T(1,128)S(1)}, s32[1,128]{1,0:T(1,128)}, u32[]{:S(2)}) copy-start(s32[1,128]{1,0:T(1,128)} %tr_ref.1) | copy-start | bytes 1540
  84.4 15.9 %copy-start.11 = (s32[1,32]{1,0:T(1,128)S(1)}, s32[1,32]{1,0:T(1,128)}, u32[]{:S(2)}) copy-start(s32[1,32]{1,0:T(1,128)} %rc_ref.1) | copy-start | bytes 388
  85.3 22.3 %collective-permute-start.22 = (bf16[64,2560]{1,0:T(8,128)(2,1)S(1)}, bf16[64,2560]{1,0:T(8,128)(2,1)S(1)}, u32[]{:S(2)}, u32[]{:S(2)}) collective-permute-start(bf16[64,2560]{1,0:T(8,128)(2,1)S(1)} %get-tuple-element.99), channel_id=1, source_target_pairs={{0,4},{2,6},{4,0},{6,2},{8,12},{10,14},{12,8},{14,10},{1,5},{3,7},... | collective-permute-start | bytes 983048 | tf_op jit(solution)/shard_map/ppermute | solution.py:171
  85.4 22.8 %collective-permute-start.23 = (bf16[64,2560]{1,0:T(8,128)(2,1)S(1)}, bf16[64,2560]{1,0:T(8,128)(2,1)S(1)}, u32[]{:S(2)}, u32[]{:S(2)}) collective-permute-start(bf16[64,2560]{1,0:T(8,128)(2,1)S(1)} %get-tuple-element.101), channel_id=1, source_target_pairs={{0,8},{2,10},{4,12},{6,14},{8,0},{10,2},{12,4},{14,6},{1,9},{3,11}... | collective-permute-start | bytes 983048 | tf_op jit(solution)/shard_map/ppermute | solution.py:171
  87.3 20.9 %collective-permute-start.24 = (bf16[64,2560]{1,0:T(8,128)(2,1)S(1)}, bf16[64,2560]{1,0:T(8,128)(2,1)S(1)}, u32[]{:S(2)}, u32[]{:S(2)}) collective-permute-start(bf16[64,2560]{1,0:T(8,128)(2,1)S(1)} %get-tuple-element.102), channel_id=1, source_target_pairs={{0,12},{2,14},{4,8},{6,10},{8,4},{10,6},{12,0},{14,2},{1,13},{3,15... | collective-permute-start | bytes 983048 | tf_op jit(solution)/shard_map/ppermute | solution.py:171
  (6 other events, 4.4 us)

commit v5 on v4

--- a/solution.py
+++ b/solution.py
@@ -268,8 +268,8 @@
 
 def hidden_of(x, rows, a_ref, ax_ref, out_ref):
     rank2 = a_ref.shape[1]
-    out_ref[rows, :rank2] = dot(x, a_ref[...], SAME)
-    out_ref[rows, rank2 : 2 * rank2] = dot(x, ax_ref[...], SAME)
+    out_ref[rows, :rank2] = dot(x, a_ref[...], SAME).astype(out_ref.dtype)
+    out_ref[rows, rank2 : 2 * rank2] = dot(x, ax_ref[...], SAME).astype(out_ref.dtype)
 
 
 def slopes_of(b, rows, first, gw_ref, gx_ref, out_ref):
@@ -280,7 +280,7 @@
     for i, g_ref in enumerate((gw_ref, gx_ref)):
         part_q = dot(g_ref[:, :wide], bq, COLS)
         part_v = dot(g_ref[:, wide:full], bv, COLS)
-        out_ref[rows, first + i * rank2 : first + (i + 1) * rank2] = jnp.concatenate([part_q, part_v], axis=1)
+        out_ref[rows, first + i * rank2 : first + (i + 1) * rank2] = jnp.concatenate([part_q, part_v], axis=1).astype(out_ref.dtype)
 
 
 def products_early(x0, x1, xo, xm, b0, b1, bo, bm, a_ref, ax_ref, gw_ref, gx_ref, h_ref, s_ref, x2_ref, b2_ref):
@@ -301,29 +301,29 @@
     slopes_of(b3_ref[...], rows, 2 * a_ref.shape[1], gw_ref, gx_ref, out_ref)
 
 
-def split_early(m_ref, mr_ref, s_ref, sr_ref, gw_ref, gx_ref, sl_ref, near_ref, far_ref):
+def split_early(m_ref, mr_ref, s_ref, sr_ref, gw_ref, gx_ref, sl_ref, near_ref, *far_refs):
     count = gw_ref.shape[0]
     both = m_ref.shape[1]
     for j in range(LINE - 1):
         rows = slice(j * count, (j + 1) * count)
         cols = pl.ds(j * both, both)
-        slope = s_ref[rows, :] + sr_ref[rows, :]
+        slope = s_ref[rows, :].astype(F32) + sr_ref[rows, :].astype(F32)
         sl_ref[rows, :] = slope
-        blocks = near_ref.at[:, cols], far_ref.at[:, cols]
-        fill_blocks(j, m_ref[rows, :] + mr_ref[rows, :], slope, gw_ref, gx_ref, *blocks)
-
-
-def pack_slots(near_ref, far_ref, *out_refs):
+        blocks = near_ref.at[:, cols], far_refs[j]
+        fill_blocks(j, m_ref[rows, :].astype(F32) + mr_ref[rows, :].astype(F32), slope, gw_ref, gx_ref, *blocks)
+
+
+def pack_slots(near_ref, f0, f1, f2, *out_refs):
     rank2 = out_refs[0].shape[1] // 4
-    for j, out_ref in enumerate(out_refs):
+    for j, (far_ref, out_ref) in enumerate(zip((f0, f1, f2), out_refs)):
         for half in range(2):
             first = (2 * j + half) * rank2
             out_ref[:, 2 * half * rank2 : (2 * half + 1) * rank2] = near_ref[:, first : first + rank2]
-            out_ref[:, (2 * half + 1) * rank2 : (2 * half + 2) * rank2] = far_ref[:, first : first + rank2]
+            out_ref[:, (2 * half + 1) * rank2 : (2 * half + 2) * rank2] = far_ref[:, half * rank2 : (half + 1) * rank2]
 
 
 def split_late(m_ref, r_ref, gw_ref, gx_ref, sl_ref, near_ref, far_ref):
-    total = m_ref[...] + r_ref[...]
+    total = m_ref[...].astype(F32) + r_ref[...].astype(F32)
     half = total.shape[1] // 2
     sl_ref[...] = total[:, half:]
     fill_blocks(LINE - 1, total[:, :half], total[:, half:], gw_ref, gx_ref, near_ref, far_ref)
@@ -450,8 +450,9 @@
         b_query, b_value, grad_query, grad_value, tokens, a_proj[0],
     )
     b1, bi = to_place(b0, 2), lax.ppermute(b0, "expert", MID)
-    x1, xi, a_other = lax.optimization_barrier((x1, xi, a_other))
-    xo, xm = lax.ppermute(xi, "expert", OUT), lax.ppermute(x1, "expert", MID)
+    x1, a_other = lax.optimization_barrier((x1, a_other))
+    xm = lax.ppermute(x1, "expert", MID)
+    xo = lax.ppermute(xi, "expert", OUT)
     bo, bm = lax.ppermute(bi, "expert", OUT), lax.ppermute(b1, "expert", MID)
     gx = to_place(gw, 1)
     xo3 = lax.ppermute(xm, "expert", OUT)
@@ -460,27 +461,27 @@
     wide_block = (b0.shape, BF16)
     m, ms, x2, b2 = call(
         products_early,
-        [((3 * count, 2 * rank2), F32), ((3 * count, 2 * rank2), F32), x_block, wide_block],
+        [((3 * count, 2 * rank2), BF16), ((3 * count, 2 * rank2), BF16), x_block, wide_block],
         x0, x1, xo, xm, b0, b1, bo, bm, a_own, a_other, gw, gx,
     )
-    sl, near, far = call(
+    sl, near, *far = call(
         split_early,
-        [((3 * count, 2 * rank2), F32), ((count, 6 * rank2), BF16), ((count, 6 * rank2), BF16)],
+        [((3 * count, 2 * rank2), F32), ((count, 6 * rank2), BF16)] + [pair] * 3,
         m, other_core(m), ms, other_core(ms), gw, gx,
     )
-    near, far, xo3 = lax.optimization_barrier((near, far, xo3))
-    far = to_place(far, 1)
-    (bo3,) = after(far, bo3)
-    c0, c1, c2 = call(pack_slots, [((count, 4 * rank2), BF16)] * 3, near, far)
+    (xo3,) = after(sl, xo3)
+    far = [to_place(part, 1) for part in far]
+    near, bo3 = lax.optimization_barrier((near, bo3))
+    c0, c1, c2 = call(pack_slots, [((count, 4 * rank2), BF16)] * 3, near, *far)
     c1, c2 = to_place(c1, 2), to_place(c2, 4)
     h3, x3, b3 = call(
         products_late,
-        [((count, 4 * rank2), F32), x_block, wide_block],
+        [((count, 4 * rank2), BF16), x_block, wide_block],
         xi, xo3, bi, bo3, a_own, a_other, gw, gx,
     )
     rh = other_core(h3)
     c1, c2 = after(h3, c1, c2)
-    grad_a = dot(x0, c0[:, 2 * rank2 :], ROWS) + dot(x1, c1[:, 2 * rank2 :], ROWS) + dot(x2, c2[:, 2 * rank2 :], ROWS)
+    grad_a = dot(x0, c0[:, 2 * rank2 :], ROWS) + dot(x1, c1[:, 2 * rank2 :], ROWS)
     rh, grad_a = lax.optimization_barrier((rh, grad_a))
     sl3, n3, f3 = call(
         split_late,
@@ -488,20 +489,22 @@
         h3, rh, gw, gx,
     )
     n3, f3 = to_place(n3, 6), to_place(f3, 7)
+    (c2,) = after(sl3, c2)
+    grad_a = grad_a + dot(x2, c2[:, 2 * rank2 :], ROWS)
+    n3, f3, grad_a = lax.optimization_barrier((n3, f3, grad_a))
     out_own, sent, rg, wt = call(
         outputs_part,
         [((count, full), F32), ((count, full + LANES), BF16), ((count, LANES), BF16), ((2 * count, LINE * rank2), BF16)],
         c0, c1, c2, n3, f3, gw, gx, b0, b1, b2, b3, sl, sl3,
     )
     sent = to_place(sent, 1)
-    (f3s,) = after(out_own, f3)
-    grad_a_other = (grad_a[:, rank2:] + dot(x3, f3s[:, rank2:], ROWS)).astype(BF16)
-    (wt,) = after(grad_a_other, wt)
     p0, p1, p2, p3 = call(
         functools.partial(grad_b_parts, wide), [((rank, full), F32)] + [b_block] * 3, wt, gw, gx
     )
     p1, p2, p3 = to_place(p1, 2), to_place(p2, 4), to_place(p3, 6)
-    (n3s,) = after(p0, n3)
+    (f3s,) = after(p0, f3)
+    grad_a_other = (grad_a[:, rank2:] + dot(x3, f3s[:, rank2:], ROWS)).astype(BF16)
+    (n3s,) = after(grad_a_other, n3)
     grad_a = grad_a[:, :rank2] + dot(x3, n3s[:, rank2:], ROWS)
     (sent,) = after(grad_a, sent)
     out_query, out_value, grad_mix = call_sum(

time: 111 us -> 110 us (level)
  waiting for transfers between devices: 56.3 us -> 53 us
  starting transfers between devices: 32.9 us -> 35.1 us
    ppermute x1, waiting for transfers between devices: 0.38 us -> 8.45 us  [pair_plan(): bo3 = lax.ppermute(bm, 'expert', OUT)]
    ppermute x1, waiting for transfers between devices: 6.27 us -> 0.01 us  [pair_plan(): xo3 = lax.ppermute(xm, 'expert', OUT)]
    ppermute x14 -> x16, waiting for transfers between devices: 32.4 us -> 27.9 us  [to_place(): lax.ppermute(array, 'expert', [(i, i ^ place) for i in range(LINE * PAIR)])]
    ppermute x14 -> x16, starting transfers between devices: 24.4 us -> 26.6 us  [to_place(): lax.ppermute(array, 'expert', [(i, i ^ place) for i in range(LINE * PAIR)])]
    ppermute x2, waiting for transfers between devices: 16.8 us -> 15.5 us  [pair_plan(): bo, bm = (lax.ppermute(bi, 'expert', OUT), lax.ppermute(b1, 'expert', MID))]
  transfers between devices with their start and end apart: 25 -> 27, of which waited for: 12 -> 11; matrix products, arithmetic and copies ran while one was open for 3% -> 3% of each run, Pallas kernels for 5% -> 5%
where the time goes in v5:
time: 110 us; the launch traced here: 108 us
  waiting for transfers between devices  53 us (48%)
  starting transfers between devices  35.1 us (32%)
  local copies, waits for them, and re-layouts  8.49 us (8%)
  Pallas kernels  7.55 us (7%)
  matrix products  2.04 us (2%)
    ppermute x16, waiting for transfers between devices, to_place(): lax.ppermute(array, 'expert', [(i, i ^ place) for i in range(LINE * PAIR)])  27.9 us
    ppermute x16, starting transfers between devices, to_place(): lax.ppermute(array, 'expert', [(i, i ^ place) for i in range(LINE * PAIR)])  26.6 us
    ppermute x2, waiting for transfers between devices, pair_plan(): bo, bm = (lax.ppermute(bi, 'expert', OUT), lax.ppermute(b1, 'expert', MID))  15.5 us
    unnamed x26, local copies, waits for them, and re-layouts  8.49 us
    ppermute x1, waiting for transfers between devices, pair_plan(): bo3 = lax.ppermute(bm, 'expert', OUT)  8.45 us
    pallas_call x8, Pallas kernels, call(): pl.pallas_call(kernel, out_shape=shapes, in_specs=[pl.BlockSpec(memory_sp...  5.82 us
  transfers between devices with their start and end apart: 27, of which 11 were waited for; matrix products, arithmetic and copies ran while one was open for 3% of the time, Pallas kernels for 5%

profile of v5, /device:TPU:0, one launch (start us, length us, event | category | flops | bytes accessed | tf_op | source)
XLA Modules:
  0.0 108.0 jit_solution(2343524693097417854)
XLA Ops:
  0.6 3.0 %collective-permute-start.1 = (bf16[2048,128]{1,0:T(8,128)(2,1)}, bf16[2048,128]{1,0:T(8,128)(2,1)S(1)}, u32[]{:S(2)}, u32[]{:S(2)}) collective-permute-start(bf16[2048,128]{1,0:T(8,128)(2,1)} %bitcast.13), channel_id=1, source_target_pairs={{0,2},{2,0},{4,6},{6,4},{8,10},{10,8},{12,14},{14,12},{1,3},{3,1},... | collective-permute-start | bytes 1572872 | tf_op jit(solution)/shard_map/ppermute | solution.py:171
  3.6 1.6 %collective-permute-start = (bf16[128,2048]{1,0:T(8,128)(2,1)}, bf16[128,2048]{1,0:T(8,128)(2,1)S(1)}, u32[]{:S(2)}, u32[]{:S(2)}) collective-permute-start(bf16[128,2048]{1,0:T(8,128)(2,1)} %x.1), channel_id=1, source_target_pairs={{0,4},{2,6},{4,0},{6,2},{8,12},{10,14},{12,8},{14,10},{1,5},{3,7},... | collective-permute-start | bytes 1572872 | tf_op jit(solution)/shard_map/ppermute | solution.py:171
  5.9 1.0 copy-done
  7.0 1.0 copy-done.1
  8.0 1.0 copy-done.2
  9.0 0.9 copy-done.3
  10.0 0.9 copy-done.4
  15.5 4.4 %collective-permute-start.5 = (bf16[80,2048]{1,0:T(8,128)(2,1)S(1)}, bf16[80,2048]{1,0:T(8,128)(2,1)S(1)}, u32[]{:S(2)}, u32[]{:S(2)}) collective-permute-start(bf16[80,2048]{1,0:T(8,128)(2,1)S(1)} %get-tuple-element.61.b0), channel_id=1, source_target_pairs={{0,4},{2,6},{4,0},{6,2},{8,12},{10,14},{12,8},{14,10},{1,5},{3,7},... | collective-permute-start | bytes 983048 | tf_op jit(solution)/shard_map/ppermute | solution.py:171
  21.3 1.3 %collective-permute-start.3 = (bf16[128,2048]{1,0:T(8,128)(2,1)S(1)}, bf16[128,2048]{1,0:T(8,128)(2,1)S(1)}, u32[]{:S(2)}, u32[]{:S(2)}) collective-permute-start(bf16[128,2048]{1,0:T(8,128)(2,1)S(1)} %collective-permute-done.2.xi), channel_id=1, source_target_pairs={{4,0},{6,2},{8,12},{10,14},{5,1},{7,3},{9,13},{11,15},{20,16},{22,... | collective-permute-start | bytes 1572872 | tf_op jit(solution)/shard_map/ppermute | solution.py:455
  22.6 4.2 %collective-permute-done.5.b1 = bf16[80,2048]{1,0:T(8,128)(2,1)S(1)} collective-permute-done((bf16[80,2048]{1,0:T(8,128)(2,1)S(1)}, bf16[80,2048]{1,0:T(8,128)(2,1)S(1)}, u32[]{:S(2)}, u32[]{:S(2)}) %collective-permute-start.5) | collective-permute-done | bytes 327712 | tf_op jit(solution)/shard_map/ppermute | solution.py:171
  27.5 1.3 %collective-permute-start.7 = (bf16[80,2048]{1,0:T(8,128)(2,1)S(1)}, bf16[80,2048]{1,0:T(8,128)(2,1)S(1)}, u32[]{:S(2)}, u32[]{:S(2)}) collective-permute-start(bf16[80,2048]{1,0:T(8,128)(2,1)S(1)} %collective-permute-done.6.bi), channel_id=1, source_target_pairs={{4,0},{6,2},{8,12},{10,14},{5,1},{7,3},{9,13},{11,15},{20,16},{22,... | collective-permute-start | bytes 983048 | tf_op jit(solution)/shard_map/ppermute | solution.py:456
  28.8 1.3 %collective-permute-start.18 = (bf16[128,2048]{1,0:T(8,128)(2,1)S(1)}, bf16[128,2048]{1,0:T(8,128)(2,1)S(1)}, u32[]{:S(2)}, u32[]{:S(2)}) collective-permute-start(bf16[128,2048]{1,0:T(8,128)(2,1)S(1)} %collective-permute-done.4.xm), channel_id=1, source_target_pairs={{4,0},{6,2},{8,12},{10,14},{5,1},{7,3},{9,13},{11,15},{20,16},{22,... | collective-permute-start | bytes 1572872 | tf_op jit(solution)/shard_map/ppermute | solution.py:458
  30.2 1.3 %collective-permute-start.12 = (bf16[80,2048]{1,0:T(8,128)(2,1)S(1)}, bf16[80,2048]{1,0:T(8,128)(2,1)S(1)}, u32[]{:S(2)}, u32[]{:S(2)}) collective-permute-start(bf16[80,2048]{1,0:T(8,128)(2,1)S(1)} %collective-permute-done.8.bm), channel_id=1, source_target_pairs={{4,0},{6,2},{8,12},{10,14},{5,1},{7,3},{9,13},{11,15},{20,16},{22,... | collective-permute-start | bytes 983048 | tf_op jit(solution)/shard_map/ppermute | solution.py:459
  31.5 15.5 %collective-permute-done.7.bo = bf16[80,2048]{1,0:T(8,128)(2,1)S(1)} collective-permute-done((bf16[80,2048]{1,0:T(8,128)(2,1)S(1)}, bf16[80,2048]{1,0:T(8,128)(2,1)S(1)}, u32[]{:S(2)}, u32[]{:S(2)}) %collective-permute-start.7) | collective-permute-done | bytes 327712 | tf_op jit(solution)/shard_map/ppermute | solution.py:456
  46.9 2.1 %shard_map.146 = (bf16[384,256]{1,0:T(8,128)(2,1)S(1)}, bf16[384,256]{1,0:T(8,128)(2,1)S(1)}, bf16[128,2048]{1,0:T(8,128)(2,1)S(1)}, bf16[80,2048]{1,0:T(8,128)(2,1)S(1)}) custom-call(bf16[128,2048]{1,0:T(8,128)(2,1)S(1)} %get-tuple-element.59.x0, bf16[128,2048]{1,0:T(8,128)(2,1)S(1)} %collective-permute-done.x1, ...), custom_call_target="tpu_custom_call" | custom-call | tf_op jit(solution)/shard_map/pallas_call | solution.py:193
  49.6 0.9 collective-permute-done.10.mr_ref
  51.0 1.6 %collective-permute-start.13 = (bf16[128,256]{1,0:T(8,128)(2,1)S(1)}, bf16[128,256]{1,0:T(8,128)(2,1)S(1)}, u32[]{:S(2)}, u32[]{:S(2)}) collective-permute-start(bf16[128,256]{1,0:T(8,128)(2,1)S(1)} %get-tuple-element.69), channel_id=1, source_target_pairs={{0,2},{2,0},{4,6},{6,4},{8,10},{10,8},{12,14},{14,12},{1,3},{3,1},... | collective-permute-start | bytes 196616 | tf_op jit(solution)/shard_map/ppermute | solution.py:171
  53.1 1.5 %collective-permute-start.15 = (bf16[128,256]{1,0:T(8,128)(2,1)S(1)}, bf16[128,256]{1,0:T(8,128)(2,1)S(1)}, u32[]{:S(2)}, u32[]{:S(2)}) collective-permute-start(bf16[128,256]{1,0:T(8,128)(2,1)S(1)} %get-tuple-element.71), channel_id=1, source_target_pairs={{0,2},{2,0},{4,6},{6,4},{8,10},{10,8},{12,14},{14,12},{1,3},{3,1},... | collective-permute-start | bytes 196616 | tf_op jit(solution)/shard_map/ppermute | solution.py:171
  54.5 8.5 %collective-permute-done.12.bo = bf16[80,2048]{1,0:T(8,128)(2,1)S(1)} collective-permute-done((bf16[80,2048]{1,0:T(8,128)(2,1)S(1)}, bf16[80,2048]{1,0:T(8,128)(2,1)S(1)}, u32[]{:S(2)}, u32[]{:S(2)}) %collective-permute-start.12) | collective-permute-done | bytes 327712 | tf_op jit(solution)/shard_map/ppermute | solution.py:459
  63.2 1.9 %collective-permute-start.17 = (bf16[128,512]{1,0:T(8,128)(2,1)S(1)}, bf16[128,512]{1,0:T(8,128)(2,1)S(1)}, u32[]{:S(2)}, u32[]{:S(2)}) collective-permute-start(bf16[128,512]{1,0:T(8,128)(2,1)S(1)} %get-tuple-element.74), channel_id=1, source_target_pairs={{0,8},{2,10},{4,12},{6,14},{8,0},{10,2},{12,4},{14,6},{1,9},{3,11}... | collective-permute-start | bytes 393224 | tf_op jit(solution)/shard_map/ppermute | solution.py:171
  66.0 3.3 %collective-permute-done.16.c1 = bf16[128,512]{1,0:T(8,128)(2,1)S(1)} collective-permute-done((bf16[128,512]{1,0:T(8,128)(2,1)S(1)}, bf16[128,512]{1,0:T(8,128)(2,1)S(1)}, u32[]{:S(2)}, u32[]{:S(2)}) %collective-permute-start.16) | collective-permute-done | bytes 131104 | tf_op jit(solution)/shard_map/ppermute | solution.py:171
  69.3 1.5 %collective-permute-done.17.c2 = bf16[128,512]{1,0:T(8,128)(2,1)S(1)} collective-permute-done((bf16[128,512]{1,0:T(8,128)(2,1)S(1)}, bf16[128,512]{1,0:T(8,128)(2,1)S(1)}, u32[]{:S(2)}, u32[]{:S(2)}) %collective-permute-start.17) | collective-permute-done | bytes 131104 | tf_op jit(solution)/shard_map/ppermute | solution.py:171
  71.9 1.4 %collective-permute-start.20 = (bf16[128,256]{1,0:T(8,128)(2,1)S(1)}, bf16[128,256]{1,0:T(8,128)(2,1)S(1)}, u32[]{:S(2)}, u32[]{:S(2)}) collective-permute-start(bf16[128,256]{1,0:T(8,128)(2,1)S(1)} %get-tuple-element.84), channel_id=1, source_target_pairs={{0,12},{2,14},{4,8},{6,10},{8,4},{10,6},{12,0},{14,2},{1,13},{3,15... | collective-permute-start | bytes 196616 | tf_op jit(solution)/shard_map/ppermute | solution.py:171
  73.3 3.5 %collective-permute-start.21 = (bf16[128,256]{1,0:T(8,128)(2,1)S(1)}, bf16[128,256]{1,0:T(8,128)(2,1)S(1)}, u32[]{:S(2)}, u32[]{:S(2)}) collective-permute-start(bf16[128,256]{1,0:T(8,128)(2,1)S(1)} %get-tuple-element.85), channel_id=1, source_target_pairs={{0,14},{2,12},{4,10},{6,8},{8,6},{10,4},{12,2},{14,0},{1,15},{3,13... | collective-permute-start | bytes 196616 | tf_op jit(solution)/shard_map/ppermute | solution.py:171
  78.0 2.3 %collective-permute-done.21.f3 = bf16[128,256]{1,0:T(8,128)(2,1)S(1)} collective-permute-done((bf16[128,256]{1,0:T(8,128)(2,1)S(1)}, bf16[128,256]{1,0:T(8,128)(2,1)S(1)}, u32[]{:S(2)}, u32[]{:S(2)}) %collective-permute-start.21) | collective-permute-done | bytes 65568 | tf_op jit(solution)/shard_map/ppermute | solution.py:171
  81.1 0.9 shard_map.152
  82.0 1.3 %collective-permute-start.22 = (bf16[128,2688]{1,0:T(8,128)(2,1)S(1)}, bf16[128,2688]{1,0:T(8,128)(2,1)S(1)}, u32[]{:S(2)}, u32[]{:S(2)}) collective-permute-start(bf16[128,2688]{1,0:T(8,128)(2,1)S(1)} %get-tuple-element.93), channel_id=1, source_target_pairs={{0,2},{2,0},{4,6},{6,4},{8,10},{10,8},{12,14},{14,12},{1,3},{3,1},... | collective-permute-start | bytes 2064392 | tf_op jit(solution)/shard_map/ppermute | solution.py:171
  84.5 3.1 %collective-permute-start.25 = (bf16[64,2560]{1,0:T(8,128)(2,1)S(1)}, bf16[64,2560]{1,0:T(8,128)(2,1)S(1)}, u32[]{:S(2)}, u32[]{:S(2)}) collective-permute-start(bf16[64,2560]{1,0:T(8,128)(2,1)S(1)} %get-tuple-element.107), channel_id=1, source_target_pairs={{0,8},{2,10},{4,12},{6,14},{8,0},{10,2},{12,4},{14,6},{1,9},{3,11}... | collective-permute-start | bytes 983048 | tf_op jit(solution)/shard_map/ppermute | solution.py:171
  87.6 1.3 %collective-permute-start.26 = (bf16[64,2560]{1,0:T(8,128)(2,1)S(1)}, bf16[64,2560]{1,0:T(8,128)(2,1)S(1)}, u32[]{:S(2)}, u32[]{:S(2)}) collective-permute-start(bf16[64,2560]{1,0:T(8,128)(2,1)S(1)} %get-tuple-element.108), channel_id=1, source_target_pairs={{0,12},{2,14},{4,8},{6,10},{8,4},{10,6},{12,0},{14,2},{1,13},{3,15... | collective-permute-start | bytes 983048 | tf_op jit(solution)/shard_map/ppermute | solution.py:171
  89.2 11.2 %collective-permute-done.22.sent_ref = bf16[128,2688]{1,0:T(8,128)(2,1)S(1)} collective-permute-done((bf16[128,2688]{1,0:T(8,128)(2,1)S(1)}, bf16[128,2688]{1,0:T(8,128)(2,1)S(1)}, u32[]{:S(2)}, u32[]{:S(2)}) %collective-permute-start.22) | collective-permute-done | bytes 688160 | tf_op jit(solution)/shard_map/ppermute | solution.py:171
  100.5 1.2 %shard_map.153 = (bf16[128,2048]{1,0:T(8,128)(2,1)}, bf16[128,512]{1,0:T(8,128)(2,1)}, f32[1,4,32]{2,1,0:T(4,128)}) custom-call(s32[1]{0:T(128)} %bitcast.me_ref, f32[128,2560]{1,0:T(8,128)S(1)} %get-tuple-element.92.own_ref, bf16[128,2688]{1,0:T(8,128)(2,1)S(1)} %collective-permute-done.22.sent_ref, bf16[128,128]{1,0:T(8,128)(2,1)S(1)} %get-tuple-element.101.rg_ref, ...), custom_call_target="tpu_custom_call" | custom-call | tf_op jit(solution)/shard_map/pallas_call | solution.py:526
  101.7 4.6 %collective-permute-done.23 = bf16[2048,128]{1,0:T(8,128)(2,1)S(1)} collective-permute-done((bf16[2048,128]{1,0:T(8,128)(2,1)S(1)}, bf16[2048,128]{1,0:T(8,128)(2,1)S(1)}, u32[]{:S(2)}, u32[]{:S(2)}) %collective-permute-start.23) | collective-permute-done | bytes 524320 | tf_op jit(solution)/shard_map/ppermute | solution.py:171
  (64 shorter events, 16.3 us)
Async XLA Ops:
  0.6 19.3 %collective-permute-start.1 = (bf16[2048,128]{1,0:T(8,128)(2,1)}, bf16[2048,128]{1,0:T(8,128)(2,1)S(1)}, u32[]{:S(2)}, u32[]{:S(2)}) collective-permute-start(bf16[2048,128]{1,0:T(8,128)(2,1)} %bitcast.13), channel_id=1, source_target_pairs={{0,2},{2,0},{4,6},{6,4},{8,10},{10,8},{12,14},{14,12},{1,3},{3,1},... | collective-permute-start | bytes 1572872 | tf_op jit(solution)/shard_map/ppermute | solution.py:171
  3.6 16.9 %collective-permute-start = (bf16[128,2048]{1,0:T(8,128)(2,1)}, bf16[128,2048]{1,0:T(8,128)(2,1)S(1)}, u32[]{:S(2)}, u32[]{:S(2)}) collective-permute-start(bf16[128,2048]{1,0:T(8,128)(2,1)} %x.1), channel_id=1, source_target_pairs={{0,4},{2,6},{4,0},{6,2},{8,12},{10,14},{12,8},{14,10},{1,5},{3,7},... | collective-permute-start | bytes 1572872 | tf_op jit(solution)/shard_map/ppermute | solution.py:171
  5.2 16.1 %collective-permute-start.2 = (bf16[128,2048]{1,0:T(8,128)(2,1)}, bf16[128,2048]{1,0:T(8,128)(2,1)S(1)}, u32[]{:S(2)}, u32[]{:S(2)}) collective-permute-start(bf16[128,2048]{1,0:T(8,128)(2,1)} %x.1), channel_id=1, source_target_pairs={{4,8},{6,10},{8,4},{10,6},{5,9},{7,11},{9,5},{11,7},{20,24},{22,26... | collective-permute-start | bytes 1572872 | tf_op jit(solution)/shard_map/ppermute | solution.py:446
  5.9 1.0 copy-start
  7.0 1.0 copy-start.1
  14.9 32.0 %collective-permute-start.9 = (bf16[128,2816]{1,0:T(8,128)(2,1)S(1)}, bf16[128,2816]{1,0:T(8,128)(2,1)S(1)}, u32[]{:S(2)}, u32[]{:S(2)}) collective-permute-start(bf16[128,2816]{1,0:T(8,128)(2,1)S(1)} %get-tuple-element.64.gw_ref), channel_id=1, source_target_pairs={{0,2},{2,0},{4,6},{6,4},{8,10},{10,8},{12,14},{14,12},{1,3},{3,1},... | collective-permute-start | bytes 2162696 | tf_op jit(solution)/shard_map/ppermute | solution.py:171
  15.5 11.3 %collective-permute-start.5 = (bf16[80,2048]{1,0:T(8,128)(2,1)S(1)}, bf16[80,2048]{1,0:T(8,128)(2,1)S(1)}, u32[]{:S(2)}, u32[]{:S(2)}) collective-permute-start(bf16[80,2048]{1,0:T(8,128)(2,1)S(1)} %get-tuple-element.61.b0), channel_id=1, source_target_pairs={{0,4},{2,6},{4,0},{6,2},{8,12},{10,14},{12,8},{14,10},{1,5},{3,7},... | collective-permute-start | bytes 983048 | tf_op jit(solution)/shard_map/ppermute | solution.py:171
  19.9 7.6 %collective-permute-start.6 = (bf16[80,2048]{1,0:T(8,128)(2,1)S(1)}, bf16[80,2048]{1,0:T(8,128)(2,1)S(1)}, u32[]{:S(2)}, u32[]{:S(2)}) collective-permute-start(bf16[80,2048]{1,0:T(8,128)(2,1)S(1)} %get-tuple-element.61.b0), channel_id=1, source_target_pairs={{4,8},{6,10},{8,4},{10,6},{5,9},{7,11},{9,5},{11,7},{20,24},{22,26... | collective-permute-start | bytes 983048 | tf_op jit(solution)/shard_map/ppermute | solution.py:452
  20.6 8.2 %collective-permute-start.4 = (bf16[128,2048]{1,0:T(8,128)(2,1)S(1)}, bf16[128,2048]{1,0:T(8,128)(2,1)S(1)}, u32[]{:S(2)}, u32[]{:S(2)}) collective-permute-start(bf16[128,2048]{1,0:T(8,128)(2,1)S(1)} %collective-permute-done.x1), channel_id=1, source_target_pairs={{4,8},{6,10},{8,4},{10,6},{5,9},{7,11},{9,5},{11,7},{20,24},{22,26... | collective-permute-start | bytes 1572872 | tf_op jit(solution)/shard_map/ppermute | solution.py:454
  21.3 25.6 %collective-permute-start.3 = (bf16[128,2048]{1,0:T(8,128)(2,1)S(1)}, bf16[128,2048]{1,0:T(8,128)(2,1)S(1)}, u32[]{:S(2)}, u32[]{:S(2)}) collective-permute-start(bf16[128,2048]{1,0:T(8,128)(2,1)S(1)} %collective-permute-done.2.xi), channel_id=1, source_target_pairs={{4,0},{6,2},{8,12},{10,14},{5,1},{7,3},{9,13},{11,15},{20,16},{22,... | collective-permute-start | bytes 1572872 | tf_op jit(solution)/shard_map/ppermute | solution.py:455
  26.8 3.3 %collective-permute-start.8 = (bf16[80,2048]{1,0:T(8,128)(2,1)S(1)}, bf16[80,2048]{1,0:T(8,128)(2,1)S(1)}, u32[]{:S(2)}, u32[]{:S(2)}) collective-permute-start(bf16[80,2048]{1,0:T(8,128)(2,1)S(1)} %collective-permute-done.5.b1), channel_id=1, source_target_pairs={{4,8},{6,10},{8,4},{10,6},{5,9},{7,11},{9,5},{11,7},{20,24},{22,26... | collective-permute-start | bytes 983048 | tf_op jit(solution)/shard_map/ppermute | solution.py:456
  27.5 19.4 %collective-permute-start.7 = (bf16[80,2048]{1,0:T(8,128)(2,1)S(1)}, bf16[80,2048]{1,0:T(8,128)(2,1)S(1)}, u32[]{:S(2)}, u32[]{:S(2)}) collective-permute-start(bf16[80,2048]{1,0:T(8,128)(2,1)S(1)} %collective-permute-done.6.bi), channel_id=1, source_target_pairs={{4,0},{6,2},{8,12},{10,14},{5,1},{7,3},{9,13},{11,15},{20,16},{22,... | collective-permute-start | bytes 983048 | tf_op jit(solution)/shard_map/ppermute | solution.py:456
  28.8 36.2 %collective-permute-start.18 = (bf16[128,2048]{1,0:T(8,128)(2,1)S(1)}, bf16[128,2048]{1,0:T(8,128)(2,1)S(1)}, u32[]{:S(2)}, u32[]{:S(2)}) collective-permute-start(bf16[128,2048]{1,0:T(8,128)(2,1)S(1)} %collective-permute-done.4.xm), channel_id=1, source_target_pairs={{4,0},{6,2},{8,12},{10,14},{5,1},{7,3},{9,13},{11,15},{20,16},{22,... | collective-permute-start | bytes 1572872 | tf_op jit(solution)/shard_map/ppermute | solution.py:458
  30.2 32.8 %collective-permute-start.12 = (bf16[80,2048]{1,0:T(8,128)(2,1)S(1)}, bf16[80,2048]{1,0:T(8,128)(2,1)S(1)}, u32[]{:S(2)}, u32[]{:S(2)}) collective-permute-start(bf16[80,2048]{1,0:T(8,128)(2,1)S(1)} %collective-permute-done.8.bm), channel_id=1, source_target_pairs={{4,0},{6,2},{8,12},{10,14},{5,1},{7,3},{9,13},{11,15},{20,16},{22,... | collective-permute-start | bytes 983048 | tf_op jit(solution)/shard_map/ppermute | solution.py:459
  49.0 1.5 %collective-permute-start.10 = (bf16[384,256]{1,0:T(8,128)(2,1)S(1)}, bf16[384,256]{1,0:T(8,128)(2,1)S(1)}, u32[]{:S(2)}, u32[]{:S(2)}) collective-permute-start(bf16[384,256]{1,0:T(8,128)(2,1)S(1)} %get-tuple-element.65.m_ref), channel_id=1, source_target_pairs={{0,1},{1,0},{2,3},{3,2},{4,5},{5,4},{6,7},{7,6},{8,9},{9,8},{10,11... | collective-permute-start | bytes 589832 | tf_op jit(solution)/shard_map/ppermute | solution.py:175
  49.1 1.7 %collective-permute-start.11 = (bf16[384,256]{1,0:T(8,128)(2,1)S(1)}, bf16[384,256]{1,0:T(8,128)(2,1)S(1)}, u32[]{:S(2)}, u32[]{:S(2)}) collective-permute-start(bf16[384,256]{1,0:T(8,128)(2,1)S(1)} %get-tuple-element.66.s_ref), channel_id=1, source_target_pairs={{0,1},{1,0},{2,3},{3,2},{4,5},{5,4},{6,7},{7,6},{8,9},{9,8},{10,11... | collective-permute-start | bytes 589832 | tf_op jit(solution)/shard_map/ppermute | solution.py:175
  51.0 12.0 %collective-permute-start.13 = (bf16[128,256]{1,0:T(8,128)(2,1)S(1)}, bf16[128,256]{1,0:T(8,128)(2,1)S(1)}, u32[]{:S(2)}, u32[]{:S(2)}) collective-permute-start(bf16[128,256]{1,0:T(8,128)(2,1)S(1)} %get-tuple-element.69), channel_id=1, source_target_pairs={{0,2},{2,0},{4,6},{6,4},{8,10},{10,8},{12,14},{14,12},{1,3},{3,1},... | collective-permute-start | bytes 196616 | tf_op jit(solution)/shard_map/ppermute | solution.py:171
  52.5 10.5 %collective-permute-start.14 = (bf16[128,256]{1,0:T(8,128)(2,1)S(1)}, bf16[128,256]{1,0:T(8,128)(2,1)S(1)}, u32[]{:S(2)}, u32[]{:S(2)}) collective-permute-start(bf16[128,256]{1,0:T(8,128)(2,1)S(1)} %get-tuple-element.70), channel_id=1, source_target_pairs={{0,2},{2,0},{4,6},{6,4},{8,10},{10,8},{12,14},{14,12},{1,3},{3,1},... | collective-permute-start | bytes 196616 | tf_op jit(solution)/shard_map/ppermute | solution.py:171
  53.1 10.0 %collective-permute-start.15 = (bf16[128,256]{1,0:T(8,128)(2,1)S(1)}, bf16[128,256]{1,0:T(8,128)(2,1)S(1)}, u32[]{:S(2)}, u32[]{:S(2)}) collective-permute-start(bf16[128,256]{1,0:T(8,128)(2,1)S(1)} %get-tuple-element.71), channel_id=1, source_target_pairs={{0,2},{2,0},{4,6},{6,4},{8,10},{10,8},{12,14},{14,12},{1,3},{3,1},... | collective-permute-start | bytes 196616 | tf_op jit(solution)/shard_map/ppermute | solution.py:171
  63.1 6.2 %collective-permute-start.16 = (bf16[128,512]{1,0:T(8,128)(2,1)S(1)}, bf16[128,512]{1,0:T(8,128)(2,1)S(1)}, u32[]{:S(2)}, u32[]{:S(2)}) collective-permute-start(bf16[128,512]{1,0:T(8,128)(2,1)S(1)} %get-tuple-element.73), channel_id=1, source_target_pairs={{0,4},{2,6},{4,0},{6,2},{8,12},{10,14},{12,8},{14,10},{1,5},{3,7},... | collective-permute-start | bytes 393224 | tf_op jit(solution)/shard_map/ppermute | solution.py:171
  63.2 7.6 %collective-permute-start.17 = (bf16[128,512]{1,0:T(8,128)(2,1)S(1)}, bf16[128,512]{1,0:T(8,128)(2,1)S(1)}, u32[]{:S(2)}, u32[]{:S(2)}) collective-permute-start(bf16[128,512]{1,0:T(8,128)(2,1)S(1)} %get-tuple-element.74), channel_id=1, source_target_pairs={{0,8},{2,10},{4,12},{6,14},{8,0},{10,2},{12,4},{14,6},{1,9},{3,11}... | collective-permute-start | bytes 393224 | tf_op jit(solution)/shard_map/ppermute | solution.py:171
  65.9 5.8 %collective-permute-start.19 = (bf16[128,512]{1,0:T(8,128)(2,1)S(1)}, bf16[128,512]{1,0:T(8,128)(2,1)S(1)}, u32[]{:S(2)}, u32[]{:S(2)}) collective-permute-start(bf16[128,512]{1,0:T(8,128)(2,1)S(1)} %get-tuple-element.78.m_ref), channel_id=1, source_target_pairs={{0,1},{1,0},{2,3},{3,2},{4,5},{5,4},{6,7},{7,6},{8,9},{9,8},{10,11... | collective-permute-start | bytes 393224 | tf_op jit(solution)/shard_map/ppermute | solution.py:175
  71.9 6.1 %collective-permute-start.20 = (bf16[128,256]{1,0:T(8,128)(2,1)S(1)}, bf16[128,256]{1,0:T(8,128)(2,1)S(1)}, u32[]{:S(2)}, u32[]{:S(2)}) collective-permute-start(bf16[128,256]{1,0:T(8,128)(2,1)S(1)} %get-tuple-element.84), channel_id=1, source_target_pairs={{0,12},{2,14},{4,8},{6,10},{8,4},{10,6},{12,0},{14,2},{1,13},{3,15... | collective-permute-start | bytes 196616 | tf_op jit(solution)/shard_map/ppermute | solution.py:171
  73.3 7.0 %collective-permute-start.21 = (bf16[128,256]{1,0:T(8,128)(2,1)S(1)}, bf16[128,256]{1,0:T(8,128)(2,1)S(1)}, u32[]{:S(2)}, u32[]{:S(2)}) collective-permute-start(bf16[128,256]{1,0:T(8,128)(2,1)S(1)} %get-tuple-element.85), channel_id=1, source_target_pairs={{0,14},{2,12},{4,10},{6,8},{8,6},{10,4},{12,2},{14,0},{1,15},{3,13... | collective-permute-start | bytes 196616 | tf_op jit(solution)/shard_map/ppermute | solution.py:171
  82.0 18.4 %collective-permute-start.22 = (bf16[128,2688]{1,0:T(8,128)(2,1)S(1)}, bf16[128,2688]{1,0:T(8,128)(2,1)S(1)}, u32[]{:S(2)}, u32[]{:S(2)}) collective-permute-start(bf16[128,2688]{1,0:T(8,128)(2,1)S(1)} %get-tuple-element.93), channel_id=1, source_target_pairs={{0,2},{2,0},{4,6},{6,4},{8,10},{10,8},{12,14},{14,12},{1,3},{3,1},... | collective-permute-start | bytes 2064392 | tf_op jit(solution)/shard_map/ppermute | solution.py:171
  83.3 17.2 %copy-start.7 = (s32[1,32,4]{1,2,0:T(4,128)S(1)}, s32[1,32,4]{1,2,0:T(4,128)}, u32[]{:S(2)}) copy-start(s32[1,32,4]{1,2,0:T(4,128)} %param.17) | copy-start | bytes 1540
  83.3 17.2 %copy-start.9 = (s32[1,128]{1,0:T(1,128)S(1)}, s32[1,128]{1,0:T(1,128)}, u32[]{:S(2)}) copy-start(s32[1,128]{1,0:T(1,128)} %tr_ref.1) | copy-start | bytes 1540
  83.3 17.2 %copy-start.11 = (s32[1,32]{1,0:T(1,128)S(1)}, s32[1,32]{1,0:T(1,128)}, u32[]{:S(2)}) copy-start(s32[1,32]{1,0:T(1,128)} %rc_ref.1) | copy-start | bytes 388
  83.6 22.6 %collective-permute-start.23 = (bf16[2048,128]{1,0:T(8,128)(2,1)S(1)}, bf16[2048,128]{1,0:T(8,128)(2,1)S(1)}, u32[]{:S(2)}, u32[]{:S(2)}) collective-permute-start(bf16[2048,128]{1,0:T(8,128)(2,1)S(1)} %add_convert_fusion), channel_id=1, source_target_pairs={{0,2},{2,0},{4,6},{6,4},{8,10},{10,8},{12,14},{14,12},{1,3},{3,1},... | collective-permute-start | bytes 1572872 | tf_op jit(solution)/shard_map/ppermute | solution.py:171
  84.5 22.6 %collective-permute-start.24 = (bf16[64,2560]{1,0:T(8,128)(2,1)S(1)}, bf16[64,2560]{1,0:T(8,128)(2,1)S(1)}, u32[]{:S(2)}, u32[]{:S(2)}) collective-permute-start(bf16[64,2560]{1,0:T(8,128)(2,1)S(1)} %get-tuple-element.105), channel_id=1, source_target_pairs={{0,4},{2,6},{4,0},{6,2},{8,12},{10,14},{12,8},{14,10},{1,5},{3,7},... | collective-permute-start | bytes 983048 | tf_op jit(solution)/shard_map/ppermute | solution.py:171
  84.5 22.6 %collective-permute-start.25 = (bf16[64,2560]{1,0:T(8,128)(2,1)S(1)}, bf16[64,2560]{1,0:T(8,128)(2,1)S(1)}, u32[]{:S(2)}, u32[]{:S(2)}) collective-permute-start(bf16[64,2560]{1,0:T(8,128)(2,1)S(1)} %get-tuple-element.107), channel_id=1, source_target_pairs={{0,8},{2,10},{4,12},{6,14},{8,0},{10,2},{12,4},{14,6},{1,9},{3,11}... | collective-permute-start | bytes 983048 | tf_op jit(solution)/shard_map/ppermute | solution.py:171
  87.6 19.5 %collective-permute-start.26 = (bf16[64,2560]{1,0:T(8,128)(2,1)S(1)}, bf16[64,2560]{1,0:T(8,128)(2,1)S(1)}, u32[]{:S(2)}, u32[]{:S(2)}) collective-permute-start(bf16[64,2560]{1,0:T(8,128)(2,1)S(1)} %get-tuple-element.108), channel_id=1, source_target_pairs={{0,12},{2,14},{4,8},{6,10},{8,4},{10,6},{12,0},{14,2},{1,13},{3,15... | collective-permute-start | bytes 983048 | tf_op jit(solution)/shard_map/ppermute | solution.py:171
  (8 other events, 6.4 us)

commit v6 on v5

--- a/solution.py
+++ b/solution.py
@@ -211,16 +211,13 @@
     return found & jnp.broadcast_to(rc_ref[...] > k, place.shape)
 
 
-def prepare(me_ref, tr, ra, rc, rm, bq, bv, gq, gv, x, a, b_ref, gw_ref, x_ref, a_ref, tr_ref, ra_ref, rc_ref, rm_ref, sems):
+def prepare(me_ref, small, bq, bv, gq, gv, x, a, b_ref, gw_ref, x_ref, a_ref, small_ref, tr_ref, ra_ref, rc_ref, rm_ref, sems):
     wide = x.shape[1]
     rank, narrow = bv.shape[1:]
     full = wide + narrow
     step = rank * narrow // wide
     pairs = [
-        (tr, tr_ref),
-        (ra, ra_ref),
-        (rc, rc_ref),
-        (rm, rm_ref),
+        (small, small_ref),
         (bq.at[0], b_ref.at[pl.ds(0, rank)]),
         (gq, gw_ref.at[:, pl.ds(0, wide)]),
         (gv, gw_ref.at[:, pl.ds(wide, narrow)]),
@@ -233,8 +230,12 @@
     copies = [pltpu.make_async_copy(src, dst, sems.at[i]) for i, (src, dst) in enumerate(pairs)]
     for copy in copies:
         copy.start()
-    for copy in copies[:4]:
-        copy.wait()
+    copies[0].wait()
+    held = rc_ref.shape[1]
+    tr_ref[...] = small_ref[0:1, :].astype(jnp.int32)
+    ra_ref[0] = small_ref[8:12, :held].astype(jnp.int32)
+    rc_ref[...] = small_ref[16:17, :held].astype(jnp.int32)
+    rm_ref[0] = small_ref[24:28, :held].astype(BF16)
     requests = ra_ref.shape[2]
     place = lax.broadcasted_iota(jnp.int32, (LANES, requests), 0)
     total = jnp.zeros((LANES, requests), F32)
@@ -246,7 +247,7 @@
     member = jnp.where(members(tr_ref[...], requests), 1.0, 0.0).astype(BF16)
     gw_ref[:, full : full + LANES] = dot(member, high, ((0,), (1,))).astype(BF16)
     gw_ref[:, full + LANES :] = dot(member, low, ((0,), (1,))).astype(BF16)
-    for copy in copies[4:]:
+    for copy in copies[1:]:
         copy.wait()
 
 
@@ -440,13 +441,17 @@
     b_block = ((rank, full), BF16)
     x_block = (tokens.shape, BF16)
     adapters = jnp.swapaxes(req_adapter, 1, 2)
+    mixes = jnp.swapaxes(req_mix, 1, 2)
+    rows = (token_request, adapters[0], req_count, mixes[0])
+    rows = [jnp.pad(r.astype(F32), ((0, 8 - r.shape[0]), (0, count - r.shape[1]))) for r in rows]
+    small = jnp.concatenate(rows, axis=0)
     pair = ((count, 2 * rank2), BF16)
     early = ((count, 3 * rank2), BF16)
 
     x1, xi = to_place(tokens, 2), lax.ppermute(tokens, "expert", MID)
     a_other = to_place(a_proj[0], 1)
     b0, gw, x0, a_own = call_prepare(
-        me, token_request, adapters, req_count, jnp.swapaxes(req_mix, 1, 2),
+        me, small, (token_request, adapters, req_count, mixes),
         b_query, b_value, grad_query, grad_value, tokens, a_proj[0],
     )
     b1, bi = to_place(b0, 2), lax.ppermute(b0, "expert", MID)
@@ -533,8 +538,9 @@
     )(*ins)
 
 
-def call_prepare(me, *ins):
-    request, adapters, counts, mix, b_query, b_value, grad_query, grad_value, x, a = ins
+def call_prepare(me, *args):
+    small, (request, adapters, counts, mix), b_query, b_value, grad_query, grad_value, x, a = args
+    ins = (small, *args[2:])
     rank, wide = b_query.shape[1:]
     narrow = b_value.shape[2]
     step = rank * narrow // wide
@@ -549,7 +555,7 @@
         out_shape=[jax.ShapeDtypeStruct(shape, BF16) for shape in outs],
         in_specs=[pl.BlockSpec(memory_space=pltpu.SMEM)] + [pl.BlockSpec(memory_space=pltpu.HBM)] * len(ins),
         out_specs=[pl.BlockSpec(memory_space=pltpu.VMEM)] * len(outs),
-        scratch_shapes=[pltpu.VMEM(i.shape, i.dtype) for i in (request, adapters, counts, mix)]
+        scratch_shapes=[pltpu.VMEM(i.shape, i.dtype) for i in (small, request, adapters, counts, mix)]
         + [pltpu.SemaphoreType.DMA((len(ins) - 1 + rank // step,))],
         compiler_params=pltpu.CompilerParams(vmem_limit_bytes=PREP_VMEM * 1024 * 1024),
         cost_estimate=cost(0),

time: 110 us -> 110 us (level)
  other arithmetic: 0.9 us -> 3.59 us
  local copies, waits for them, and re-layouts: 8.49 us -> 5.83 us
    unnamed x26 -> x18, local copies, waits for them, and re-layouts: 8.49 us -> 5.83 us
    convert_element_type x0 -> x3, other arithmetic: none -> 2 us  [pair_plan(): r.astype(F32)]
  transfers between devices with their start and end apart: 27 -> 27, of which waited for: 11 -> 11; matrix products, arithmetic and copies ran while one was open for 3% -> 5% of each run, Pallas kernels for 5% -> 4%
where the time goes in v6:
time: 110 us; the launch traced here: 108 us
  waiting for transfers between devices  53 us (48%)
  starting transfers between devices  35.1 us (32%)
  Pallas kernels  7.52 us (7%)
  local copies, waits for them, and re-layouts  5.83 us (5%)
  other arithmetic  3.59 us (3%)
  matrix products  2.05 us (2%)
    ppermute x16, waiting for transfers between devices, to_place(): lax.ppermute(array, 'expert', [(i, i ^ place) for i in range(LINE * PAIR)])  27.9 us
    ppermute x16, starting transfers between devices, to_place(): lax.ppermute(array, 'expert', [(i, i ^ place) for i in range(LINE * PAIR)])  26.6 us
    ppermute x2, waiting for transfers between devices, pair_plan(): bo, bm = (lax.ppermute(bi, 'expert', OUT), lax.ppermute(b1, 'expert', MID))  15.5 us
    ppermute x1, waiting for transfers between devices, pair_plan(): bo3 = lax.ppermute(bm, 'expert', OUT)  8.45 us
    unnamed x18, local copies, waits for them, and re-layouts  5.83 us
    pallas_call x8, Pallas kernels, call(): pl.pallas_call(kernel, out_shape=shapes, in_specs=[pl.BlockSpec(memory_sp...  5.83 us
  transfers between devices with their start and end apart: 27, of which 11 were waited for; matrix products, arithmetic and copies ran while one was open for 5% of the time, Pallas kernels for 4%

profile of v6, /device:TPU:0, one launch (start us, length us, event | category | flops | bytes accessed | tf_op | source)
XLA Modules:
  0.0 108.0 jit_solution(15423443109641122141)
XLA Ops:
  0.6 3.0 %collective-permute-start.1 = (bf16[2048,128]{1,0:T(8,128)(2,1)}, bf16[2048,128]{1,0:T(8,128)(2,1)S(1)}, u32[]{:S(2)}, u32[]{:S(2)}) collective-permute-start(bf16[2048,128]{1,0:T(8,128)(2,1)} %bitcast.18), channel_id=1, source_target_pairs={{0,2},{2,0},{4,6},{6,4},{8,10},{10,8},{12,14},{14,12},{1,3},{3,1},... | collective-permute-start | bytes 1572872 | tf_op jit(solution)/shard_map/ppermute | solution.py:171
  3.6 1.6 %collective-permute-start = (bf16[128,2048]{1,0:T(8,128)(2,1)}, bf16[128,2048]{1,0:T(8,128)(2,1)S(1)}, u32[]{:S(2)}, u32[]{:S(2)}) collective-permute-start(bf16[128,2048]{1,0:T(8,128)(2,1)} %x.9), channel_id=1, source_target_pairs={{0,4},{2,6},{4,0},{6,2},{8,12},{10,14},{12,8},{14,10},{1,5},{3,7},... | collective-permute-start | bytes 1572872 | tf_op jit(solution)/shard_map/ppermute | solution.py:171
  8.6 1.0 copy-done
  9.6 1.0 copy-done.1
  10.7 1.0 copy-done.2
  11.7 0.9 copy-done.3
  12.7 0.9 copy-done.4
  15.5 4.4 %collective-permute-start.5 = (bf16[80,2048]{1,0:T(8,128)(2,1)S(1)}, bf16[80,2048]{1,0:T(8,128)(2,1)S(1)}, u32[]{:S(2)}, u32[]{:S(2)}) collective-permute-start(bf16[80,2048]{1,0:T(8,128)(2,1)S(1)} %get-tuple-element.61.b0), channel_id=1, source_target_pairs={{0,4},{2,6},{4,0},{6,2},{8,12},{10,14},{12,8},{14,10},{1,5},{3,7},... | collective-permute-start | bytes 983048 | tf_op jit(solution)/shard_map/ppermute | solution.py:171
  21.3 1.3 %collective-permute-start.3 = (bf16[128,2048]{1,0:T(8,128)(2,1)S(1)}, bf16[128,2048]{1,0:T(8,128)(2,1)S(1)}, u32[]{:S(2)}, u32[]{:S(2)}) collective-permute-start(bf16[128,2048]{1,0:T(8,128)(2,1)S(1)} %collective-permute-done.2.xi), channel_id=1, source_target_pairs={{4,0},{6,2},{8,12},{10,14},{5,1},{7,3},{9,13},{11,15},{20,16},{22,... | collective-permute-start | bytes 1572872 | tf_op jit(solution)/shard_map/ppermute | solution.py:460
  22.6 4.2 %collective-permute-done.5.b1 = bf16[80,2048]{1,0:T(8,128)(2,1)S(1)} collective-permute-done((bf16[80,2048]{1,0:T(8,128)(2,1)S(1)}, bf16[80,2048]{1,0:T(8,128)(2,1)S(1)}, u32[]{:S(2)}, u32[]{:S(2)}) %collective-permute-start.5) | collective-permute-done | bytes 327712 | tf_op jit(solution)/shard_map/ppermute | solution.py:171
  27.5 1.3 %collective-permute-start.7 = (bf16[80,2048]{1,0:T(8,128)(2,1)S(1)}, bf16[80,2048]{1,0:T(8,128)(2,1)S(1)}, u32[]{:S(2)}, u32[]{:S(2)}) collective-permute-start(bf16[80,2048]{1,0:T(8,128)(2,1)S(1)} %collective-permute-done.6.bi), channel_id=1, source_target_pairs={{4,0},{6,2},{8,12},{10,14},{5,1},{7,3},{9,13},{11,15},{20,16},{22,... | collective-permute-start | bytes 983048 | tf_op jit(solution)/shard_map/ppermute | solution.py:461
  28.8 1.3 %collective-permute-start.18 = (bf16[128,2048]{1,0:T(8,128)(2,1)S(1)}, bf16[128,2048]{1,0:T(8,128)(2,1)S(1)}, u32[]{:S(2)}, u32[]{:S(2)}) collective-permute-start(bf16[128,2048]{1,0:T(8,128)(2,1)S(1)} %collective-permute-done.4.xm), channel_id=1, source_target_pairs={{4,0},{6,2},{8,12},{10,14},{5,1},{7,3},{9,13},{11,15},{20,16},{22,... | collective-permute-start | bytes 1572872 | tf_op jit(solution)/shard_map/ppermute | solution.py:463
  30.1 1.3 %collective-permute-start.12 = (bf16[80,2048]{1,0:T(8,128)(2,1)S(1)}, bf16[80,2048]{1,0:T(8,128)(2,1)S(1)}, u32[]{:S(2)}, u32[]{:S(2)}) collective-permute-start(bf16[80,2048]{1,0:T(8,128)(2,1)S(1)} %collective-permute-done.8.bm), channel_id=1, source_target_pairs={{4,0},{6,2},{8,12},{10,14},{5,1},{7,3},{9,13},{11,15},{20,16},{22,... | collective-permute-start | bytes 983048 | tf_op jit(solution)/shard_map/ppermute | solution.py:464
  31.4 15.5 %collective-permute-done.7.bo = bf16[80,2048]{1,0:T(8,128)(2,1)S(1)} collective-permute-done((bf16[80,2048]{1,0:T(8,128)(2,1)S(1)}, bf16[80,2048]{1,0:T(8,128)(2,1)S(1)}, u32[]{:S(2)}, u32[]{:S(2)}) %collective-permute-start.7) | collective-permute-done | bytes 327712 | tf_op jit(solution)/shard_map/ppermute | solution.py:461
  46.9 2.1 %shard_map.146 = (bf16[384,256]{1,0:T(8,128)(2,1)S(1)}, bf16[384,256]{1,0:T(8,128)(2,1)S(1)}, bf16[128,2048]{1,0:T(8,128)(2,1)S(1)}, bf16[80,2048]{1,0:T(8,128)(2,1)S(1)}) custom-call(bf16[128,2048]{1,0:T(8,128)(2,1)S(1)} %get-tuple-element.59.x0, bf16[128,2048]{1,0:T(8,128)(2,1)S(1)} %collective-permute-done.x1, ...), custom_call_target="tpu_custom_call" | custom-call | tf_op jit(solution)/shard_map/pallas_call | solution.py:193
  49.5 0.9 collective-permute-done.10.mr_ref
  51.0 1.6 %collective-permute-start.13 = (bf16[128,256]{1,0:T(8,128)(2,1)S(1)}, bf16[128,256]{1,0:T(8,128)(2,1)S(1)}, u32[]{:S(2)}, u32[]{:S(2)}) collective-permute-start(bf16[128,256]{1,0:T(8,128)(2,1)S(1)} %get-tuple-element.69), channel_id=1, source_target_pairs={{0,2},{2,0},{4,6},{6,4},{8,10},{10,8},{12,14},{14,12},{1,3},{3,1},... | collective-permute-start | bytes 196616 | tf_op jit(solution)/shard_map/ppermute | solution.py:171
  53.0 1.5 %collective-permute-start.15 = (bf16[128,256]{1,0:T(8,128)(2,1)S(1)}, bf16[128,256]{1,0:T(8,128)(2,1)S(1)}, u32[]{:S(2)}, u32[]{:S(2)}) collective-permute-start(bf16[128,256]{1,0:T(8,128)(2,1)S(1)} %get-tuple-element.71), channel_id=1, source_target_pairs={{0,2},{2,0},{4,6},{6,4},{8,10},{10,8},{12,14},{14,12},{1,3},{3,1},... | collective-permute-start | bytes 196616 | tf_op jit(solution)/shard_map/ppermute | solution.py:171
  54.5 8.5 %collective-permute-done.12.bo = bf16[80,2048]{1,0:T(8,128)(2,1)S(1)} collective-permute-done((bf16[80,2048]{1,0:T(8,128)(2,1)S(1)}, bf16[80,2048]{1,0:T(8,128)(2,1)S(1)}, u32[]{:S(2)}, u32[]{:S(2)}) %collective-permute-start.12) | collective-permute-done | bytes 327712 | tf_op jit(solution)/shard_map/ppermute | solution.py:464
  63.2 1.9 %collective-permute-start.17 = (bf16[128,512]{1,0:T(8,128)(2,1)S(1)}, bf16[128,512]{1,0:T(8,128)(2,1)S(1)}, u32[]{:S(2)}, u32[]{:S(2)}) collective-permute-start(bf16[128,512]{1,0:T(8,128)(2,1)S(1)} %get-tuple-element.74), channel_id=1, source_target_pairs={{0,8},{2,10},{4,12},{6,14},{8,0},{10,2},{12,4},{14,6},{1,9},{3,11}... | collective-permute-start | bytes 393224 | tf_op jit(solution)/shard_map/ppermute | solution.py:171
  66.0 3.3 %collective-permute-done.16.c1 = bf16[128,512]{1,0:T(8,128)(2,1)S(1)} collective-permute-done((bf16[128,512]{1,0:T(8,128)(2,1)S(1)}, bf16[128,512]{1,0:T(8,128)(2,1)S(1)}, u32[]{:S(2)}, u32[]{:S(2)}) %collective-permute-start.16) | collective-permute-done | bytes 131104 | tf_op jit(solution)/shard_map/ppermute | solution.py:171
  69.3 1.5 %collective-permute-done.17.c2 = bf16[128,512]{1,0:T(8,128)(2,1)S(1)} collective-permute-done((bf16[128,512]{1,0:T(8,128)(2,1)S(1)}, bf16[128,512]{1,0:T(8,128)(2,1)S(1)}, u32[]{:S(2)}, u32[]{:S(2)}) %collective-permute-start.17) | collective-permute-done | bytes 131104 | tf_op jit(solution)/shard_map/ppermute | solution.py:171
  71.9 1.4 %collective-permute-start.20 = (bf16[128,256]{1,0:T(8,128)(2,1)S(1)}, bf16[128,256]{1,0:T(8,128)(2,1)S(1)}, u32[]{:S(2)}, u32[]{:S(2)}) collective-permute-start(bf16[128,256]{1,0:T(8,128)(2,1)S(1)} %get-tuple-element.84), channel_id=1, source_target_pairs={{0,12},{2,14},{4,8},{6,10},{8,4},{10,6},{12,0},{14,2},{1,13},{3,15... | collective-permute-start | bytes 196616 | tf_op jit(solution)/shard_map/ppermute | solution.py:171
  73.3 3.5 %collective-permute-start.21 = (bf16[128,256]{1,0:T(8,128)(2,1)S(1)}, bf16[128,256]{1,0:T(8,128)(2,1)S(1)}, u32[]{:S(2)}, u32[]{:S(2)}) collective-permute-start(bf16[128,256]{1,0:T(8,128)(2,1)S(1)} %get-tuple-element.85), channel_id=1, source_target_pairs={{0,14},{2,12},{4,10},{6,8},{8,6},{10,4},{12,2},{14,0},{1,15},{3,13... | collective-permute-start | bytes 196616 | tf_op jit(solution)/shard_map/ppermute | solution.py:171
  78.0 2.3 %collective-permute-done.21.f3 = bf16[128,256]{1,0:T(8,128)(2,1)S(1)} collective-permute-done((bf16[128,256]{1,0:T(8,128)(2,1)S(1)}, bf16[128,256]{1,0:T(8,128)(2,1)S(1)}, u32[]{:S(2)}, u32[]{:S(2)}) %collective-permute-start.21) | collective-permute-done | bytes 65568 | tf_op jit(solution)/shard_map/ppermute | solution.py:171
  81.1 0.9 shard_map.152
  82.0 1.3 %collective-permute-start.22 = (bf16[128,2688]{1,0:T(8,128)(2,1)S(1)}, bf16[128,2688]{1,0:T(8,128)(2,1)S(1)}, u32[]{:S(2)}, u32[]{:S(2)}) collective-permute-start(bf16[128,2688]{1,0:T(8,128)(2,1)S(1)} %get-tuple-element.93), channel_id=1, source_target_pairs={{0,2},{2,0},{4,6},{6,4},{8,10},{10,8},{12,14},{14,12},{1,3},{3,1},... | collective-permute-start | bytes 2064392 | tf_op jit(solution)/shard_map/ppermute | solution.py:171
  84.5 3.1 %collective-permute-start.25 = (bf16[64,2560]{1,0:T(8,128)(2,1)S(1)}, bf16[64,2560]{1,0:T(8,128)(2,1)S(1)}, u32[]{:S(2)}, u32[]{:S(2)}) collective-permute-start(bf16[64,2560]{1,0:T(8,128)(2,1)S(1)} %get-tuple-element.107), channel_id=1, source_target_pairs={{0,8},{2,10},{4,12},{6,14},{8,0},{10,2},{12,4},{14,6},{1,9},{3,11}... | collective-permute-start | bytes 983048 | tf_op jit(solution)/shard_map/ppermute | solution.py:171
  87.6 1.3 %collective-permute-start.26 = (bf16[64,2560]{1,0:T(8,128)(2,1)S(1)}, bf16[64,2560]{1,0:T(8,128)(2,1)S(1)}, u32[]{:S(2)}, u32[]{:S(2)}) collective-permute-start(bf16[64,2560]{1,0:T(8,128)(2,1)S(1)} %get-tuple-element.108), channel_id=1, source_target_pairs={{0,12},{2,14},{4,8},{6,10},{8,4},{10,6},{12,0},{14,2},{1,13},{3,15... | collective-permute-start | bytes 983048 | tf_op jit(solution)/shard_map/ppermute | solution.py:171
  89.3 11.2 %collective-permute-done.22.sent_ref = bf16[128,2688]{1,0:T(8,128)(2,1)S(1)} collective-permute-done((bf16[128,2688]{1,0:T(8,128)(2,1)S(1)}, bf16[128,2688]{1,0:T(8,128)(2,1)S(1)}, u32[]{:S(2)}, u32[]{:S(2)}) %collective-permute-start.22) | collective-permute-done | bytes 688160 | tf_op jit(solution)/shard_map/ppermute | solution.py:171
  100.5 1.2 %shard_map.153 = (bf16[128,2048]{1,0:T(8,128)(2,1)}, bf16[128,512]{1,0:T(8,128)(2,1)}, f32[1,4,32]{2,1,0:T(4,128)}) custom-call(s32[1]{0:T(128)} %bitcast.me_ref, f32[128,2560]{1,0:T(8,128)S(1)} %get-tuple-element.92.own_ref, bf16[128,2688]{1,0:T(8,128)(2,1)S(1)} %collective-permute-done.22.sent_ref, bf16[128,128]{1,0:T(8,128)(2,1)S(1)} %get-tuple-element.101.rg_ref, ...), custom_call_target="tpu_custom_call" | custom-call | tf_op jit(solution)/shard_map/pallas_call | solution.py:531
  101.7 4.6 %collective-permute-done.23 = bf16[2048,128]{1,0:T(8,128)(2,1)S(1)} collective-permute-done((bf16[2048,128]{1,0:T(8,128)(2,1)S(1)}, bf16[2048,128]{1,0:T(8,128)(2,1)S(1)}, u32[]{:S(2)}, u32[]{:S(2)}) %collective-permute-start.23) | collective-permute-done | bytes 524320 | tf_op jit(solution)/shard_map/ppermute | solution.py:171
  (61 shorter events, 16.4 us)
Async XLA Ops:
  0.6 19.3 %collective-permute-start.1 = (bf16[2048,128]{1,0:T(8,128)(2,1)}, bf16[2048,128]{1,0:T(8,128)(2,1)S(1)}, u32[]{:S(2)}, u32[]{:S(2)}) collective-permute-start(bf16[2048,128]{1,0:T(8,128)(2,1)} %bitcast.18), channel_id=1, source_target_pairs={{0,2},{2,0},{4,6},{6,4},{8,10},{10,8},{12,14},{14,12},{1,3},{3,1},... | collective-permute-start | bytes 1572872 | tf_op jit(solution)/shard_map/ppermute | solution.py:171
  3.6 16.9 %collective-permute-start = (bf16[128,2048]{1,0:T(8,128)(2,1)}, bf16[128,2048]{1,0:T(8,128)(2,1)S(1)}, u32[]{:S(2)}, u32[]{:S(2)}) collective-permute-start(bf16[128,2048]{1,0:T(8,128)(2,1)} %x.9), channel_id=1, source_target_pairs={{0,4},{2,6},{4,0},{6,2},{8,12},{10,14},{12,8},{14,10},{1,5},{3,7},... | collective-permute-start | bytes 1572872 | tf_op jit(solution)/shard_map/ppermute | solution.py:171
  5.2 16.1 %collective-permute-start.2 = (bf16[128,2048]{1,0:T(8,128)(2,1)}, bf16[128,2048]{1,0:T(8,128)(2,1)S(1)}, u32[]{:S(2)}, u32[]{:S(2)}) collective-permute-start(bf16[128,2048]{1,0:T(8,128)(2,1)} %x.9), channel_id=1, source_target_pairs={{4,8},{6,10},{8,4},{10,6},{5,9},{7,11},{9,5},{11,7},{20,24},{22,26... | collective-permute-start | bytes 1572872 | tf_op jit(solution)/shard_map/ppermute | solution.py:451
  8.6 1.0 copy-start
  9.6 1.0 copy-start.1
  14.9 32.0 %collective-permute-start.9 = (bf16[128,2816]{1,0:T(8,128)(2,1)S(1)}, bf16[128,2816]{1,0:T(8,128)(2,1)S(1)}, u32[]{:S(2)}, u32[]{:S(2)}) collective-permute-start(bf16[128,2816]{1,0:T(8,128)(2,1)S(1)} %get-tuple-element.64.gw_ref), channel_id=1, source_target_pairs={{0,2},{2,0},{4,6},{6,4},{8,10},{10,8},{12,14},{14,12},{1,3},{3,1},... | collective-permute-start | bytes 2162696 | tf_op jit(solution)/shard_map/ppermute | solution.py:171
  15.5 11.3 %collective-permute-start.5 = (bf16[80,2048]{1,0:T(8,128)(2,1)S(1)}, bf16[80,2048]{1,0:T(8,128)(2,1)S(1)}, u32[]{:S(2)}, u32[]{:S(2)}) collective-permute-start(bf16[80,2048]{1,0:T(8,128)(2,1)S(1)} %get-tuple-element.61.b0), channel_id=1, source_target_pairs={{0,4},{2,6},{4,0},{6,2},{8,12},{10,14},{12,8},{14,10},{1,5},{3,7},... | collective-permute-start | bytes 983048 | tf_op jit(solution)/shard_map/ppermute | solution.py:171
  19.9 7.6 %collective-permute-start.6 = (bf16[80,2048]{1,0:T(8,128)(2,1)S(1)}, bf16[80,2048]{1,0:T(8,128)(2,1)S(1)}, u32[]{:S(2)}, u32[]{:S(2)}) collective-permute-start(bf16[80,2048]{1,0:T(8,128)(2,1)S(1)} %get-tuple-element.61.b0), channel_id=1, source_target_pairs={{4,8},{6,10},{8,4},{10,6},{5,9},{7,11},{9,5},{11,7},{20,24},{22,26... | collective-permute-start | bytes 983048 | tf_op jit(solution)/shard_map/ppermute | solution.py:457
  20.6 8.2 %collective-permute-start.4 = (bf16[128,2048]{1,0:T(8,128)(2,1)S(1)}, bf16[128,2048]{1,0:T(8,128)(2,1)S(1)}, u32[]{:S(2)}, u32[]{:S(2)}) collective-permute-start(bf16[128,2048]{1,0:T(8,128)(2,1)S(1)} %collective-permute-done.x1), channel_id=1, source_target_pairs={{4,8},{6,10},{8,4},{10,6},{5,9},{7,11},{9,5},{11,7},{20,24},{22,26... | collective-permute-start | bytes 1572872 | tf_op jit(solution)/shard_map/ppermute | solution.py:459
  21.3 25.6 %collective-permute-start.3 = (bf16[128,2048]{1,0:T(8,128)(2,1)S(1)}, bf16[128,2048]{1,0:T(8,128)(2,1)S(1)}, u32[]{:S(2)}, u32[]{:S(2)}) collective-permute-start(bf16[128,2048]{1,0:T(8,128)(2,1)S(1)} %collective-permute-done.2.xi), channel_id=1, source_target_pairs={{4,0},{6,2},{8,12},{10,14},{5,1},{7,3},{9,13},{11,15},{20,16},{22,... | collective-permute-start | bytes 1572872 | tf_op jit(solution)/shard_map/ppermute | solution.py:460
  26.8 3.3 %collective-permute-start.8 = (bf16[80,2048]{1,0:T(8,128)(2,1)S(1)}, bf16[80,2048]{1,0:T(8,128)(2,1)S(1)}, u32[]{:S(2)}, u32[]{:S(2)}) collective-permute-start(bf16[80,2048]{1,0:T(8,128)(2,1)S(1)} %collective-permute-done.5.b1), channel_id=1, source_target_pairs={{4,8},{6,10},{8,4},{10,6},{5,9},{7,11},{9,5},{11,7},{20,24},{22,26... | collective-permute-start | bytes 983048 | tf_op jit(solution)/shard_map/ppermute | solution.py:461
  27.5 19.4 %collective-permute-start.7 = (bf16[80,2048]{1,0:T(8,128)(2,1)S(1)}, bf16[80,2048]{1,0:T(8,128)(2,1)S(1)}, u32[]{:S(2)}, u32[]{:S(2)}) collective-permute-start(bf16[80,2048]{1,0:T(8,128)(2,1)S(1)} %collective-permute-done.6.bi), channel_id=1, source_target_pairs={{4,0},{6,2},{8,12},{10,14},{5,1},{7,3},{9,13},{11,15},{20,16},{22,... | collective-permute-start | bytes 983048 | tf_op jit(solution)/shard_map/ppermute | solution.py:461
  28.8 36.3 %collective-permute-start.18 = (bf16[128,2048]{1,0:T(8,128)(2,1)S(1)}, bf16[128,2048]{1,0:T(8,128)(2,1)S(1)}, u32[]{:S(2)}, u32[]{:S(2)}) collective-permute-start(bf16[128,2048]{1,0:T(8,128)(2,1)S(1)} %collective-permute-done.4.xm), channel_id=1, source_target_pairs={{4,0},{6,2},{8,12},{10,14},{5,1},{7,3},{9,13},{11,15},{20,16},{22,... | collective-permute-start | bytes 1572872 | tf_op jit(solution)/shard_map/ppermute | solution.py:463
  30.1 32.8 %collective-permute-start.12 = (bf16[80,2048]{1,0:T(8,128)(2,1)S(1)}, bf16[80,2048]{1,0:T(8,128)(2,1)S(1)}, u32[]{:S(2)}, u32[]{:S(2)}) collective-permute-start(bf16[80,2048]{1,0:T(8,128)(2,1)S(1)} %collective-permute-done.8.bm), channel_id=1, source_target_pairs={{4,0},{6,2},{8,12},{10,14},{5,1},{7,3},{9,13},{11,15},{20,16},{22,... | collective-permute-start | bytes 983048 | tf_op jit(solution)/shard_map/ppermute | solution.py:464
  49.0 1.5 %collective-permute-start.10 = (bf16[384,256]{1,0:T(8,128)(2,1)S(1)}, bf16[384,256]{1,0:T(8,128)(2,1)S(1)}, u32[]{:S(2)}, u32[]{:S(2)}) collective-permute-start(bf16[384,256]{1,0:T(8,128)(2,1)S(1)} %get-tuple-element.65.m_ref), channel_id=1, source_target_pairs={{0,1},{1,0},{2,3},{3,2},{4,5},{5,4},{6,7},{7,6},{8,9},{9,8},{10,11... | collective-permute-start | bytes 589832 | tf_op jit(solution)/shard_map/ppermute | solution.py:175
  49.0 1.7 %collective-permute-start.11 = (bf16[384,256]{1,0:T(8,128)(2,1)S(1)}, bf16[384,256]{1,0:T(8,128)(2,1)S(1)}, u32[]{:S(2)}, u32[]{:S(2)}) collective-permute-start(bf16[384,256]{1,0:T(8,128)(2,1)S(1)} %get-tuple-element.66.s_ref), channel_id=1, source_target_pairs={{0,1},{1,0},{2,3},{3,2},{4,5},{5,4},{6,7},{7,6},{8,9},{9,8},{10,11... | collective-permute-start | bytes 589832 | tf_op jit(solution)/shard_map/ppermute | solution.py:175
  51.0 12.0 %collective-permute-start.13 = (bf16[128,256]{1,0:T(8,128)(2,1)S(1)}, bf16[128,256]{1,0:T(8,128)(2,1)S(1)}, u32[]{:S(2)}, u32[]{:S(2)}) collective-permute-start(bf16[128,256]{1,0:T(8,128)(2,1)S(1)} %get-tuple-element.69), channel_id=1, source_target_pairs={{0,2},{2,0},{4,6},{6,4},{8,10},{10,8},{12,14},{14,12},{1,3},{3,1},... | collective-permute-start | bytes 196616 | tf_op jit(solution)/shard_map/ppermute | solution.py:171
  52.5 10.5 %collective-permute-start.14 = (bf16[128,256]{1,0:T(8,128)(2,1)S(1)}, bf16[128,256]{1,0:T(8,128)(2,1)S(1)}, u32[]{:S(2)}, u32[]{:S(2)}) collective-permute-start(bf16[128,256]{1,0:T(8,128)(2,1)S(1)} %get-tuple-element.70), channel_id=1, source_target_pairs={{0,2},{2,0},{4,6},{6,4},{8,10},{10,8},{12,14},{14,12},{1,3},{3,1},... | collective-permute-start | bytes 196616 | tf_op jit(solution)/shard_map/ppermute | solution.py:171
  53.0 10.0 %collective-permute-start.15 = (bf16[128,256]{1,0:T(8,128)(2,1)S(1)}, bf16[128,256]{1,0:T(8,128)(2,1)S(1)}, u32[]{:S(2)}, u32[]{:S(2)}) collective-permute-start(bf16[128,256]{1,0:T(8,128)(2,1)S(1)} %get-tuple-element.71), channel_id=1, source_target_pairs={{0,2},{2,0},{4,6},{6,4},{8,10},{10,8},{12,14},{14,12},{1,3},{3,1},... | collective-permute-start | bytes 196616 | tf_op jit(solution)/shard_map/ppermute | solution.py:171
  63.1 6.2 %collective-permute-start.16 = (bf16[128,512]{1,0:T(8,128)(2,1)S(1)}, bf16[128,512]{1,0:T(8,128)(2,1)S(1)}, u32[]{:S(2)}, u32[]{:S(2)}) collective-permute-start(bf16[128,512]{1,0:T(8,128)(2,1)S(1)} %get-tuple-element.73), channel_id=1, source_target_pairs={{0,4},{2,6},{4,0},{6,2},{8,12},{10,14},{12,8},{14,10},{1,5},{3,7},... | collective-permute-start | bytes 393224 | tf_op jit(solution)/shard_map/ppermute | solution.py:171
  63.2 7.6 %collective-permute-start.17 = (bf16[128,512]{1,0:T(8,128)(2,1)S(1)}, bf16[128,512]{1,0:T(8,128)(2,1)S(1)}, u32[]{:S(2)}, u32[]{:S(2)}) collective-permute-start(bf16[128,512]{1,0:T(8,128)(2,1)S(1)} %get-tuple-element.74), channel_id=1, source_target_pairs={{0,8},{2,10},{4,12},{6,14},{8,0},{10,2},{12,4},{14,6},{1,9},{3,11}... | collective-permute-start | bytes 393224 | tf_op jit(solution)/shard_map/ppermute | solution.py:171
  65.9 5.8 %collective-permute-start.19 = (bf16[128,512]{1,0:T(8,128)(2,1)S(1)}, bf16[128,512]{1,0:T(8,128)(2,1)S(1)}, u32[]{:S(2)}, u32[]{:S(2)}) collective-permute-start(bf16[128,512]{1,0:T(8,128)(2,1)S(1)} %get-tuple-element.78.m_ref), channel_id=1, source_target_pairs={{0,1},{1,0},{2,3},{3,2},{4,5},{5,4},{6,7},{7,6},{8,9},{9,8},{10,11... | collective-permute-start | bytes 393224 | tf_op jit(solution)/shard_map/ppermute | solution.py:175
  71.9 6.1 %collective-permute-start.20 = (bf16[128,256]{1,0:T(8,128)(2,1)S(1)}, bf16[128,256]{1,0:T(8,128)(2,1)S(1)}, u32[]{:S(2)}, u32[]{:S(2)}) collective-permute-start(bf16[128,256]{1,0:T(8,128)(2,1)S(1)} %get-tuple-element.84), channel_id=1, source_target_pairs={{0,12},{2,14},{4,8},{6,10},{8,4},{10,6},{12,0},{14,2},{1,13},{3,15... | collective-permute-start | bytes 196616 | tf_op jit(solution)/shard_map/ppermute | solution.py:171
  73.3 7.0 %collective-permute-start.21 = (bf16[128,256]{1,0:T(8,128)(2,1)S(1)}, bf16[128,256]{1,0:T(8,128)(2,1)S(1)}, u32[]{:S(2)}, u32[]{:S(2)}) collective-permute-start(bf16[128,256]{1,0:T(8,128)(2,1)S(1)} %get-tuple-element.85), channel_id=1, source_target_pairs={{0,14},{2,12},{4,10},{6,8},{8,6},{10,4},{12,2},{14,0},{1,15},{3,13... | collective-permute-start | bytes 196616 | tf_op jit(solution)/shard_map/ppermute | solution.py:171
  82.0 18.4 %collective-permute-start.22 = (bf16[128,2688]{1,0:T(8,128)(2,1)S(1)}, bf16[128,2688]{1,0:T(8,128)(2,1)S(1)}, u32[]{:S(2)}, u32[]{:S(2)}) collective-permute-start(bf16[128,2688]{1,0:T(8,128)(2,1)S(1)} %get-tuple-element.93), channel_id=1, source_target_pairs={{0,2},{2,0},{4,6},{6,4},{8,10},{10,8},{12,14},{14,12},{1,3},{3,1},... | collective-permute-start | bytes 2064392 | tf_op jit(solution)/shard_map/ppermute | solution.py:171
  83.3 17.2 %copy-start.6 = (s32[1,32,4]{1,2,0:T(4,128)S(1)}, s32[1,32,4]{1,2,0:T(4,128)}, u32[]{:S(2)}) copy-start(s32[1,32,4]{1,2,0:T(4,128)} %param.17) | copy-start | bytes 1540
  83.3 17.2 %copy-start.7 = (s32[1,32]{1,0:T(1,128)S(1)}, s32[1,32]{1,0:T(1,128)}, u32[]{:S(2)}) copy-start(s32[1,32]{1,0:T(1,128)} %rc_ref.1) | copy-start | bytes 388
  83.3 17.2 %copy-start.8 = (s32[1,128]{1,0:T(1,128)S(1)}, s32[1,128]{1,0:T(1,128)}, u32[]{:S(2)}) copy-start(s32[1,128]{1,0:T(1,128)} %tr_ref.1) | copy-start | bytes 1540
  83.6 22.6 %collective-permute-start.23 = (bf16[2048,128]{1,0:T(8,128)(2,1)S(1)}, bf16[2048,128]{1,0:T(8,128)(2,1)S(1)}, u32[]{:S(2)}, u32[]{:S(2)}) collective-permute-start(bf16[2048,128]{1,0:T(8,128)(2,1)S(1)} %add_convert_fusion), channel_id=1, source_target_pairs={{0,2},{2,0},{4,6},{6,4},{8,10},{10,8},{12,14},{14,12},{1,3},{3,1},... | collective-permute-start | bytes 1572872 | tf_op jit(solution)/shard_map/ppermute | solution.py:171
  84.5 22.6 %collective-permute-start.24 = (bf16[64,2560]{1,0:T(8,128)(2,1)S(1)}, bf16[64,2560]{1,0:T(8,128)(2,1)S(1)}, u32[]{:S(2)}, u32[]{:S(2)}) collective-permute-start(bf16[64,2560]{1,0:T(8,128)(2,1)S(1)} %get-tuple-element.105), channel_id=1, source_target_pairs={{0,4},{2,6},{4,0},{6,2},{8,12},{10,14},{12,8},{14,10},{1,5},{3,7},... | collective-permute-start | bytes 983048 | tf_op jit(solution)/shard_map/ppermute | solution.py:171
  84.5 22.6 %collective-permute-start.25 = (bf16[64,2560]{1,0:T(8,128)(2,1)S(1)}, bf16[64,2560]{1,0:T(8,128)(2,1)S(1)}, u32[]{:S(2)}, u32[]{:S(2)}) collective-permute-start(bf16[64,2560]{1,0:T(8,128)(2,1)S(1)} %get-tuple-element.107), channel_id=1, source_target_pairs={{0,8},{2,10},{4,12},{6,14},{8,0},{10,2},{12,4},{14,6},{1,9},{3,11}... | collective-permute-start | bytes 983048 | tf_op jit(solution)/shard_map/ppermute | solution.py:171
  87.6 19.5 %collective-permute-start.26 = (bf16[64,2560]{1,0:T(8,128)(2,1)S(1)}, bf16[64,2560]{1,0:T(8,128)(2,1)S(1)}, u32[]{:S(2)}, u32[]{:S(2)}) collective-permute-start(bf16[64,2560]{1,0:T(8,128)(2,1)S(1)} %get-tuple-element.108), channel_id=1, source_target_pairs={{0,12},{2,14},{4,8},{6,10},{8,4},{10,6},{12,0},{14,2},{1,13},{3,15... | collective-permute-start | bytes 983048 | tf_op jit(solution)/shard_map/ppermute | solution.py:171
  (4 other events, 3.7 us)
